TPU v7x, 512 devices: a whole 4x8x8 slice. The times are simulated.
512 devices in a mesh: tok: 8 (over z), row: 8 (over x, core), col: 8 (over y).
Axes of the slice: x: 4, y: 8, z: 8, core: 2. Of those that a mesh axis runs over, the one named last changes fastest.
Arguments:
- tokens: bfloat16 [576, 8192], P('tok', ('row', 'col')), may hold values from -50 to 50
- d_out: bfloat16 [576, 8192], P('tok', ('row', 'col')), may hold values from -25 to 25
- gain: bfloat16 [8192], P(('row', 'col')), may hold values from 0.3984375 to 2.5
- gate_weight: bfloat16 [14336, 8192], P(('tok', 'col'), 'row'), may hold values from -0.0625 to 0.0625
- up_weight: bfloat16 [14336, 8192], P(('tok', 'col'), 'row'), may hold values from -0.0625 to 0.0625
- down_weight: bfloat16 [14336, 8192], P(('tok', 'col'), 'row'), may hold values from -0.046875 to 0.046875
Outputs:
- d_tokens: bfloat16 [576, 8192], P('tok', ('row', 'col'))
- d_gain: float32 [8192], P(('row', 'col'))
- d_down: bfloat16 [14336, 8192], P(('tok', 'col'), 'row')
All inputs are finite; a program needn't handle non-finite values.
Results may differ from a plain program's by a relative error of at most 0.007.
Values may be sent and summed in bfloat16 or wider, within the bound.
No kernel may reach another device: no remote copies, remote signals or barrier semaphores. Data moves between devices by JAX's collectives and lax.ppermute only.
A program may use at most 64 MiB of HBM per device.

v0:
```python
import jax
import jax.numpy as jnp
from jax import lax
from jax.sharding import PartitionSpec as P

D = 8192


epsilon = 1e-05


def swiglu_grads(gate, up_proj, hidden_grad):
    gate_sig = jax.nn.sigmoid(gate)
    hidden = (gate * gate_sig * up_proj).astype(jnp.bfloat16)
    gate_grad = (hidden_grad * up_proj * gate_sig * (1.0 + gate * (1.0 - gate_sig))).astype(
        jnp.bfloat16
    )
    up_grad = (hidden_grad * gate * gate_sig).astype(jnp.bfloat16)
    return (hidden, gate_grad, up_grad)


def on_device(tokens, d_out, gain, gate_weight, up_weight, down_weight):
    group_count = lax.axis_size("tok")
    col_count = lax.axis_size("col")
    own_rows = tokens.shape[0]
    hidden_local = gate_weight.shape[0]
    feat_rows, gain_rows, grad_rows = (
        lax.all_gather(tokens, "col", axis=1, tiled=True),
        lax.all_gather(gain, "col", axis=0, tiled=True),
        lax.all_gather(d_out, "col", axis=1, tiled=True),
    )
    gain_block = gain_rows.astype(jnp.float32)
    local_inputs = tokens.astype(jnp.float32)
    squares = lax.psum(jnp.sum(local_inputs * local_inputs, axis=1), ("row", "col"))
    inv_rms = lax.rsqrt(squares / D + epsilon)
    normed = (feat_rows.astype(jnp.float32) * inv_rms[:, None] * gain_block).astype(jnp.bfloat16)
    normed_all, grad_all = (
        lax.all_gather(normed, "tok", axis=0, tiled=True),
        lax.all_gather(grad_rows, "tok", axis=0, tiled=True),
    )
    gate_part = jnp.einsum("td,fd->tf", normed_all, gate_weight, preferred_element_type=jnp.float32)
    up_part = jnp.einsum("td,fd->tf", normed_all, up_weight, preferred_element_type=jnp.float32)
    back_part = jnp.einsum("td,fd->tf", grad_all, down_weight, preferred_element_type=jnp.float32)
    gate, up_proj, hidden_grad = lax.psum((gate_part, up_part, back_part), "row")
    hidden, gate_grad, up_grad = swiglu_grads(gate, up_proj, hidden_grad)

    def add_block(running, block_pair):
        block_term = jnp.einsum(
            "tf,td->fd", block_pair[0], block_pair[1], preferred_element_type=jnp.float32
        )
        rounded = lax.optimization_barrier(block_term.astype(jnp.bfloat16))
        return (running + rounded.astype(jnp.float32), None)

    hidden_blocks = hidden.reshape(group_count, own_rows, hidden_local)
    grad_blocks = grad_all.reshape(group_count, own_rows, grad_all.shape[1])
    down_sum, _ = lax.scan(
        add_block,
        jnp.zeros((hidden_local, grad_all.shape[1]), jnp.float32),
        (hidden_blocks, grad_blocks),
    )
    gate_blocks = gate_grad.reshape(group_count, own_rows, hidden_local)
    up_blocks = up_grad.reshape(group_count, own_rows, hidden_local)
    gate_table = gate_weight.reshape(hidden_local, col_count, -1)
    up_table = up_weight.reshape(hidden_local, col_count, -1)
    input_term = jnp.einsum(
        "atf,fcd->actd", gate_blocks, gate_table, preferred_element_type=jnp.float32
    )
    input_term = input_term + jnp.einsum(
        "atf,fcd->actd", up_blocks, up_table, preferred_element_type=jnp.float32
    )
    input_term = input_term.reshape(group_count * col_count * own_rows, -1)
    normed_grad = lax.psum_scatter(input_term, ("tok", "col"), scatter_dimension=0, tiled=True)
    scaled = local_inputs * inv_rms[:, None]
    weighted = normed_grad * gain.astype(jnp.float32)
    inner_sum = lax.psum(jnp.sum(weighted * scaled, axis=1), ("row", "col")) / D
    d_tokens = (
        d_out.astype(jnp.float32) + inv_rms[:, None] * (weighted - scaled * inner_sum[:, None])
    ).astype(jnp.bfloat16)
    d_gain = lax.psum(jnp.sum(normed_grad * scaled, axis=0), "tok")
    return (d_tokens, d_gain, down_sum.astype(jnp.bfloat16))


def solution(mesh):
    placed = (
        P("tok", ("row", "col")),
        P("tok", ("row", "col")),
        P(("row", "col")),
        P(("tok", "col"), "row"),
        P(("tok", "col"), "row"),
        P(("tok", "col"), "row"),
    )
    return jax.shard_map(
        on_device,
        mesh=mesh,
        in_specs=placed,
        out_specs=(P("tok", ("row", "col")), P(("row", "col")), P(("tok", "col"), "row")),
        check_vma=False,
    )
```

profile of v0, /device:TPU:8, one launch (start us, length us, event | category | flops | bytes accessed | tf_op | source)
XLA Modules:
  0.0 738.1 jit_solution(130293549523986390)
XLA Ops:
  7.2 0.0 copy-start
  7.2 0.0 all-gather.6.cloned.1.call-start
  7.2 0.9 fusion.17
  8.1 24.3 %all_gather.17 = bf16[72,1024]{1,0:T(8,128)(2,1)S(1)} all-gather(bf16[72,128]{1,0:T(8,128)(2,1)} %param.8), channel_id=1, replica_groups=mesh['tok'=8,'row'=8,'col'=8] {'col'}, dimensions={1}, use_global_device_ids=true | all-gather | bytes 165888 | tf_op jit(solution)/shard_map/all_gather | solution.py:28
  32.4 127.3 %psum.42 = f32[72]{0:T(128)S(1)} all-reduce(f32[72]{0:T(128)S(1)} %fusion.17), channel_id=1, replica_groups=mesh['tok'=8,'row'=8,'col'=8] {'row','col'}, use_global_device_ids=true, to_apply=%region_1.0 | all-reduce | flops 72 | bytes 576 | tf_op jit(solution)/shard_map/psum | solution.py:34
  159.7 13.1 %all-gather = bf16[8,1,128]{2,1,0:T(2,128)(2,1)S(1)} all-gather(bf16[1,1,128]{2,1,0:T(2,128)(2,1)} %bitcast.62), channel_id=1, replica_groups=mesh['tok'=8,'row'=8,'col'=8] {'col'}, dimensions={0}, use_global_device_ids=true | all-gather | bytes 2304 | tf_op jit(solution)/shard_map/all_gather | solution.py:29
  172.7 0.8 multiply_convert_fusion.3
  173.5 0.0 all-gather.6.cloned.1.call-update
  173.5 0.0 all-gather.4.cloned.1.call-start
  173.6 23.4 %all_gather.15 = bf16[72,1024]{1,0:T(8,128)(2,1)} all-gather(bf16[72,128]{1,0:T(8,128)(2,1)} %param.9), channel_id=1, replica_groups=mesh['tok'=8,'row'=8,'col'=8] {'col'}, dimensions={1}, use_global_device_ids=true | all-gather | bytes 165888 | tf_op jit(solution)/shard_map/all_gather | solution.py:30
  197.0 0.0 all-gather.4.cloned.1.call-update
  197.0 0.0 all-reduce.4.cloned.1.call-start
  197.1 17.4 %all-gather.6.cloned.1.call-done = bf16[576,1024]{1,0:T(8,128)(2,1)} async-done(((bf16[72,1024]{1,0:T(8,128)(2,1)}), bf16[576,1024]{1,0:T(8,128)(2,1)}) %all-gather.6.cloned.1.call-update) | async-done | bytes 1179664 | tf_op jit(solution)/shard_map/all_gather | solution.py:38
  214.5 0.0 copy-start.1
  214.5 2.9 fusion.19
  217.3 0.0 copy-done
  217.3 0.0 copy-done.1
  217.3 0.0 copy-start.4
  217.4 1.4 fusion.20
  218.8 38.2 %all-gather.4.cloned.1.call-done = bf16[576,1024]{1,0:T(8,128)(2,1)} async-done(((bf16[72,1024]{1,0:T(8,128)(2,1)}), bf16[576,1024]{1,0:T(8,128)(2,1)}) %all-gather.4.cloned.1.call-update) | async-done | bytes 1179664 | tf_op jit(solution)/shard_map/all_gather | solution.py:39
  257.0 0.0 copy-done.4
  257.0 2.7 fusion.18
  259.7 0.0 all-reduce.4.cloned.1.call-update
  259.7 0.0 reduce-scatter.4.cloned.1.call-start
  259.8 73.7 %all-reduce.4.cloned.1.call-done = (f32[576,224]{0,1:T(8,128)}, f32[576,224]{0,1:T(8,128)}, f32[576,224]{0,1:T(8,128)}) async-done(((f32[576,224]{0,1:T(8,128)}, f32[576,224]{0,1:T(8,128)}, f32[576,224]{0,1:T(8,128)}), (f32[576,224]{0,1:T(8,128)}, f32[576,224]{0,1:T(8,128)}, f32[576,224]{0,1:T(8,128)})) %all-reduce.4.cloned.1.call-update) | async-done | bytes 1548304 | tf_op jit(solution)/shard_map/psum | solution.py:44
  333.5 2.6 multiply_convert_fusion
  336.0 0.9 copy.19
  336.9 0.0 copy-start.2
  336.9 1.5 fusion.6
  338.4 1.8 copy.21
  340.2 0.0 copy-done.2
  340.2 2.9 convolution_add_fusion
  343.1 0.0 copy-start.7
  343.1 0.0 reduce-scatter.4.cloned.1.call-update
  343.1 0.6 copy-done.7
  343.7 0.3 copy-done.3
  344.0 0.2 copy.23
  344.2 12.4 %while.11 = (s32[]{:T(128)}, f32[224,1024]{1,0:T(8,128)S(1)}, bf16[8,72,224]{2,1,0:T(8,128)(2,1)S(1)}, bf16[8,72,1024]{2,1,0:T(8,128)(2,1)}, s32[]{:T(128)}, /*index=5*/s32[]{:T(128)}) while((s32[]{:T(128)}, f32[224,1024]{1,0:T(8,128)S(1)}, bf16[8,72,224]{2,1,0:T(8,128)(2,1)S(1)}, bf16[8,72,1024]{2,1,0:T(8,128)(2,1)}, ...), condition=%wide.region_11.12_spmd.clone, body=%wide.region_10.11_spmd.clone.sunk | while | flops 33947648 | bytes 2937935 | solution.py:56
  344.2 1.2 convolution_convert_fusion.2
  345.4 0.3 select_add_fusion.2
  345.8 1.2 convolution_convert_fusion.2
  347.0 0.3 select_add_fusion.2
  347.3 1.2 convolution_convert_fusion.2
  348.5 0.3 select_add_fusion.2
  348.9 1.2 convolution_convert_fusion.2
  350.1 0.3 select_add_fusion.2
  350.4 1.2 convolution_convert_fusion.2
  351.6 0.3 select_add_fusion.2
  352.0 1.2 convolution_convert_fusion.2
  353.2 0.3 select_add_fusion.2
  353.5 1.2 convolution_convert_fusion.2
  354.7 0.3 select_add_fusion.2
  355.1 1.2 convolution_convert_fusion.2
  356.3 0.3 select_add_fusion.2
  356.6 0.0 copy-start.5
  356.6 0.0 copy-start.6
  356.6 0.8 convert_element_type.49
  357.5 229.7 %reduce-scatter.4.cloned.1.call-done = f32[72,128]{1,0:T(8,128)} async-done(((f32[4608,128]{1,0:T(8,128)}), f32[72,128]{1,0:T(8,128)}) %reduce-scatter.4.cloned.1.call-update) | async-done | bytes 36880
  587.2 0.0 copy-done.5
  587.2 1.0 fusion.16
  588.1 125.5 %psum.46 = f32[72]{0:T(128)S(1)} all-reduce(f32[72]{0:T(128)S(1)} %get-tuple-element.46), channel_id=1, replica_groups=mesh['tok'=8,'row'=8,'col'=8] {'row','col'}, use_global_device_ids=true, to_apply=%region_7.8 | all-reduce | flops 72 | bytes 576 | tf_op jit(solution)/shard_map/psum | solution.py:75
  713.6 16.4 %psum.47 = f32[128]{0:T(128)} all-reduce(f32[128]{0:T(128)S(1)} %get-tuple-element.45), channel_id=1, replica_groups=mesh['tok'=8,'row'=8,'col'=8] {'tok'}, use_global_device_ids=true, to_apply=%region_9.10 | all-reduce | flops 128 | bytes 1024 | tf_op jit(solution)/shard_map/psum | solution.py:79
  730.1 0.0 copy-done.6
  730.1 1.5 fusion.15
  (6 shorter events, 0.0 us)
Async XLA Ops:
  7.2 210.2 %copy-start = (bf16[224,1024]{1,0:T(8,128)(2,1)S(1)}, bf16[224,1024]{1,0:T(8,128)(2,1)}, u32[]{:S(2)}) copy-start(bf16[224,1024]{1,0:T(8,128)(2,1)} %param.11) | copy-start | bytes 1376260
  7.2 207.3 %all-gather.6.cloned.1.call-start = ((), (), s32[]{:S(2)}) async-start(), calls=%async_computation.2 | async-start | bytes 1327104 | tf_op jit(solution)/shard_map/all_gather | solution.py:38
  173.5 83.5 %all-gather.4.cloned.1.call-start = ((), (), s32[]{:S(2)}) async-start(), calls=%async_computation.1 | async-start | bytes 1327104 | tf_op jit(solution)/shard_map/all_gather | solution.py:39
  197.0 136.4 %all-reduce.4.cloned.1.call-start = ((), (), s32[]{:S(2)}) async-start(), calls=%async_computation.4 | async-start | bytes 3440640 | tf_op jit(solution)/shard_map/psum | solution.py:44
  214.5 2.9 copy-start.1
  217.3 39.7 %copy-start.4 = (bf16[224,1024]{1,0:T(8,128)(2,1)S(1)}, bf16[224,1024]{1,0:T(8,128)(2,1)}, u32[]{:S(2)}) copy-start(bf16[224,1024]{1,0:T(8,128)(2,1)} %param.13) | copy-start | bytes 1376260
  259.7 327.5 %reduce-scatter.4.cloned.1.call-start = ((), (), s32[]{:S(2)}) async-start(), calls=%async_computation.3 | async-start | bytes 2396160
  336.9 3.3 copy-start.2
  343.1 0.7 copy-start.7
  343.1 1.0 copy-start.3
  356.6 230.6 %copy-start.5 = (bf16[72,128]{1,0:T(8,128)(2,1)S(1)}, bf16[72,128]{1,0:T(8,128)(2,1)}, u32[]{:S(2)}) copy-start(bf16[72,128]{1,0:T(8,128)(2,1)} %param.8) | copy-start | bytes 55300
  356.6 373.4 %copy-start.6 = (bf16[72,128]{1,0:T(8,128)(2,1)S(1)}, bf16[72,128]{1,0:T(8,128)(2,1)}, u32[]{:S(2)}) copy-start(bf16[72,128]{1,0:T(8,128)(2,1)} %param.9) | copy-start | bytes 55300
Sparse Core Ops, SparseCore 0:
  173.6 40.7 all-gather.5
  216.5 40.4 all-gather.3
  259.8 73.5 all-reduce.3
  343.2 243.9 reduce-scatter.3
where the time goes:
time: 739 us; the launch traced here: 738 us
  waiting for transfers between devices  359 us (49%)
  blocking collectives  330 us (45%)
  matrix products  21.1 us (3%)
  between operations  13.8 us (2%)
  other arithmetic  9.87 us (1%)
    unnamed x5, waiting for transfers between devices  230 us
    psum x1, blocking collectives, on_device(): lax.psum(jnp.sum(local_inputs * local_inputs, axis=1), ('row', 'col'))  127 us
    psum x1, blocking collectives, on_device(): inner_sum = lax.psum(jnp.sum(weighted * scaled, axis=1), ('row', 'col')) / D  125 us
    psum x1, waiting for transfers between devices, on_device(): lax.psum((gate_part, up_part, back_part), 'row')  73.7 us
    all_gather x1, waiting for transfers between devices, on_device(): lax.all_gather(grad_rows, 'tok', axis=0, tiled=True)  38.2 us
    all_gather x1, blocking collectives, on_device(): lax.all_gather(tokens, 'col', axis=1, tiled=True)  24.3 us
    all_gather x1, blocking collectives, on_device(): lax.all_gather(d_out, 'col', axis=1, tiled=True)  23.4 us
    all_gather x1, waiting for transfers between devices, on_device(): lax.all_gather(normed, 'tok', axis=0, tiled=True)  17.4 us
  transfers between devices with their start and end apart: 4, of which 4 were waited for; matrix products, arithmetic and copies ran while one was open for 2% of the time, Pallas kernels for 0%

commit v1 on v0

v1 whole, which is shorter than its diff:
```python
import jax
import jax.numpy as jnp
from jax import lax
from jax.sharding import PartitionSpec as P

epsilon = 1e-05
F32 = jnp.float32
BF16 = jnp.bfloat16
AXES = ("tok", "row", "col")


def split_wide(value):
    high = lax.reduce_precision(value, 8, 7)
    return high.astype(BF16), (value - high).astype(BF16)


def mixed_groups(tok_count, row_count, col_count, even_along_tok):
    groups = []
    for row in range(row_count):
        if (row % 2 == 0) == even_along_tok:
            for col in range(col_count):
                groups.append([(tok * row_count + row) * col_count + col for tok in range(tok_count)])
        else:
            for tok in range(tok_count):
                groups.append([(tok * row_count + row) * col_count + col for col in range(col_count)])
    return groups


def gather_stage(block, count, groups):
    copies = jnp.broadcast_to(block[None], (count,) + block.shape)
    return lax.all_to_all(copies, AXES, 0, 0, tiled=True, axis_index_groups=groups)


def pad_columns(value, extras=()):
    rows, width = value.shape
    parts = [value.astype(BF16)] + [e.reshape(rows, 1).astype(BF16) for e in extras]
    total = width + len(extras)
    goal = -(-total // 128) * 128
    parts.append(jnp.zeros((rows, goal - total), BF16))
    return jnp.concatenate(parts, axis=1)


def on_device(tokens, d_out, gain, gate_weight, up_weight, down_weight):
    nt, nr, nc = (lax.axis_size(a) for a in AXES)
    rows, feats = tokens.shape
    hidden_count = gate_weight.shape[0]
    width = nc * feats
    model = nr * width
    odd = lax.rem(lax.axis_index("row"), 2) == 1

    block = jnp.concatenate([tokens, d_out, jnp.broadcast_to(gain[None], (8, feats))], axis=0)
    stage = gather_stage(block, nc, mixed_groups(nt, nr, nc, False))
    stage = gather_stage(stage, nt, mixed_groups(nt, nr, nc, True))
    stage = jnp.where(odd, jnp.swapaxes(stage, 0, 1), stage)
    tokens_all = jnp.swapaxes(stage[:, :, :rows], 1, 2).reshape(nt * rows, width)
    grad_all = jnp.swapaxes(stage[:, :, rows : 2 * rows], 1, 2).reshape(nt * rows, width)
    gain_all = stage[0, :, 2 * rows].reshape(width)

    wide = tokens_all.astype(F32)
    squares_part = jnp.sum(wide * wide, axis=1)
    scaled_in = (wide * gain_all.astype(F32)).astype(BF16)
    gate_part = jnp.einsum("td,fd->tf", scaled_in, gate_weight, preferred_element_type=F32)
    up_part = jnp.einsum("td,fd->tf", scaled_in, up_weight, preferred_element_type=F32)
    back_part = jnp.einsum("td,fd->tf", grad_all, down_weight, preferred_element_type=F32)
    sums = jnp.concatenate(
        [pad_columns(gate_part, split_wide(squares_part)), pad_columns(up_part), pad_columns(back_part)], axis=1
    )
    slot = sums.shape[1] // 3
    sums = lax.all_to_all(sums.reshape(nr, rows, 3 * slot), "row", 0, 0, tiled=True)
    sums = jnp.sum(sums.astype(F32), axis=0)
    squares = sums[:, hidden_count] + sums[:, hidden_count + 1]
    inv_rms = lax.rsqrt(squares / model + epsilon)
    gate = sums[:, :hidden_count] * inv_rms[:, None]
    up_proj = sums[:, slot : slot + hidden_count] * inv_rms[:, None]
    hidden_grad = sums[:, 2 * slot : 2 * slot + hidden_count]
    gate_sig = jax.nn.sigmoid(gate)
    hidden = (gate * gate_sig * up_proj).astype(BF16)
    gate_grad = (hidden_grad * up_proj * gate_sig * (1.0 + gate * (1.0 - gate_sig))).astype(BF16)
    up_grad = (hidden_grad * gate * gate_sig).astype(BF16)
    inner_part = jnp.sum(gate_grad.astype(F32) * gate + up_grad.astype(F32) * up_proj, axis=1)
    packed = jnp.concatenate(
        [
            pad_columns(hidden, split_wide(inner_part) + split_wide(inv_rms)),
            pad_columns(gate_grad),
            pad_columns(up_grad),
        ],
        axis=1,
    )
    packed = lax.all_gather(packed, "row", axis=0, tiled=True)
    hidden_all = packed[:, :hidden_count]
    gate_grad_all = packed[:, slot : slot + hidden_count]
    up_grad_all = packed[:, 2 * slot : 2 * slot + hidden_count]
    inner_rows = packed[:, hidden_count : hidden_count + 2]
    inv_pair = packed[:, hidden_count + 2 : hidden_count + 4].astype(F32)
    inv_all = inv_pair[:, 0] + inv_pair[:, 1]

    input_term = jnp.einsum("tf,fd->td", gate_grad_all, gate_weight, preferred_element_type=F32)
    input_term = input_term + jnp.einsum("tf,fd->td", up_grad_all, up_weight, preferred_element_type=F32)
    gain_term = jnp.sum(input_term * wide * inv_all[:, None], axis=0)
    d_down = jnp.einsum("tf,td->fd", hidden_all, grad_all, preferred_element_type=F32).astype(BF16)

    inner_rows = jnp.swapaxes(inner_rows.reshape(nt, 1, rows, 2), 2, 3)
    inner_rows = jnp.pad(inner_rows, ((0, 0), (0, 0), (0, 0), (0, feats - rows)))
    gain_rows = jnp.stack(split_wide(gain_term)).reshape(2, nc, feats).swapaxes(0, 1)[None]
    blocks = jnp.concatenate(
        [
            jnp.swapaxes(input_term.astype(BF16).reshape(nt, rows, nc, feats), 1, 2),
            jnp.broadcast_to(inner_rows, (nt, nc, 2, feats)),
            jnp.broadcast_to(gain_rows, (nt, nc, 2, feats)),
            jnp.zeros((nt, nc, 4, feats), BF16),
        ],
        axis=2,
    )
    blocks = lax.all_to_all(blocks.reshape(nt * nc, rows + 8, feats), ("tok", "col"), 0, 0, tiled=True)
    total = jnp.sum(blocks.astype(F32), axis=0)
    normed_grad = total[:rows]
    inner = (total[rows, :rows] + total[rows + 1, :rows]) / model
    d_gain = total[rows + 2] + total[rows + 3]
    inv_own = lax.dynamic_slice_in_dim(inv_all, lax.axis_index("tok") * rows, rows)[:, None]
    scaled = tokens.astype(F32) * inv_own
    weighted = normed_grad * gain.astype(F32)
    d_tokens = (d_out.astype(F32) + inv_own * (weighted - scaled * inner[:, None])).astype(BF16)
    return (d_tokens, d_gain, d_down)


def solution(mesh):
    placed = (
        P("tok", ("row", "col")),
        P("tok", ("row", "col")),
        P(("row", "col")),
        P(("tok", "col"), "row"),
        P(("tok", "col"), "row"),
        P(("tok", "col"), "row"),
    )
    return jax.shard_map(
        on_device,
        mesh=mesh,
        in_specs=placed,
        out_specs=(P("tok", ("row", "col")), P(("row", "col")), P(("tok", "col"), "row")),
        check_vma=False,
    )
```

time: 739 us -> 173 us (0.23)
  blocking collectives: 330 us -> 31.3 us
  waiting for transfers between devices: 359 us -> 82.5 us
  starting transfers between devices: 0.16 us -> 19.3 us
  between operations: 13.8 us -> 0.89 us
  local copies, waits for them, and re-layouts: 3.84 us -> 14.8 us
  matrix products: 21.1 us -> 13.2 us
    psum x3 -> x0, blocking collectives: 269 us -> none  [the longest x1 127 us: on_device(): lax.psum(jnp.sum(local_inputs * local_inputs, axis=1), ('row', 'col'))]
    unnamed x5 -> x0, waiting for transfers between devices: 230 us -> none
    all_to_all x0 -> x3, waiting for transfers between devices: none -> 82.5 us  [the longest x1 34.4 us: gather_stage(): lax.all_to_all(copies, AXES, 0, 0, tiled=True, axis_index_groups=groups)]
    psum x1 -> x0, waiting for transfers between devices: 73.7 us -> none  [on_device(): lax.psum((gate_part, up_part, back_part), 'row')]
    all_gather x2 -> x0, waiting for transfers between devices: 55.6 us -> none  [the longest x1 38.2 us: on_device(): lax.all_gather(grad_rows, 'tok', axis=0, tiled=True)]
    all_gather x3 -> x1, blocking collectives: 60.8 us -> 13.6 us  [on_device(): packed = lax.all_gather(packed, 'row', axis=0, tiled=True)]
    all_to_all x0 -> x3, starting transfers between devices: none -> 19.3 us  [the longest x1 9.47 us: gather_stage(): lax.all_to_all(copies, AXES, 0, 0, tiled=True, axis_index_groups=groups)]
    all_to_all x0 -> x1, blocking collectives: none -> 17.7 us  [gather_stage(): lax.all_to_all(copies, AXES, 0, 0, tiled=True, axis_index_groups=groups)]
  transfers between devices with their start and end apart: 4 -> 3, of which waited for: 4 -> 3; matrix products, arithmetic and copies ran while one was open for 2% -> 1% of each run, Pallas kernels for 0% -> 0%
where the time goes in v1:
time: 173 us
  waiting for transfers between devices  82.5 us (48%)
  blocking collectives  31.3 us (18%)
  starting transfers between devices  19.3 us (11%)
  local copies, waits for them, and re-layouts  14.8 us (9%)
  matrix products  13.2 us (8%)
  other arithmetic  10.7 us (6%)
    all_to_all x1, waiting for transfers between devices, gather_stage(): lax.all_to_all(copies, AXES, 0, 0, tiled=True, axis_index_groups=groups)  34.4 us
    all_to_all x1, waiting for transfers between devices, on_device(): lax.all_to_all(blocks.reshape(nt * nc, rows + 8, feats), ('tok', 'col'),...  33.8 us
    all_to_all x1, blocking collectives, gather_stage(): lax.all_to_all(copies, AXES, 0, 0, tiled=True, axis_index_groups=groups)  17.7 us
    all_to_all x1, waiting for transfers between devices, on_device(): lax.all_to_all(sums.reshape(nr, rows, 3 * slot), 'row', 0, 0, tiled=True)  14.2 us
    all_gather x1, blocking collectives, on_device(): packed = lax.all_gather(packed, 'row', axis=0, tiled=True)  13.6 us
    all_to_all x1, starting transfers between devices, gather_stage(): lax.all_to_all(copies, AXES, 0, 0, tiled=True, axis_index_groups=groups)  9.47 us
    all_to_all x1, starting transfers between devices, on_device(): lax.all_to_all(blocks.reshape(nt * nc, rows + 8, feats), ('tok', 'col'),...  5.57 us
    convert_element_type x3, local copies, waits for them, and re-layouts, pad_columns(): value.astype(BF16)  4.8 us
  transfers between devices with their start and end apart: 3, of which 3 were waited for; matrix products, arithmetic and copies ran while one was open for 1% of the time, Pallas kernels for 0%

profile of v1, /device:TPU:8, one launch (start us, length us, event | category | flops | bytes accessed | tf_op | source)
XLA Modules:
  0.0 172.7 jit_solution(9136131511813534669)
XLA Ops:
  0.6 0.0 copy-start
  0.6 0.7 broadcast_in_dim.18
  1.4 0.7 pad_maximum_fusion
  2.1 17.7 %all_to_all.20 = bf16[8,152,128]{2,1,0:T(8,128)(2,1)S(1)} all-to-all(bf16[8,152,128]{2,1,0:T(8,128)(2,1)S(1)} %broadcast_in_dim.19), channel_id=1, replica_groups={{0,1,2,3,4,5,6,7},{64,65,66,67,68,69,70,71},{128,129,130,131,132,133,13..., dimensions={0} | all-to-all | bytes 622592 | tf_op jit(solution)/shard_map/all_to_all | solution.py:31
  19.9 1.8 %broadcast_in_dim.20 = bf16[8,8,152,128]{3,1,2,0:T(8,128)(2,1)} broadcast(bf16[8,152,128]{2,0,1:T(8,128)(2,1)S(1)} %copy.47), dimensions={1,2,3} | broadcast | bytes 2801664 | tf_op jit(solution)/shard_map/broadcast_in_dim | solution.py:30
  21.7 9.5 %all-to-all-start.1 = ((bf16[8,8,152,128]{3,1,2,0:T(8,128)(2,1)}), bf16[8,8,152,128]{3,1,2,0:T(8,128)(2,1)S(1)}, u32[]{:S(2)}, u32[]{:S(2)}) async-start(bf16[8,8,152,128]{3,1,2,0:T(8,128)(2,1)} %broadcast_in_dim.20), calls=%async_computation.1 | async-start | bytes 4980736 | tf_op jit(solution)/shard_map/all_to_all | solution.py:31
  31.2 34.4 %all-to-all-done.1 = bf16[8,8,152,128]{3,1,2,0:T(8,128)(2,1)S(1)} async-done(((bf16[8,8,152,128]{3,1,2,0:T(8,128)(2,1)}), bf16[8,8,152,128]{3,1,2,0:T(8,128)(2,1)S(1)}, u32[]{:S(2)}, u32[]{:S(2)}) %all-to-all-start.1) | async-done | bytes 2490400 | tf_op jit(solution)/shard_map/all_to_all | solution.py:31
  65.6 2.7 %copy_select_fusion = bf16[8,8,152,128]{3,1,2,0:T(8,128)(2,1)S(1)} fusion(bf16[8,8,152,128]{3,1,2,0:T(8,128)(2,1)S(1)} %all-to-all-done.1, bf16[8,8,152,128]{3,0,2,1:T(8,128)(2,1)S(1)} %bitcast.67, pred[]{:T(512)S(6)} %eq.3), kind=kLoop, calls=%fused_computation.1 | loop fusion | flops 1245184 | bytes 7471105 | tf_op jit(solution)/shard_map/jit(_where)/select_n | solution.py:54
  68.4 1.1 multiply_reduce_fusion
  69.5 1.3 fusion.26
  70.7 0.2 copy.53
  70.9 0.8 copy.52
  71.7 2.7 %convolution_convert_fusion.1 = bf16[576,224]{0,1:T(8,128)(2,1)} fusion(bf16[224,1024]{1,0:T(8,128)(2,1)} %param.11, bf16[72,8,8,128]{3,2,1,0:T(8,128)(2,1)} %bitcast.73), kind=kOutput, calls=%fused_computation.12 | convolution fusion | flops 264370176 | bytes 1896448 | tf_op jit(solution)/shard_map/td,fd->tf/dot_general | solution.py:64
  74.4 0.0 copy-start.2
  74.4 1.9 %copy.51 = bf16[576,224]{1,0:T(8,128)(2,1)} copy(bf16[576,224]{0,1:T(8,128)(2,1)} %convolution_convert_fusion.1) | data formatting | bytes 516096 | tf_op jit(solution)/shard_map/convert_element_type | solution.py:36
  76.3 0.0 copy-done
  76.3 1.4 convolution_convert_fusion.2
  77.7 1.8 %copy.50 = bf16[576,224]{1,0:T(8,128)(2,1)} copy(bf16[576,224]{0,1:T(8,128)(2,1)} %convolution_convert_fusion.2) | data formatting | bytes 516096 | tf_op jit(solution)/shard_map/convert_element_type | solution.py:36
  79.5 0.0 copy-done.2
  79.5 1.4 convolution_convert_fusion.3
  80.8 1.1 copy.49
  82.0 0.7 broadcast_in_dim.21
  82.7 3.3 %concatenate.27 = bf16[8,72,768]{2,1,0:T(8,128)(2,1)} concatenate(bf16[8,72,224]{2,1,0:T(8,128)(2,1)S(1)} %bitcast.72, bf16[8,72,1]{2,1,0:T(8,128)(2,1)} %copy.52, bf16[8,72,1]{2,1,0:T(8,128)(2,1)S(1)} %copy.53, bf16[8,72,30]{2,1,0:T(8,128)(2,1)} %broadcast_in_dim.21, bf16[8,72,224]{2,1,0:T(8,128)(2,1)} %bitcast.71, bf16[8,72,32]{2,1,0:T(8,128)(2,1)S(1)} %concatenate.25, ...), dimensions={2} | concatenate | bytes 1769472 | tf_op jit(solution)/shard_map/concatenate | solution.py:65
  85.9 4.3 %all-to-all-start.2 = ((bf16[8,72,768]{2,1,0:T(8,128)(2,1)}), bf16[8,72,768]{2,1,0:T(8,128)(2,1)}, u32[]{:S(2)}, u32[]{:S(2)}) async-start(bf16[8,72,768]{2,1,0:T(8,128)(2,1)} %concatenate.27), calls=%async_computation.2 | async-start | bytes 1769472 | tf_op jit(solution)/shard_map/all_to_all | solution.py:69
  90.2 0.1 pad.8.clone
  90.3 14.2 %all-to-all-done.2 = bf16[8,72,768]{2,1,0:T(8,128)(2,1)} async-done(((bf16[8,72,768]{2,1,0:T(8,128)(2,1)}), bf16[8,72,768]{2,1,0:T(8,128)(2,1)}, u32[]{:S(2)}, u32[]{:S(2)}) %all-to-all-start.2) | async-done | bytes 884768 | tf_op jit(solution)/shard_map/all_to_all | solution.py:69
  104.6 1.3 convert_reduce_fusion.1
  105.9 0.1 fusion.28
  105.9 0.1 copy.64
  106.0 0.1 copy.63
  106.1 0.2 add_reduce_fusion
  106.4 0.1 copy.57
  106.5 0.1 copy.58
  106.6 0.1 copy.59
  106.7 0.1 copy.56
  106.9 0.1 concatenate.28
  107.0 13.6 %all_gather.3 = bf16[576,768]{1,0:T(8,128)(2,1)S(1)} all-gather(bf16[72,768]{1,0:T(8,128)(2,1)S(1)} %concatenate.28), channel_id=1, replica_groups=mesh['tok'=8,'row'=8,'col'=8] {'row'}, dimensions={0}, use_global_device_ids=true | all-gather | bytes 995328 | tf_op jit(solution)/shard_map/all_gather | solution.py:89
  120.6 0.0 copy-start.1
  120.6 0.1 fusion.27
  120.7 0.8 copy-done.1
  121.5 2.9 %fusion.11 = f32[576,1024]{1,0:T(8,128)} fusion(bf16[224,1024]{1,0:T(8,128)(2,1)} %param.9, bf16[576,768]{1,0:T(8,128)(2,1)S(1)} %all_gather.3), kind=kOutput, calls=%fused_computation.24 | convolution fusion | flops 264241152 | bytes 3112960 | tf_op jit(solution)/shard_map/tf,fd->td/dot_general | solution.py:97
  124.4 0.1 copy.61
  124.6 0.3 fusion.25
  124.8 2.6 %convert_bitcast_fusion = (bf16[72,8,8,128]{3,1,2,0:T(8,128)(2,1)S(1)}, f32[1024]{0:T(1024)S(1)}) fusion(f32[576]{0:T(1024)S(1)} %get-tuple-element.3, f32[72,8,8,128]{3,2,1,0:T(8,128)S(1)} %bitcast.66, f32[576,1024]{1,0:T(8,128)} %fusion.11, bf16[224,1024]{1,0:T(8,128)(2,1)S(1)} %copy-done, bf16[576,768]{1,0:T(8,128)(2,1)} %copy-done.1), kind=kOutput, calls=%fused_computation.19 | convolution fusion | flops 267189248 | bytes 6658304 | tf_op jit(solution)/shard_map/tf,fd->td/dot_general | solution.py:98
  127.4 0.3 copy.67
  127.7 0.2 copy.82
  128.0 0.0 copy-start.6
  128.0 0.0 copy-start.3
  128.0 1.5 maximum_maximum_fusion
  129.5 5.6 %all-to-all-start.3 = ((bf16[64,80,128]{2,1,0:T(8,128)(2,1)}), bf16[64,80,128]{2,1,0:T(8,128)(2,1)S(1)}, u32[]{:S(2)}, u32[]{:S(2)}) async-start(bf16[64,80,128]{2,1,0:T(8,128)(2,1)} %bitcast.16), calls=%async_computation.3 | async-start | bytes 2621440 | tf_op jit(solution)/shard_map/all_to_all | solution.py:114
  135.0 0.0 copy-done.6
  135.1 0.0 copy-start.4
  135.1 0.0 copy-start.5
  135.1 0.1 dynamic-slice_reduce_fusion
  135.2 0.0 copy-done.3
  135.2 2.3 %convolution_convert_fusion = bf16[224,1024]{1,0:T(8,128)(2,1)} fusion(bf16[72,8,8,128]{3,2,1,0:T(8,128)(2,1)S(1)} %bitcast.74, bf16[576,768]{1,0:T(8,128)(2,1)} %copy-done.1), kind=kOutput, calls=%fused_computation.11 | convolution fusion | flops 264470528 | bytes 1933312 | tf_op jit(solution)/shard_map/tf,td->fd/dot_general | solution.py:100
  137.5 33.8 %all-to-all-done.3 = bf16[64,80,128]{2,1,0:T(8,128)(2,1)S(1)} async-done(((bf16[64,80,128]{2,1,0:T(8,128)(2,1)}), bf16[64,80,128]{2,1,0:T(8,128)(2,1)S(1)}, u32[]{:S(2)}, u32[]{:S(2)}) %all-to-all-start.3) | async-done | bytes 1310752 | tf_op jit(solution)/shard_map/all_to_all | solution.py:114
  171.3 0.2 convert_reduce_fusion
  171.5 0.5 fusion.22
  172.0 0.0 copy-done.4
  172.0 0.0 copy-done.5
  172.0 0.7 fusion.16
  (19 shorter events, 0.3 us)
Async XLA Ops:
  0.6 75.7 %copy-start = (bf16[224,1024]{1,0:T(8,128)(2,1)S(1)}, bf16[224,1024]{1,0:T(8,128)(2,1)}, u32[]{:S(2)}) copy-start(bf16[224,1024]{1,0:T(8,128)(2,1)} %param.10) | copy-start | bytes 1376260
  21.7 43.9 %all-to-all-start.1 = ((bf16[8,8,152,128]{3,1,2,0:T(8,128)(2,1)}), bf16[8,8,152,128]{3,1,2,0:T(8,128)(2,1)S(1)}, u32[]{:S(2)}, u32[]{:S(2)}) async-start(bf16[8,8,152,128]{3,1,2,0:T(8,128)(2,1)} %broadcast_in_dim.20), calls=%async_computation.1 | async-start | bytes 4980736 | tf_op jit(solution)/shard_map/all_to_all | solution.py:31
  74.4 5.1 %copy-start.2 = (bf16[224,1024]{1,0:T(8,128)(2,1)S(1)}, bf16[224,1024]{1,0:T(8,128)(2,1)}, u32[]{:S(2)}) copy-start(bf16[224,1024]{1,0:T(8,128)(2,1)} %param.9) | copy-start | bytes 1376260
  85.9 18.6 %all-to-all-start.2 = ((bf16[8,72,768]{2,1,0:T(8,128)(2,1)}), bf16[8,72,768]{2,1,0:T(8,128)(2,1)}, u32[]{:S(2)}, u32[]{:S(2)}) async-start(bf16[8,72,768]{2,1,0:T(8,128)(2,1)} %concatenate.27), calls=%async_computation.2 | async-start | bytes 1769472 | tf_op jit(solution)/shard_map/all_to_all | solution.py:69
  120.6 0.9 copy-start.1
  128.0 7.1 %copy-start.6 = (bf16[128]{0:T(256)(128)(2,1)S(1)}, bf16[128]{0:T(256)(128)(2,1)}, u32[]{:S(2)}) copy-start(bf16[128]{0:T(256)(128)(2,1)} %param.8) | copy-start | bytes 772
  128.0 7.2 %copy-start.3 = (bf16[8,8,72,128]{3,1,2,0:T(8,128)(2,1)S(1)}, bf16[8,8,72,128]{3,1,2,0:T(8,128)(2,1)}, u32[]{:S(2)}) copy-start(bf16[8,8,72,128]{3,1,2,0:T(8,128)(2,1)} %get-tuple-element.10) | copy-start | bytes 3538948
  129.5 41.8 %all-to-all-start.3 = ((bf16[64,80,128]{2,1,0:T(8,128)(2,1)}), bf16[64,80,128]{2,1,0:T(8,128)(2,1)S(1)}, u32[]{:S(2)}, u32[]{:S(2)}) async-start(bf16[64,80,128]{2,1,0:T(8,128)(2,1)} %bitcast.16), calls=%async_computation.3 | async-start | bytes 2621440 | tf_op jit(solution)/shard_map/all_to_all | solution.py:114
  135.1 37.0 %copy-start.4 = (bf16[72,128]{1,0:T(8,128)(2,1)S(1)}, bf16[72,128]{1,0:T(8,128)(2,1)}, u32[]{:S(2)}) copy-start(bf16[72,128]{1,0:T(8,128)(2,1)} %param.7) | copy-start | bytes 55300
  135.1 36.9 %copy-start.5 = (bf16[72,128]{1,0:T(8,128)(2,1)S(1)}, bf16[72,128]{1,0:T(8,128)(2,1)}, u32[]{:S(2)}) copy-start(bf16[72,128]{1,0:T(8,128)(2,1)} %param.6) | copy-start | bytes 55300

commit v2 on v1

v2 whole, which is shorter than its diff:
```python
import functools

import jax
import jax.numpy as jnp
from jax import lax
from jax.experimental import pallas as pl
from jax.experimental.pallas import tpu as pltpu
from jax.sharding import PartitionSpec as P

epsilon = 1e-05
F32 = jnp.float32
BF16 = jnp.bfloat16
AXES = ("tok", "row", "col")
SLOT = 256
EXTRA = 8
NT_DIMS = (((1,), (1,)), ((), ()))
PARAMS = pltpu.CompilerParams(vmem_limit_bytes=40 * 1024 * 1024)


def split_wide(value):
    high = value.astype(BF16).astype(F32)
    return high, value - high


def mixed_groups(tok_count, row_count, col_count, even_along_tok):
    groups = []
    for row in range(row_count):
        if (row % 2 == 0) == even_along_tok:
            for col in range(col_count):
                groups.append([(tok * row_count + row) * col_count + col for tok in range(tok_count)])
        else:
            for tok in range(tok_count):
                groups.append([(tok * row_count + row) * col_count + col for col in range(col_count)])
    return groups


def gather_stage(block, count, groups):
    copies = jnp.broadcast_to(block[None], (count,) + block.shape)
    return lax.all_to_all(copies, AXES, 0, 0, tiled=True, axis_index_groups=groups)


def block_pair(ref, odd, pair, col, nt, nc, rows):
    out = []
    for tok in (2 * pair, 2 * pair + 1):
        at = jnp.where(odd, col * nt + tok, tok * nc + col)
        out.append(ref[at].astype(F32))
    joined = jnp.concatenate([out[0][:rows], out[1][:rows]], axis=0)
    return joined, out[0]


def padded_weight(ref, scratch):
    count = ref.shape[0]
    scratch[:count, :] = ref[...]
    scratch[count:, :] = jnp.zeros((scratch.shape[0] - count, ref.shape[1]), BF16)
    return scratch[...]


def up_kernel(nt, nc, rows, odd_ref, blocks_ref, gate_ref, up_ref, part_ref, tokens_ref, scaled_ref, w_ref):
    odd = odd_ref[0] == 1
    count, feats = gate_ref.shape[0], blocks_ref.shape[2]
    totals = []
    for pair in range(nt // 2):
        at = pl.ds(pair * 2 * rows, 2 * rows)
        squares = jnp.zeros((2 * rows, feats), F32)
        for col in range(nc):
            wide, first = block_pair(blocks_ref, odd, pair, col, nt, nc, rows)
            cols = pl.ds(col * feats, feats)
            tokens_ref[at, cols] = wide.astype(BF16)
            scaled_ref[at, cols] = (wide * first[rows : rows + 1]).astype(BF16)
            squares = squares + wide * wide
        totals.append(jnp.sum(squares, axis=1, keepdims=True))
    high, low = split_wide(jnp.concatenate(totals, axis=0))
    scaled = scaled_ref[...]
    gate = lax.dot_general(scaled, padded_weight(gate_ref, w_ref.at[0]), NT_DIMS, preferred_element_type=F32)
    lane = lax.broadcasted_iota(jnp.int32, gate.shape, 1)
    gate = jnp.where(lane == count, high, jnp.where(lane == count + 1, low, gate))
    up = lax.dot_general(scaled, padded_weight(up_ref, w_ref.at[1]), NT_DIMS, preferred_element_type=F32)
    for tok in range(nt):
        part_ref[tok, :, :SLOT] = gate[tok * rows : (tok + 1) * rows].astype(BF16)
        part_ref[tok, :, SLOT:] = up[tok * rows : (tok + 1) * rows].astype(BF16)


def back_kernel(nt, nc, rows, odd_ref, blocks_ref, down_ref, part_ref, grads_ref, w_ref):
    odd = odd_ref[0] == 1
    feats = blocks_ref.shape[2]
    for pair in range(nt // 2):
        at = pl.ds(pair * 2 * rows, 2 * rows)
        for col in range(nc):
            wide, _ = block_pair(blocks_ref, odd, pair, col, nt, nc, rows)
            grads_ref[at, pl.ds(col * feats, feats)] = wide.astype(BF16)
    back = lax.dot_general(
        grads_ref[...], padded_weight(down_ref, w_ref), NT_DIMS, preferred_element_type=F32
    )
    for tok in range(nt):
        part_ref[tok] = back[tok * rows : (tok + 1) * rows].astype(BF16)


def swiglu_kernel(model, count, forward_ref, back_ref, packed_ref):
    sums = jnp.sum(forward_ref[...].astype(F32), axis=0)
    hidden_grad = jnp.sum(back_ref[...].astype(F32), axis=0)
    gate, up_proj = sums[:, :SLOT], sums[:, SLOT:]
    lane = lax.broadcasted_iota(jnp.int32, gate.shape, 1)
    at_squares = (lane >= count) & (lane < count + 2)
    squares = jnp.sum(jnp.where(at_squares, gate, 0.0), axis=1, keepdims=True)
    inv_rms = lax.rsqrt(squares / model + epsilon)
    gate = jnp.where(lane < count, gate * inv_rms, 0.0)
    up_proj = up_proj * inv_rms
    sig = jax.nn.sigmoid(gate)
    hidden = gate * sig * up_proj
    gate_grad = (hidden_grad * up_proj * sig * (1.0 + gate * (1.0 - sig))).astype(BF16)
    up_grad = (hidden_grad * gate * sig).astype(BF16)
    inner = jnp.sum(gate_grad.astype(F32) * gate + up_grad.astype(F32) * up_proj, axis=1, keepdims=True)
    for place, value in enumerate(split_wide(inner) + split_wide(inv_rms)):
        hidden = jnp.where(lane == count + place, value, hidden)
    packed_ref[:, :SLOT] = hidden.astype(BF16)
    packed_ref[:, SLOT : 2 * SLOT] = gate_grad
    packed_ref[:, 2 * SLOT :] = up_grad


def input_kernel(nt, rows, feats, count, packed_ref, gate_ref, up_ref, tokens_ref, out_ref, inv_ref, extra_ref):
    base = count % 128

    @pl.when(pl.program_id(0) == 0)
    def _():
        tail = packed_ref[:, SLOT - 128 : SLOT].astype(F32)
        lane = lax.broadcasted_iota(jnp.int32, tail.shape, 1)
        at_inv = (lane >= base + 2) & (lane < base + 4)
        inv_ref[...] = jnp.sum(jnp.where(at_inv, tail, 0.0), axis=1, keepdims=True)
        for tok in range(nt):
            piece = tail[tok * rows : (tok + 1) * rows]
            square = jnp.concatenate([piece, jnp.zeros((128 - rows, 128), F32)], axis=0)
            extra_ref[tok] = square.T[base : base + EXTRA]

    fill = jnp.zeros((SLOT - count, gate_ref.shape[1]), BF16)
    term = jnp.dot(
        packed_ref[:, SLOT : 2 * SLOT],
        jnp.concatenate([gate_ref[...], fill], axis=0),
        preferred_element_type=F32,
    )
    term = term + jnp.dot(
        packed_ref[:, 2 * SLOT :],
        jnp.concatenate([up_ref[...], fill], axis=0),
        preferred_element_type=F32,
    )
    gain_term = jnp.sum(term * (tokens_ref[...].astype(F32) * inv_ref[...]), axis=0, keepdims=True)
    high, low = split_wide(gain_term)
    spot = lax.broadcasted_iota(jnp.int32, (EXTRA, feats), 0)
    for part in range(gate_ref.shape[1] // feats):
        cols = slice(part * feats, (part + 1) * feats)
        for tok in range(nt):
            extra = jnp.where(spot == 2, high[:, cols], jnp.where(spot == 3, low[:, cols], extra_ref[tok]))
            block = jnp.concatenate([term[tok * rows : (tok + 1) * rows, cols], extra], axis=0)
            out_ref[tok, part] = block.astype(BF16)


def whole(memory=pltpu.VMEM):
    return pl.BlockSpec(memory_space=memory)


def on_device(tokens, d_out, gain, gate_weight, up_weight, down_weight):
    nt, nr, nc = (lax.axis_size(a) for a in AXES)
    rows, feats = tokens.shape
    count = gate_weight.shape[0]
    width = nc * feats
    model = nr * width
    odd = lax.rem(lax.axis_index("row"), 2)
    odd_flag = odd.reshape(1).astype(jnp.int32)

    block = jnp.concatenate([tokens, jnp.broadcast_to(gain[None], (EXTRA, feats)), d_out], axis=0)
    stage = gather_stage(block, nc, mixed_groups(nt, nr, nc, False))
    second = mixed_groups(nt, nr, nc, True)
    tall = rows + EXTRA
    token_blocks = gather_stage(stage[:, :tall], nt, second).reshape(nt * nc, tall, feats)
    grad_blocks = gather_stage(stage[:, tall:], nt, second).reshape(nt * nc, rows, feats)

    flops = 2 * nt * rows * width * SLOT
    forward, tokens_all = pl.pallas_call(
        functools.partial(up_kernel, nt, nc, rows),
        out_shape=(
            jax.ShapeDtypeStruct((nt, rows, 2 * SLOT), BF16),
            jax.ShapeDtypeStruct((nt * rows, width), BF16),
        ),
        in_specs=[whole(pltpu.SMEM)] + [whole()] * 3,
        out_specs=(whole(), whole()),
        scratch_shapes=[pltpu.VMEM((nt * rows, width), BF16), pltpu.VMEM((2, SLOT, width), BF16)],
        compiler_params=PARAMS,
        cost_estimate=pl.CostEstimate(flops=2 * flops, bytes_accessed=4 * nt * rows * width, transcendentals=0),
        name="gate_up_parts",
    )(odd_flag, token_blocks, gate_weight, up_weight)
    back, grad_all = pl.pallas_call(
        functools.partial(back_kernel, nt, nc, rows),
        out_shape=(
            jax.ShapeDtypeStruct((nt, rows, SLOT), BF16),
            jax.ShapeDtypeStruct((nt * rows, width), BF16),
        ),
        in_specs=[whole(pltpu.SMEM)] + [whole()] * 2,
        out_specs=(whole(), whole()),
        scratch_shapes=[pltpu.VMEM((SLOT, width), BF16)],
        compiler_params=PARAMS,
        cost_estimate=pl.CostEstimate(flops=flops, bytes_accessed=4 * nt * rows * width, transcendentals=0),
        name="hidden_grad_parts",
    )(odd_flag, grad_blocks, down_weight)
    forward = lax.all_to_all(forward, "row", 0, 0, tiled=True)
    back = lax.all_to_all(back, "row", 0, 0, tiled=True)
    packed = pl.pallas_call(
        functools.partial(swiglu_kernel, model, count),
        out_shape=jax.ShapeDtypeStruct((rows, 3 * SLOT), BF16),
        in_specs=[whole()] * 2,
        out_specs=whole(),
        compiler_params=PARAMS,
        cost_estimate=pl.CostEstimate(flops=20 * rows * SLOT, bytes_accessed=8 * rows * SLOT * nr, transcendentals=rows * SLOT),
        name="swiglu_grads",
    )(forward, back)
    packed = lax.all_gather(packed, "row", axis=0, tiled=True)

    chunk = 2 * feats
    blocks = pl.pallas_call(
        functools.partial(input_kernel, nt, rows, feats, count),
        out_shape=jax.ShapeDtypeStruct((nt, nc, rows + EXTRA, feats), BF16),
        grid=(width // chunk,),
        in_specs=[
            whole(),
            pl.BlockSpec((count, chunk), lambda j: (0, j)),
            pl.BlockSpec((count, chunk), lambda j: (0, j)),
            pl.BlockSpec((nt * rows, chunk), lambda j: (0, j)),
        ],
        out_specs=pl.BlockSpec((nt, 2, rows + EXTRA, feats), lambda j: (0, j, 0, 0)),
        scratch_shapes=[pltpu.VMEM((nt * rows, 1), F32), pltpu.VMEM((nt, EXTRA, 128), F32)],
        compiler_params=PARAMS,
        cost_estimate=pl.CostEstimate(flops=2 * flops, bytes_accessed=6 * nt * rows * width, transcendentals=0),
        name="input_grad_blocks",
    )(packed, gate_weight, up_weight, tokens_all)
    blocks = lax.all_to_all(blocks.reshape(nt * nc, rows + EXTRA, feats), ("tok", "col"), 0, 0, tiled=True)

    terms = jnp.einsum(
        "btf,btd->bfd",
        packed[:, :count].reshape(nt, rows, count),
        grad_all.reshape(nt, rows, width),
        preferred_element_type=F32,
    )
    terms = lax.optimization_barrier(terms.astype(BF16))
    d_down = jnp.sum(terms.astype(F32), axis=0).astype(BF16)

    own = lax.dynamic_slice_in_dim(packed, lax.axis_index("tok") * rows, rows)
    inv_own = own[:, count + 2 : count + 3].astype(F32) + own[:, count + 3 : count + 4].astype(F32)
    total = jnp.sum(blocks.astype(F32), axis=0)
    normed_grad = total[:rows]
    inner = (total[rows, :rows] + total[rows + 1, :rows]) / model
    d_gain = total[rows + 2] + total[rows + 3]
    scaled = tokens.astype(F32) * inv_own
    weighted = normed_grad * gain.astype(F32)
    d_tokens = (d_out.astype(F32) + inv_own * (weighted - scaled * inner[:, None])).astype(BF16)
    return (d_tokens, d_gain, d_down)


def solution(mesh):
    placed = (
        P("tok", ("row", "col")),
        P("tok", ("row", "col")),
        P(("row", "col")),
        P(("tok", "col"), "row"),
        P(("tok", "col"), "row"),
        P(("tok", "col"), "row"),
    )
    return jax.shard_map(
        on_device,
        mesh=mesh,
        in_specs=placed,
        out_specs=(P("tok", ("row", "col")), P(("row", "col")), P(("tok", "col"), "row")),
        check_vma=False,
    )
```

time: 173 us -> 166 us (0.960)
  blocking collectives: 31.3 us -> 44.9 us
  matrix products: 13.2 us -> 2.97 us
  waiting for transfers between devices: 82.5 us -> 73.7 us
  local copies, waits for them, and re-layouts: 14.8 us -> 7.03 us
  Pallas kernels: 0 us -> 4.83 us
  starting transfers between devices: 19.3 us -> 23.8 us
  other arithmetic: 10.7 us -> 7.34 us
    all_to_all x0 -> x1, blocking collectives: none -> 13.6 us  [on_device(): forward = lax.all_to_all(forward, 'row', 0, 0, tiled=True)]
    all_to_all x2, waiting for transfers between devices: 48 us -> 35.1 us  [the longest x1 29.3 us: on_device(): lax.all_to_all(blocks.reshape(nt * nc, rows + EXTRA, feats), ('tok', 'col...]
    dot_general x6 -> x1, matrix products: 13.2 us -> 2.97 us  [on_device(): jnp.einsum('btf,btd->bfd', packed[:, :count].reshape(nt, rows, count), gr...]
    convert_element_type x9 -> x0, local copies, waits for them, and re-layouts: 6.25 us -> none  [the longest x3 4.8 us: pad_columns(): value.astype(BF16)]
    pallas_call x0 -> x4, Pallas kernels: none -> 4.83 us  [the longest x1 2.98 us: on_device(): pl.pallas_call(functools.partial(input_kernel, nt, rows, feats, count), o...]
    all_to_all x1 -> x2, waiting for transfers between devices: 34.4 us -> 38.6 us  [gather_stage(): lax.all_to_all(copies, AXES, 0, 0, tiled=True, axis_index_groups=groups)]
    all_to_all x1 -> x2, starting transfers between devices: 9.47 us -> 13 us  [gather_stage(): lax.all_to_all(copies, AXES, 0, 0, tiled=True, axis_index_groups=groups)]
    concatenate x4 -> x0, local copies, waits for them, and re-layouts: 3.49 us -> none  [the longest x2 3.28 us: on_device(): jnp.concatenate([pad_columns(gate_part, split_wide(squares_part)), pad_co...]
  transfers between devices with their start and end apart: 3 -> 4, of which waited for: 3 -> 4; matrix products, arithmetic and copies ran while one was open for 1% -> 4% of each run, Pallas kernels for 0% -> 1%
where the time goes in v2:
time: 166 us; the launch traced here: 165 us
  waiting for transfers between devices  73.7 us (44%)
  blocking collectives  44.9 us (27%)
  starting transfers between devices  23.8 us (14%)
  other arithmetic  7.34 us (4%)
  local copies, waits for them, and re-layouts  7.03 us (4%)
  Pallas kernels  4.83 us (3%)
  matrix products  2.97 us (2%)
    all_to_all x2, waiting for transfers between devices, gather_stage(): lax.all_to_all(copies, AXES, 0, 0, tiled=True, axis_index_groups=groups)  38.6 us
    all_to_all x1, waiting for transfers between devices, on_device(): lax.all_to_all(blocks.reshape(nt * nc, rows + EXTRA, feats), ('tok', 'col...  29.3 us
    all_to_all x1, blocking collectives, gather_stage(): lax.all_to_all(copies, AXES, 0, 0, tiled=True, axis_index_groups=groups)  17.7 us
    all_to_all x1, blocking collectives, on_device(): forward = lax.all_to_all(forward, 'row', 0, 0, tiled=True)  13.6 us
    all_gather x1, blocking collectives, on_device(): packed = lax.all_gather(packed, 'row', axis=0, tiled=True)  13.6 us
    all_to_all x2, starting transfers between devices, gather_stage(): lax.all_to_all(copies, AXES, 0, 0, tiled=True, axis_index_groups=groups)  13 us
    all_to_all x1, starting transfers between devices, on_device(): lax.all_to_all(blocks.reshape(nt * nc, rows + EXTRA, feats), ('tok', 'col...  6.47 us
    all_to_all x1, waiting for transfers between devices, on_device(): back = lax.all_to_all(back, 'row', 0, 0, tiled=True)  5.79 us
  transfers between devices with their start and end apart: 4, of which 4 were waited for; matrix products, arithmetic and copies ran while one was open for 4% of the time, Pallas kernels for 1%

profile of v2, /device:TPU:8, one launch (start us, length us, event | category | flops | bytes accessed | tf_op | source)
XLA Modules:
  0.0 165.4 jit_solution(800831534818631506)
XLA Ops:
  0.6 0.7 broadcast_in_dim.8
  1.3 0.7 pad_maximum_fusion
  2.1 17.7 %all_to_all.30 = bf16[8,152,128]{2,1,0:T(8,128)(2,1)S(1)} all-to-all(bf16[8,152,128]{2,1,0:T(8,128)(2,1)S(1)} %broadcast_in_dim.9), channel_id=1, replica_groups={{0,1,2,3,4,5,6,7},{64,65,66,67,68,69,70,71},{128,129,130,131,132,133,13..., dimensions={0} | all-to-all | bytes 622592 | tf_op jit(solution)/shard_map/all_to_all | solution.py:39
  19.8 1.2 broadcast_in_dim.11
  21.0 9.5 %all-to-all-start.3 = ((bf16[8,8,72,128]{3,2,1,0:T(8,128)(2,1)}), bf16[8,8,72,128]{3,2,1,0:T(8,128)(2,1)S(1)}, u32[]{:S(2)}, u32[]{:S(2)}) async-start(bf16[8,8,72,128]{3,2,1,0:T(8,128)(2,1)} %broadcast_in_dim.11), calls=%async_computation.3 | async-start | bytes 2359296 | tf_op jit(solution)/shard_map/all_to_all | solution.py:39
  30.5 20.3 %all-to-all-done.3 = bf16[8,8,72,128]{3,2,1,0:T(8,128)(2,1)S(1)} async-done(((bf16[8,8,72,128]{3,2,1,0:T(8,128)(2,1)}), bf16[8,8,72,128]{3,2,1,0:T(8,128)(2,1)S(1)}, u32[]{:S(2)}, u32[]{:S(2)}) %all-to-all-start.3) | async-done | bytes 1179680 | tf_op jit(solution)/shard_map/all_to_all | solution.py:39
  50.9 1.3 broadcast_in_dim.10
  52.1 3.6 %all-to-all-start.1 = ((bf16[8,8,80,128]{3,2,1,0:T(8,128)(2,1)}), bf16[8,8,80,128]{3,2,1,0:T(8,128)(2,1)S(1)}, u32[]{:S(2)}, u32[]{:S(2)}) async-start(bf16[8,8,80,128]{3,2,1,0:T(8,128)(2,1)} %broadcast_in_dim.10), calls=%async_computation.1 | async-start | bytes 2621440 | tf_op jit(solution)/shard_map/all_to_all | solution.py:39
  55.7 0.0 copy-start.4
  55.7 0.0 copy-start.5
  55.7 0.0 copy-start.6
  55.7 1.1 copy-done.6
  56.8 0.5 hidden_grad_parts.1
  57.4 0.0 copy-start
  57.4 1.0 copy-done
  58.4 0.0 copy-start.7
  58.4 0.7 copy-done.7
  59.1 18.3 %all-to-all-done.1 = bf16[8,8,80,128]{3,2,1,0:T(8,128)(2,1)S(1)} async-done(((bf16[8,8,80,128]{3,2,1,0:T(8,128)(2,1)}), bf16[8,8,80,128]{3,2,1,0:T(8,128)(2,1)S(1)}, u32[]{:S(2)}, u32[]{:S(2)}) %all-to-all-start.1) | async-done | bytes 1310752 | tf_op jit(solution)/shard_map/all_to_all | solution.py:39
  77.4 4.3 %all-to-all-start.4 = ((bf16[8,72,256]{2,1,0:T(8,128)(2,1)}), bf16[8,72,256]{2,1,0:T(8,128)(2,1)S(1)}, u32[]{:S(2)}, u32[]{:S(2)}) async-start(bf16[8,72,256]{2,1,0:T(8,128)(2,1)} %copy-done.7), calls=%async_computation.4 | async-start | bytes 589824 | tf_op jit(solution)/shard_map/all_to_all | solution.py:204
  81.7 0.0 copy-done.4
  81.7 0.0 copy-done.5
  81.7 1.0 gate_up_parts.1
  82.7 0.0 copy-start.2
  82.7 1.0 copy-done.2
  83.8 5.8 %all-to-all-done.4.back_ref = bf16[8,72,256]{2,1,0:T(8,128)(2,1)S(1)} async-done(((bf16[8,72,256]{2,1,0:T(8,128)(2,1)}), bf16[8,72,256]{2,1,0:T(8,128)(2,1)S(1)}, u32[]{:S(2)}, u32[]{:S(2)}) %all-to-all-start.4) | async-done | bytes 294944 | tf_op jit(solution)/shard_map/all_to_all | solution.py:204
  89.6 0.0 copy-start.3
  89.6 13.6 %all_to_all.31.forward_ref = bf16[8,72,512]{2,1,0:T(8,128)(2,1)S(1)} all-to-all(bf16[8,72,512]{2,1,0:T(8,128)(2,1)S(1)} %get-tuple-element.7), channel_id=1, replica_groups=mesh['tok'=8,'row'=8,'col'=8] {'row'}, dimensions={0} | all-to-all | bytes 1179648 | tf_op jit(solution)/shard_map/all_to_all | solution.py:203
  103.2 0.3 swiglu_grads.1
  103.4 13.6 %all_gather.3.packed_ref = bf16[576,768]{1,0:T(8,128)(2,1)S(1)} all-gather(bf16[72,768]{1,0:T(8,128)(2,1)S(1)} %swiglu_grads.1), channel_id=1, replica_groups=mesh['tok'=8,'row'=8,'col'=8] {'row'}, dimensions={0}, use_global_device_ids=true | all-gather | bytes 995328 | tf_op jit(solution)/shard_map/all_gather | solution.py:214
  117.0 0.0 copy-done.3
  117.0 3.0 %input_grad_blocks.1 = bf16[8,8,80,128]{3,2,1,0:T(8,128)(2,1)} custom-call(bf16[576,768]{1,0:T(8,128)(2,1)S(1)} %all_gather.3.packed_ref, bf16[224,1024]{1,0:T(8,128)(2,1)S(1)} %copy-done.4, bf16[224,1024]{1,0:T(8,128)(2,1)S(1)} %copy-done.5, bf16[576,1024]{1,0:T(8,128)(2,1)S(1)} %copy-done.3), custom_call_target="tpu_custom_call" | custom-call | flops 603979776 | bytes 3538944 | tf_op jit(solution)/shard_map/input_grad_blocks/pallas_call | solution.py:217
  120.0 0.0 copy-start.10
  120.0 0.0 copy-start.1
  120.0 6.5 %all-to-all-start.5 = ((bf16[64,80,128]{2,1,0:T(8,128)(2,1)}), bf16[64,80,128]{2,1,0:T(8,128)(2,1)}, u32[]{:S(2)}, u32[]{:S(2)}) async-start(bf16[64,80,128]{2,1,0:T(8,128)(2,1)} %bitcast.3), calls=%async_computation.5 | async-start | bytes 2621440 | tf_op jit(solution)/shard_map/all_to_all | solution.py:233
  126.4 0.0 copy-done.10
  126.5 0.0 copy-done.1
  126.5 3.0 %convolution_convert_fusion = bf16[8,224,1024]{2,1,0:T(8,128)(2,1)} fusion(bf16[8,72,224]{2,1,0:T(8,128)(2,1)S(1)} %bitcast.15, bf16[8,72,1024]{2,1,0:T(8,128)(2,1)S(1)} %bitcast.14), kind=kOutput, calls=%fused_computation.1 | convolution fusion | flops 266076160 | bytes 5107712 | tf_op jit(solution)/shard_map/btf,btd->bfd/dot_general | solution.py:235
  129.5 3.7 %reduce_sum.22 = bf16[224,1024]{1,0:T(8,128)(2,1)} reduce(bf16[8,224,1024]{2,1,0:T(8,128)(2,1)} %convolution_convert_fusion, bf16[]{:T(256)} %constant.25.clone.1), dimensions={0}, to_apply=%region_1.0 | reduce | flops 1605632 | bytes 4128770 | tf_op jit(solution)/shard_map/reduce_sum | solution.py:242
  133.1 0.0 copy-start.8
  133.1 0.0 copy-start.9
  133.1 0.2 add_reduce_fusion
  133.3 29.3 %all-to-all-done.5 = bf16[64,80,128]{2,1,0:T(8,128)(2,1)} async-done(((bf16[64,80,128]{2,1,0:T(8,128)(2,1)}), bf16[64,80,128]{2,1,0:T(8,128)(2,1)}, u32[]{:S(2)}, u32[]{:S(2)}) %all-to-all-start.5) | async-done | bytes 1310752 | tf_op jit(solution)/shard_map/all_to_all | solution.py:233
  162.6 1.5 convert_reduce_fusion
  164.1 0.5 fusion.4
  164.7 0.0 copy-done.8
  164.7 0.0 copy-done.9
  164.7 0.7 fusion.3
  (6 shorter events, 0.1 us)
Async XLA Ops:
  21.0 29.8 %all-to-all-start.3 = ((bf16[8,8,72,128]{3,2,1,0:T(8,128)(2,1)}), bf16[8,8,72,128]{3,2,1,0:T(8,128)(2,1)S(1)}, u32[]{:S(2)}, u32[]{:S(2)}) async-start(bf16[8,8,72,128]{3,2,1,0:T(8,128)(2,1)} %broadcast_in_dim.11), calls=%async_computation.3 | async-start | bytes 2359296 | tf_op jit(solution)/shard_map/all_to_all | solution.py:39
  52.1 25.3 %all-to-all-start.1 = ((bf16[8,8,80,128]{3,2,1,0:T(8,128)(2,1)}), bf16[8,8,80,128]{3,2,1,0:T(8,128)(2,1)S(1)}, u32[]{:S(2)}, u32[]{:S(2)}) async-start(bf16[8,8,80,128]{3,2,1,0:T(8,128)(2,1)} %broadcast_in_dim.10), calls=%async_computation.1 | async-start | bytes 2621440 | tf_op jit(solution)/shard_map/all_to_all | solution.py:39
  55.7 26.0 %copy-start.4 = (bf16[224,1024]{1,0:T(8,128)(2,1)S(1)}, bf16[224,1024]{1,0:T(8,128)(2,1)}, u32[]{:S(2)}) copy-start(bf16[224,1024]{1,0:T(8,128)(2,1)} %gate_ref.3) | copy-start | bytes 1376260
  55.7 26.0 %copy-start.5 = (bf16[224,1024]{1,0:T(8,128)(2,1)S(1)}, bf16[224,1024]{1,0:T(8,128)(2,1)}, u32[]{:S(2)}) copy-start(bf16[224,1024]{1,0:T(8,128)(2,1)} %up_ref.3) | copy-start | bytes 1376260
  55.7 1.1 copy-start.6
  57.4 1.0 copy-start
  58.4 0.7 copy-start.7
  77.4 12.2 %all-to-all-start.4 = ((bf16[8,72,256]{2,1,0:T(8,128)(2,1)}), bf16[8,72,256]{2,1,0:T(8,128)(2,1)S(1)}, u32[]{:S(2)}, u32[]{:S(2)}) async-start(bf16[8,72,256]{2,1,0:T(8,128)(2,1)} %copy-done.7), calls=%async_computation.4 | async-start | bytes 589824 | tf_op jit(solution)/shard_map/all_to_all | solution.py:204
  82.7 1.0 copy-start.2
  89.6 27.4 %copy-start.3 = (bf16[576,1024]{1,0:T(8,128)(2,1)S(1)}, bf16[576,1024]{1,0:T(8,128)(2,1)}, u32[]{:S(2)}) copy-start(bf16[576,1024]{1,0:T(8,128)(2,1)} %copy-done.2) | copy-start | bytes 3538948
  120.0 6.5 %copy-start.10 = (bf16[128]{0:T(256)(128)(2,1)S(1)}, bf16[128]{0:T(256)(128)(2,1)}, u32[]{:S(2)}) copy-start(bf16[128]{0:T(256)(128)(2,1)} %param.8) | copy-start | bytes 772
  120.0 6.5 %copy-start.1 = (bf16[576,1024]{1,0:T(8,128)(2,1)S(1)}, bf16[576,1024]{1,0:T(8,128)(2,1)}, u32[]{:S(2)}) copy-start(bf16[576,1024]{1,0:T(8,128)(2,1)} %copy-done) | copy-start | bytes 3538948
  120.0 42.6 %all-to-all-start.5 = ((bf16[64,80,128]{2,1,0:T(8,128)(2,1)}), bf16[64,80,128]{2,1,0:T(8,128)(2,1)}, u32[]{:S(2)}, u32[]{:S(2)}) async-start(bf16[64,80,128]{2,1,0:T(8,128)(2,1)} %bitcast.3), calls=%async_computation.5 | async-start | bytes 2621440 | tf_op jit(solution)/shard_map/all_to_all | solution.py:233
  133.1 31.5 %copy-start.8 = (bf16[72,128]{1,0:T(8,128)(2,1)S(1)}, bf16[72,128]{1,0:T(8,128)(2,1)}, u32[]{:S(2)}) copy-start(bf16[72,128]{1,0:T(8,128)(2,1)} %param.7) | copy-start | bytes 55300
  133.1 31.5 %copy-start.9 = (bf16[72,128]{1,0:T(8,128)(2,1)S(1)}, bf16[72,128]{1,0:T(8,128)(2,1)}, u32[]{:S(2)}) copy-start(bf16[72,128]{1,0:T(8,128)(2,1)} %param.6) | copy-start | bytes 55300

commit v3 on v2

v3 whole, which is shorter than its diff:
```python
import functools

import jax
import jax.numpy as jnp
from jax import lax
from jax.experimental import pallas as pl
from jax.experimental.pallas import tpu as pltpu
from jax.sharding import PartitionSpec as P

epsilon = 1e-05
F32 = jnp.float32
BF16 = jnp.bfloat16
AXES = ("tok", "row", "col")
SLOT = 256
EXTRA = 8
EXTRA_SENT = 16
NT_DIMS = (((1,), (1,)), ((), ()))
SMALL = pltpu.CompilerParams(vmem_limit_bytes=12 * 1024 * 1024)
LARGE = pltpu.CompilerParams(vmem_limit_bytes=24 * 1024 * 1024)


def split_wide(value):
    high = value.astype(BF16).astype(F32)
    return high, value - high


def mixed_groups(tok_count, row_count, col_count, even_along_tok):
    groups = []
    for row in range(row_count):
        if (row % 2 == 0) == even_along_tok:
            for col in range(col_count):
                groups.append([(tok * row_count + row) * col_count + col for tok in range(tok_count)])
        else:
            for tok in range(tok_count):
                groups.append([(tok * row_count + row) * col_count + col for col in range(col_count)])
    return groups


def weight_kernel(after_ref, gate_ref, up_ref, down_ref, out_ref):
    for place, weight in enumerate((gate_ref, up_ref, down_ref)):
        count, width = weight.shape
        out_ref[place, :count, :] = weight[...]
        out_ref[place, count:, :] = jnp.zeros((SLOT - count, width), BF16)


def forward_kernel(
    nt, nc, rows, count, odd_ref, blocks_ref, first_ref, w_ref, part_ref, tokens_ref, grads_ref, scaled_ref
):
    odd = odd_ref[0] == 1
    feats = blocks_ref.shape[2]
    gains = []
    for col in range(nc):
        late = blocks_ref[col, nt * 2 * rows :, :].astype(F32)
        early = first_ref[col, 2 * rows :, :].astype(F32)
        gains.append(jnp.where(odd, late, early)[0:1])
    totals = []
    for pair in range(nt // 2):
        at = pl.ds(pair * 2 * rows, 2 * rows)
        squares = jnp.zeros((2 * rows, feats), F32)
        for col in range(nc):
            two = []
            for tok in (2 * pair, 2 * pair + 1):
                outer, step = jnp.where(odd, col, tok), jnp.where(odd, tok, col)
                start = pl.multiple_of(step * (2 * rows), 16)
                two.append(blocks_ref[outer, pl.ds(start, 2 * rows), :].astype(F32))
            wide = jnp.concatenate([two[0][:rows], two[1][:rows]], axis=0)
            grads = jnp.concatenate([two[0][rows:], two[1][rows:]], axis=0)
            cols = pl.ds(col * feats, feats)
            tokens_ref[at, cols] = wide.astype(BF16)
            grads_ref[at, cols] = grads.astype(BF16)
            scaled_ref[at, cols] = (wide * gains[col]).astype(BF16)
            squares = squares + wide * wide
        totals.append(jnp.sum(squares, axis=1, keepdims=True))
    high, low = split_wide(jnp.concatenate(totals, axis=0))
    for place, source in enumerate((scaled_ref, scaled_ref, grads_ref)):
        value = lax.dot_general(source[...], w_ref[place], NT_DIMS, preferred_element_type=F32)
        if place == 0:
            lane = lax.broadcasted_iota(jnp.int32, value.shape, 1)
            value = jnp.where(lane == count, high, jnp.where(lane == count + 1, low, value))
        cols = pl.ds(place * SLOT, SLOT)
        for tok in range(nt):
            part_ref[tok, :, cols] = value[tok * rows : (tok + 1) * rows].astype(BF16)


def swiglu_kernel(model, count, parts_ref, packed_ref):
    sums = jnp.sum(parts_ref[...].astype(F32), axis=0)
    gate, up_proj, hidden_grad = sums[:, :SLOT], sums[:, SLOT : 2 * SLOT], sums[:, 2 * SLOT :]
    lane = lax.broadcasted_iota(jnp.int32, gate.shape, 1)
    at_squares = (lane >= count) & (lane < count + 2)
    squares = jnp.sum(jnp.where(at_squares, gate, 0.0), axis=1, keepdims=True)
    inv_rms = lax.rsqrt(squares / model + epsilon)
    gate = jnp.where(lane < count, gate * inv_rms, 0.0)
    up_proj = up_proj * inv_rms
    sig = jax.nn.sigmoid(gate)
    hidden = gate * sig * up_proj
    gate_grad = (hidden_grad * up_proj * sig * (1.0 + gate * (1.0 - sig))).astype(BF16)
    up_grad = (hidden_grad * gate * sig).astype(BF16)
    inner = jnp.sum(gate_grad.astype(F32) * gate + up_grad.astype(F32) * up_proj, axis=1, keepdims=True)
    for place, value in enumerate(split_wide(inner) + split_wide(inv_rms)):
        hidden = jnp.where(lane == count + place, value, hidden)
    packed_ref[:, :SLOT] = hidden.astype(BF16)
    packed_ref[:, SLOT : 2 * SLOT] = gate_grad
    packed_ref[:, 2 * SLOT :] = up_grad


def input_kernel(nt, rows, feats, count, packed_ref, gate_ref, up_ref, tokens_ref, out_ref, inv_ref, extra_ref):
    base = count % 128

    @pl.when(pl.program_id(0) == 0)
    def _():
        tail = packed_ref[:, SLOT - 128 : SLOT].astype(F32)
        lane = lax.broadcasted_iota(jnp.int32, tail.shape, 1)
        at_inv = (lane >= base + 2) & (lane < base + 4)
        inv_ref[...] = jnp.sum(jnp.where(at_inv, tail, 0.0), axis=1, keepdims=True)
        for tok in range(nt):
            piece = tail[tok * rows : (tok + 1) * rows]
            square = jnp.concatenate([piece, jnp.zeros((128 - rows, 128), F32)], axis=0)
            extra_ref[tok] = square.T[base : base + EXTRA]

    term = jnp.dot(packed_ref[:, SLOT : 2 * SLOT], gate_ref[0], preferred_element_type=F32)
    term = term + jnp.dot(packed_ref[:, 2 * SLOT :], up_ref[0], preferred_element_type=F32)
    gain_term = jnp.sum(term * (tokens_ref[...].astype(F32) * inv_ref[...]), axis=0, keepdims=True)
    high, low = split_wide(gain_term)
    spot = lax.broadcasted_iota(jnp.int32, (EXTRA, feats), 0)
    for part in range(gate_ref.shape[2] // feats):
        cols = slice(part * feats, (part + 1) * feats)
        for tok in range(nt):
            extra = jnp.where(spot == 2, high[:, cols], jnp.where(spot == 3, low[:, cols], extra_ref[tok]))
            block = jnp.concatenate([term[tok * rows : (tok + 1) * rows, cols], extra], axis=0)
            out_ref[tok, part] = block.astype(BF16)


def copy_kernel(copies, own_ref, out_ref):
    own = own_ref[...].astype(F32)
    gain = jnp.broadcast_to(own[-1:], (EXTRA_SENT, own.shape[1]))
    block = jnp.concatenate([own[:-1], gain], axis=0).astype(BF16)
    for copy in range(copies):
        out_ref[copy] = block


def message_kernel(rows, first_ref, out_ref):
    count = first_ref.shape[0]
    for at in range(count):
        out_ref[pl.ds(at * rows, rows), :] = first_ref[at, :rows, :]
    out_ref[count * rows :, :] = first_ref[0, rows:, :]


def final_kernel(model, blocks_ref, tokens_ref, grads_ref, gain_ref, inv_ref, tokens_out_ref, gain_out_ref):
    rows, feats = tokens_ref.shape
    total = lax.fori_loop(
        1,
        blocks_ref.shape[0],
        lambda at, running: running + blocks_ref[at].astype(F32),
        blocks_ref[0].astype(F32),
        unroll=7,
    )
    extra = total[rows:]
    turned = jnp.concatenate([extra, jnp.zeros((feats - EXTRA, feats), F32)], axis=0).T
    inner = (turned[:rows, 0:1] + turned[:rows, 1:2]) / model
    gain_out_ref[...] = extra[2:3] + extra[3:4]
    inv = inv_ref[...]
    scaled = tokens_ref[...].astype(F32) * inv
    weighted = total[:rows] * gain_ref[...].astype(F32)
    result = grads_ref[...].astype(F32) + inv * (weighted - scaled * inner)
    tokens_out_ref[...] = result.astype(BF16)


def whole(memory=pltpu.VMEM):
    return pl.BlockSpec(memory_space=memory)


def on_device(tokens, d_out, gain, gate_weight, up_weight, down_weight):
    nt, nr, nc = (lax.axis_size(a) for a in AXES)
    rows, feats = tokens.shape
    count = gate_weight.shape[0]
    width = nc * feats
    model = nr * width
    odd = lax.rem(lax.axis_index("row"), 2)
    odd_flag = odd.reshape(1).astype(jnp.int32)

    gain_row = gain.reshape(1, feats)
    tall = 2 * rows + EXTRA_SENT
    copies = pl.pallas_call(
        functools.partial(copy_kernel, nc),
        out_shape=jax.ShapeDtypeStruct((nc, tall, feats), BF16),
        in_specs=[whole()],
        out_specs=whole(),
        compiler_params=SMALL,
        name="own_copies",
    )(jnp.concatenate([tokens, d_out, gain_row], axis=0))
    first = mixed_groups(nt, nr, nc, False)
    stage = lax.all_to_all(copies, AXES, 0, 0, tiled=True, axis_index_groups=first)
    long = nc * 2 * rows + EXTRA_SENT
    message = pl.pallas_call(
        functools.partial(message_kernel, 2 * rows),
        out_shape=jax.ShapeDtypeStruct((long, feats), BF16),
        in_specs=[whole()],
        out_specs=whole(),
        compiler_params=SMALL,
        name="second_message",
    )(stage)
    copies = jnp.broadcast_to(message[None], (nt, long, feats))
    second = mixed_groups(nt, nr, nc, True)
    both = lax.all_to_all(copies, AXES, 0, 0, tiled=True, axis_index_groups=second)

    flops = 2 * nt * rows * width * SLOT
    weights = pl.pallas_call(
        weight_kernel,
        out_shape=jax.ShapeDtypeStruct((3, SLOT, width), BF16),
        grid=(1,),
        in_specs=[pl.BlockSpec((1, 16, feats), lambda j: (0, 0, 0))]
        + [pl.BlockSpec((count, width), lambda j: (0, 0))] * 3,
        out_specs=pl.BlockSpec((3, SLOT, width), lambda j: (0, 0, 0)),
        compiler_params=SMALL,
        cost_estimate=pl.CostEstimate(flops=0, bytes_accessed=12 * SLOT * width, transcendentals=0),
        name="padded_weights",
    )(stage, gate_weight, up_weight, down_weight)
    parts, tokens_all, grad_all = pl.pallas_call(
        functools.partial(forward_kernel, nt, nc, rows, count),
        out_shape=(
            jax.ShapeDtypeStruct((nt, rows, 3 * SLOT), BF16),
            jax.ShapeDtypeStruct((nt * rows, width), BF16),
            jax.ShapeDtypeStruct((nt * rows, width), BF16),
        ),
        in_specs=[whole(pltpu.SMEM)] + [whole()] * 3,
        out_specs=(whole(), whole(), whole()),
        scratch_shapes=[pltpu.VMEM((nt * rows, width), BF16)],
        compiler_params=LARGE,
        cost_estimate=pl.CostEstimate(flops=3 * flops, bytes_accessed=8 * nt * rows * width, transcendentals=0),
        name="forward_parts",
    )(odd_flag, both, stage, weights)
    parts = lax.all_to_all(parts, "row", 0, 0, tiled=True)
    packed = pl.pallas_call(
        functools.partial(swiglu_kernel, model, count),
        out_shape=jax.ShapeDtypeStruct((rows, 3 * SLOT), BF16),
        in_specs=[whole()],
        out_specs=whole(),
        compiler_params=SMALL,
        cost_estimate=pl.CostEstimate(flops=20 * rows * SLOT, bytes_accessed=8 * rows * SLOT * nr, transcendentals=rows * SLOT),
        name="swiglu_grads",
    )(parts)
    packed = lax.all_gather(packed, "row", axis=0, tiled=True)

    chunk = 2 * feats
    blocks = pl.pallas_call(
        functools.partial(input_kernel, nt, rows, feats, count),
        out_shape=jax.ShapeDtypeStruct((nt, nc, rows + EXTRA, feats), BF16),
        grid=(width // chunk,),
        in_specs=[
            whole(),
            pl.BlockSpec((1, SLOT, chunk), lambda j: (0, 0, j)),
            pl.BlockSpec((1, SLOT, chunk), lambda j: (1, 0, j)),
            pl.BlockSpec((nt * rows, chunk), lambda j: (0, j)),
        ],
        out_specs=pl.BlockSpec((nt, 2, rows + EXTRA, feats), lambda j: (0, j, 0, 0)),
        scratch_shapes=[pltpu.VMEM((nt * rows, 1), F32), pltpu.VMEM((nt, EXTRA, 128), F32)],
        compiler_params=LARGE,
        cost_estimate=pl.CostEstimate(flops=2 * flops, bytes_accessed=6 * nt * rows * width, transcendentals=0),
        name="input_grad_blocks",
    )(packed, weights, weights, tokens_all)
    blocks = lax.all_to_all(blocks.reshape(nt * nc, rows + EXTRA, feats), ("tok", "col"), 0, 0, tiled=True)

    terms = jnp.einsum(
        "btf,btd->bfd",
        packed[:, :count].reshape(nt, rows, count),
        grad_all.reshape(nt, rows, width),
        preferred_element_type=F32,
    )
    terms = lax.optimization_barrier(terms.astype(BF16))
    d_down = jnp.sum(terms.astype(F32), axis=0).astype(BF16)

    own = lax.dynamic_slice_in_dim(packed, lax.axis_index("tok") * rows, rows)
    inv_own = own[:, count + 2 : count + 3].astype(F32) + own[:, count + 3 : count + 4].astype(F32)
    d_tokens, d_gain = pl.pallas_call(
        functools.partial(final_kernel, model),
        out_shape=(
            jax.ShapeDtypeStruct((rows, feats), BF16),
            jax.ShapeDtypeStruct((1, feats), F32),
        ),
        in_specs=[whole()] * 5,
        out_specs=(whole(), whole()),
        compiler_params=SMALL,
        name="token_grads",
    )(blocks, tokens, d_out, gain_row, inv_own)
    d_gain = d_gain.reshape(feats)
    return (d_tokens, d_gain, d_down)


def solution(mesh):
    placed = (
        P("tok", ("row", "col")),
        P("tok", ("row", "col")),
        P(("row", "col")),
        P(("tok", "col"), "row"),
        P(("tok", "col"), "row"),
        P(("tok", "col"), "row"),
    )
    return jax.shard_map(
        on_device,
        mesh=mesh,
        in_specs=placed,
        out_specs=(P("tok", ("row", "col")), P(("row", "col")), P(("tok", "col"), "row")),
        check_vma=False,
    )
```

time: 166 us -> 146 us (0.88)
  waiting for transfers between devices: 73.7 us -> 62.8 us
  starting transfers between devices: 23.8 us -> 15.3 us
  local copies, waits for them, and re-layouts: 7.03 us -> 1.79 us
  blocking collectives: 44.9 us -> 49.9 us
  Pallas kernels: 4.83 us -> 7.77 us
  other arithmetic: 7.34 us -> 4.51 us
    all_to_all x3 -> x1, waiting for transfers between devices: 44.4 us -> 33.4 us  [on_device(): lax.all_to_all(copies, AXES, 0, 0, tiled=True, axis_index_groups=second)]
    all_to_all x3 -> x1, starting transfers between devices: 17.3 us -> 9.59 us  [on_device(): lax.all_to_all(copies, AXES, 0, 0, tiled=True, axis_index_groups=second)]
    all_to_all x2, blocking collectives: 31.3 us -> 36.3 us  [the longest x1 18.4 us: on_device(): parts = lax.all_to_all(parts, 'row', 0, 0, tiled=True)]
    unnamed x22 -> x16, local copies, waits for them, and re-layouts: 3.85 us -> 0.03 us
    pallas_call x2 -> x5, Pallas kernels: 1.59 us -> 4.45 us  [the longest x1 3.24 us: on_device(): pl.pallas_call(functools.partial(forward_kernel, nt, nc, rows, count), ou...]
  transfers between devices with their start and end apart: 4 -> 2, of which waited for: 4 -> 2; matrix products, arithmetic and copies ran while one was open for 4% -> 5% of each run, Pallas kernels for 1% -> 0%
where the time goes in v3:
time: 146 us
  waiting for transfers between devices  62.8 us (43%)
  blocking collectives  49.9 us (34%)
  starting transfers between devices  15.3 us (10%)
  Pallas kernels  7.77 us (5%)
  other arithmetic  4.51 us (3%)
  matrix products  2.98 us (2%)
  local copies, waits for them, and re-layouts  1.79 us (1%)
    all_to_all x1, waiting for transfers between devices, on_device(): lax.all_to_all(copies, AXES, 0, 0, tiled=True, axis_index_groups=second)  33.4 us
    all_to_all x1, waiting for transfers between devices, on_device(): lax.all_to_all(blocks.reshape(nt * nc, rows + EXTRA, feats), ('tok', 'col...  29.5 us
    all_to_all x1, blocking collectives, on_device(): parts = lax.all_to_all(parts, 'row', 0, 0, tiled=True)  18.4 us
    all_to_all x1, blocking collectives, on_device(): lax.all_to_all(copies, AXES, 0, 0, tiled=True, axis_index_groups=first)  17.9 us
    all_gather x1, blocking collectives, on_device(): packed = lax.all_gather(packed, 'row', axis=0, tiled=True)  13.6 us
    all_to_all x1, starting transfers between devices, on_device(): lax.all_to_all(copies, AXES, 0, 0, tiled=True, axis_index_groups=second)  9.59 us
    all_to_all x1, starting transfers between devices, on_device(): lax.all_to_all(blocks.reshape(nt * nc, rows + EXTRA, feats), ('tok', 'col...  5.68 us
    reduce_sum x1, other arithmetic, on_device(): d_down = jnp.sum(terms.astype(F32), axis=0).astype(BF16)  3.67 us
  transfers between devices with their start and end apart: 2, of which 2 were waited for; matrix products, arithmetic and copies ran while one was open for 5% of the time, Pallas kernels for 0%

profile of v3, /device:TPU:8, one launch (start us, length us, event | category | flops | bytes accessed | tf_op | source)
XLA Modules:
  0.0 145.8 jit_solution(4291605164165069349)
XLA Ops:
  0.6 0.8 pad_maximum_fusion.own_ref
  1.4 17.9 %all_to_all.20.first_ref.after_ref = bf16[8,160,128]{2,1,0:T(8,128)(2,1)S(1)} all-to-all(bf16[8,160,128]{2,1,0:T(8,128)(2,1)S(1)} %own_copies.1), channel_id=1, replica_groups={{0,1,2,3,4,5,6,7},{64,65,66,67,68,69,70,71},{128,129,130,131,132,133,13..., dimensions={0} | all-to-all | bytes 655360 | tf_op jit(solution)/shard_map/all_to_all | solution.py:192
  19.4 1.7 %broadcast_in_dim.2 = bf16[8,1168,128]{2,1,0:T(8,128)(2,1)} broadcast(bf16[1168,128]{1,0:T(8,128)(2,1)S(1)} %second_message.1), dimensions={1,2} | broadcast | bytes 2691072 | tf_op jit(solution)/shard_map/broadcast_in_dim | solution.py:202
  21.1 0.0 copy-start.2
  21.1 0.0 copy-start.3
  21.1 0.0 copy-start.4
  21.1 9.6 %all-to-all-start.1 = ((bf16[8,1168,128]{2,1,0:T(8,128)(2,1)}), bf16[8,1168,128]{2,1,0:T(8,128)(2,1)}, u32[]{:S(2)}, u32[]{:S(2)}) async-start(bf16[8,1168,128]{2,1,0:T(8,128)(2,1)} %broadcast_in_dim.2), calls=%async_computation.1 | async-start | bytes 4784128 | tf_op jit(solution)/shard_map/all_to_all | solution.py:204
  30.7 0.0 copy-done.2
  30.7 0.0 copy-done.3
  30.7 0.0 copy-done.4
  30.8 0.1 padded_weights.1.w_ref.gate_ref.up_ref
  30.9 33.4 %all-to-all-done.1.blocks_ref = bf16[8,1168,128]{2,1,0:T(8,128)(2,1)} async-done(((bf16[8,1168,128]{2,1,0:T(8,128)(2,1)}), bf16[8,1168,128]{2,1,0:T(8,128)(2,1)}, u32[]{:S(2)}, u32[]{:S(2)}) %all-to-all-start.1) | async-done | bytes 2392096 | tf_op jit(solution)/shard_map/all_to_all | solution.py:204
  64.2 3.2 %forward_parts.1 = (bf16[8,72,768]{2,1,0:T(8,128)(2,1)S(1)}, bf16[576,1024]{1,0:T(8,128)(2,1)S(1)}, bf16[576,1024]{1,0:T(8,128)(2,1)S(1)}) custom-call(s32[1]{0:T(128)} %bitcast.odd_ref, bf16[8,1168,128]{2,1,0:T(8,128)(2,1)} %all-to-all-done.1.blocks_ref, bf16[8,160,128]{2,1,0:T(8,128)(2,1)S(1)} %all_to_all.20.first_ref.after_ref, ...), custom_call_target="tpu_custom_call" | custom-call | flops 905969664 | bytes 4718592 | tf_op jit(solution)/shard_map/forward_parts/pallas_call | solution.py:218
  67.5 0.0 copy-start
  67.5 18.4 %all_to_all.21.parts_ref = bf16[8,72,768]{2,1,0:T(8,128)(2,1)S(1)} all-to-all(bf16[8,72,768]{2,1,0:T(8,128)(2,1)S(1)} %get-tuple-element.8), channel_id=1, replica_groups=mesh['tok'=8,'row'=8,'col'=8] {'row'}, dimensions={0} | all-to-all | bytes 1769472 | tf_op jit(solution)/shard_map/all_to_all | solution.py:232
  85.9 0.3 swiglu_grads.1
  86.2 0.0 copy-done
  86.2 13.6 %all_gather.3.packed_ref = bf16[576,768]{1,0:T(8,128)(2,1)S(1)} all-gather(bf16[72,768]{1,0:T(8,128)(2,1)S(1)} %swiglu_grads.1), channel_id=1, replica_groups=mesh['tok'=8,'row'=8,'col'=8] {'row'}, dimensions={0}, use_global_device_ids=true | all-gather | bytes 995328 | tf_op jit(solution)/shard_map/all_gather | solution.py:242
  99.7 3.1 %input_grad_blocks.1 = bf16[8,8,80,128]{3,2,1,0:T(8,128)(2,1)} custom-call(bf16[576,768]{1,0:T(8,128)(2,1)S(1)} %all_gather.3.packed_ref, bf16[3,256,1024]{2,1,0:T(8,128)(2,1)S(1)} %padded_weights.1.w_ref.gate_ref.up_ref, bf16[3,256,1024]{2,1,0:T(8,128)(2,1)S(1)} %padded_weights.1.w_ref.gate_ref.up_ref, bf16[576,1024]{1,0:T(8,128)(2,1)S(1)} %get-tuple-element.9.tokens_ref), custom_call_target="tpu_custom_call" | custom-call | flops 603979776 | bytes 3538944 | tf_op jit(solution)/shard_map/input_grad_blocks/pallas_call | solution.py:245
  102.8 0.0 copy-start.1
  102.8 5.7 %all-to-all-start.3 = ((bf16[64,80,128]{2,1,0:T(8,128)(2,1)}), bf16[64,80,128]{2,1,0:T(8,128)(2,1)S(1)}, u32[]{:S(2)}, u32[]{:S(2)}) async-start(bf16[64,80,128]{2,1,0:T(8,128)(2,1)} %bitcast.2), calls=%async_computation.3 | async-start | bytes 2621440 | tf_op jit(solution)/shard_map/all_to_all | solution.py:261
  108.5 0.0 copy-done.1
  108.5 3.0 %convolution_convert_fusion = bf16[8,224,1024]{2,1,0:T(8,128)(2,1)} fusion(bf16[8,72,224]{2,1,0:T(8,128)(2,1)S(1)} %bitcast.11, bf16[8,72,1024]{2,1,0:T(8,128)(2,1)S(1)} %bitcast.8), kind=kOutput, calls=%fused_computation | convolution fusion | flops 266076160 | bytes 5107712 | tf_op jit(solution)/shard_map/btf,btd->bfd/dot_general | solution.py:263
  111.5 0.0 copy-start.5
  111.5 0.0 copy-start.6
  111.5 0.0 copy-start.7
  111.5 3.7 %reduce_sum.12 = bf16[224,1024]{1,0:T(8,128)(2,1)} reduce(bf16[8,224,1024]{2,1,0:T(8,128)(2,1)} %convolution_convert_fusion, bf16[]{:T(256)} %constant.21.clone.1), dimensions={0}, to_apply=%region_0.0 | reduce | flops 1605632 | bytes 4128770 | tf_op jit(solution)/shard_map/reduce_sum | solution.py:270
  115.2 0.1 convert_add_fusion.inv_ref
  115.3 29.5 %all-to-all-done.3.blocks_ref = bf16[64,80,128]{2,1,0:T(8,128)(2,1)S(1)} async-done(((bf16[64,80,128]{2,1,0:T(8,128)(2,1)}), bf16[64,80,128]{2,1,0:T(8,128)(2,1)S(1)}, u32[]{:S(2)}, u32[]{:S(2)}) %all-to-all-start.3) | async-done | bytes 1310752 | tf_op jit(solution)/shard_map/all_to_all | solution.py:261
  144.7 0.0 copy-done.5
  144.7 0.0 copy-done.6
  144.7 0.0 copy-done.7
  144.7 1.1 token_grads.1
  (3 shorter events, 0.1 us)
Async XLA Ops:
  21.1 9.6 %copy-start.2 = (bf16[224,1024]{1,0:T(8,128)(2,1)S(1)}, bf16[224,1024]{1,0:T(8,128)(2,1)}, u32[]{:S(2)}) copy-start(bf16[224,1024]{1,0:T(8,128)(2,1)} %gate_ref.1) | copy-start | bytes 1376260
  21.1 9.6 %copy-start.3 = (bf16[224,1024]{1,0:T(8,128)(2,1)S(1)}, bf16[224,1024]{1,0:T(8,128)(2,1)}, u32[]{:S(2)}) copy-start(bf16[224,1024]{1,0:T(8,128)(2,1)} %up_ref.1) | copy-start | bytes 1376260
  21.1 9.6 %copy-start.4 = (bf16[224,1024]{1,0:T(8,128)(2,1)S(1)}, bf16[224,1024]{1,0:T(8,128)(2,1)}, u32[]{:S(2)}) copy-start(bf16[224,1024]{1,0:T(8,128)(2,1)} %down_ref.1) | copy-start | bytes 1376260
  21.1 43.1 %all-to-all-start.1 = ((bf16[8,1168,128]{2,1,0:T(8,128)(2,1)}), bf16[8,1168,128]{2,1,0:T(8,128)(2,1)}, u32[]{:S(2)}, u32[]{:S(2)}) async-start(bf16[8,1168,128]{2,1,0:T(8,128)(2,1)} %broadcast_in_dim.2), calls=%async_computation.1 | async-start | bytes 4784128 | tf_op jit(solution)/shard_map/all_to_all | solution.py:204
  67.5 18.7 %copy-start = (bf16[576,1024]{1,0:T(8,128)(2,1)}, bf16[576,1024]{1,0:T(8,128)(2,1)S(1)}, u32[]{:S(2)}) copy-start(bf16[576,1024]{1,0:T(8,128)(2,1)S(1)} %get-tuple-element.12) | copy-start | bytes 3538948
  102.8 5.7 %copy-start.1 = (bf16[576,1024]{1,0:T(8,128)(2,1)S(1)}, bf16[576,1024]{1,0:T(8,128)(2,1)}, u32[]{:S(2)}) copy-start(bf16[576,1024]{1,0:T(8,128)(2,1)} %copy-done) | copy-start | bytes 3538948
  102.8 41.9 %all-to-all-start.3 = ((bf16[64,80,128]{2,1,0:T(8,128)(2,1)}), bf16[64,80,128]{2,1,0:T(8,128)(2,1)S(1)}, u32[]{:S(2)}, u32[]{:S(2)}) async-start(bf16[64,80,128]{2,1,0:T(8,128)(2,1)} %bitcast.2), calls=%async_computation.3 | async-start | bytes 2621440 | tf_op jit(solution)/shard_map/all_to_all | solution.py:261
  111.5 33.2 %copy-start.5 = (bf16[72,128]{1,0:T(8,128)(2,1)S(1)}, bf16[72,128]{1,0:T(8,128)(2,1)}, u32[]{:S(2)}) copy-start(bf16[72,128]{1,0:T(8,128)(2,1)} %grads_ref.1) | copy-start | bytes 55300
  111.5 33.2 %copy-start.6 = (bf16[72,128]{1,0:T(8,128)(2,1)S(1)}, bf16[72,128]{1,0:T(8,128)(2,1)}, u32[]{:S(2)}) copy-start(bf16[72,128]{1,0:T(8,128)(2,1)} %tokens_ref.1) | copy-start | bytes 55300
  111.5 33.2 %copy-start.7 = (bf16[128]{0:T(256)(128)(2,1)S(1)}, bf16[128]{0:T(256)(128)(2,1)}, u32[]{:S(2)}) copy-start(bf16[128]{0:T(256)(128)(2,1)} %param.8) | copy-start | bytes 772

commit v4 on v3

v4 whole, which is shorter than its diff:
```python
import functools

import jax
import jax.numpy as jnp
from jax import lax
from jax.experimental import pallas as pl
from jax.experimental.pallas import tpu as pltpu
from jax.sharding import PartitionSpec as P

epsilon = 1e-05
F32 = jnp.float32
BF16 = jnp.bfloat16
AXES = ("tok", "row", "col")
SLOT = 256
EXTRA = 8
EXTRA_SENT = 16
WINDOW = 40
SHIFT = 32
TN_DIMS = (((0,), (0,)), ((), ()))
NT_DIMS = (((1,), (1,)), ((), ()))
SMALL = pltpu.CompilerParams(vmem_limit_bytes=12 * 1024 * 1024)
WIDE = pltpu.CompilerParams(vmem_limit_bytes=59 * 1024 * 1024)
LARGE = pltpu.CompilerParams(vmem_limit_bytes=24 * 1024 * 1024)


def split_wide(value):
    high = value.astype(BF16).astype(F32)
    return high, value - high


def mixed_groups(tok_count, row_count, col_count, even_along_tok):
    groups = []
    for row in range(row_count):
        if (row % 2 == 0) == even_along_tok:
            for col in range(col_count):
                groups.append([(tok * row_count + row) * col_count + col for tok in range(tok_count)])
        else:
            for tok in range(tok_count):
                groups.append([(tok * row_count + row) * col_count + col for col in range(col_count)])
    return groups


def weight_kernel(after_ref, gate_ref, up_ref, down_ref, out_ref, sent_ref):
    for place, weight in enumerate((gate_ref, up_ref, down_ref)):
        count, width = weight.shape
        out_ref[place, :count, :] = weight[...]
        out_ref[place, count:, :] = jnp.zeros((SLOT - count, width), BF16)
        if place < 2:
            sent_ref[place] = weight[...]


def valid_rows(shape, side):
    row = lax.broadcasted_iota(jnp.int32, shape, 0)
    return (row >= 4 * side) & (row < WINDOW - 4 + 4 * side)


def join_windows(low, high):
    row = lax.broadcasted_iota(jnp.int32, (8,) + low.shape[1:], 0)
    shared = jnp.where(row < 4, low[SHIFT:], high[: WINDOW - SHIFT])
    return jnp.concatenate([low[:SHIFT], shared, high[WINDOW - SHIFT :]], axis=0)


def block_pair(blocks_ref, odd, pair, col, rows):
    two = []
    for tok in (2 * pair, 2 * pair + 1):
        outer, step = jnp.where(odd, col, tok), jnp.where(odd, tok, col)
        start = pl.multiple_of(step * (2 * rows), 16)
        two.append(blocks_ref[outer, pl.ds(start, 2 * rows), :].astype(F32))
    return two


def forward_kernel(
    nt, nc, rows, count, flag_ref, blocks_ref, first_ref, w_ref, part_ref, grads_ref, scaled_ref
):
    odd = flag_ref[0] == 1
    feats = blocks_ref.shape[2]
    gains = []
    for col in range(nc):
        late = blocks_ref[col, nt * 2 * rows :, :].astype(F32)
        early = first_ref[col, 2 * rows :, :].astype(F32)
        gains.append(jnp.where(odd, late, early)[0:1])
    totals = []
    for pair in range(nt // 2):
        at = pl.ds(pair * 2 * rows, 2 * rows)
        squares = jnp.zeros((2 * rows, feats), F32)
        for col in range(nc):
            two = block_pair(blocks_ref, odd, pair, col, rows)
            wide = jnp.concatenate([two[0][:rows], two[1][:rows]], axis=0)
            grads = jnp.concatenate([two[0][rows:], two[1][rows:]], axis=0)
            cols = pl.ds(col * feats, feats)
            grads_ref[at, cols] = grads.astype(BF16)
            scaled_ref[at, cols] = (wide * gains[col]).astype(BF16)
            squares = squares + wide * wide
        totals.append(jnp.sum(squares, axis=1, keepdims=True))
    high, low = split_wide(jnp.concatenate(totals, axis=0))
    for place, source in enumerate((scaled_ref, scaled_ref, grads_ref)):
        value = lax.dot_general(source[...], w_ref[place], NT_DIMS, preferred_element_type=F32)
        if place == 0:
            lane = lax.broadcasted_iota(jnp.int32, value.shape, 1)
            value = jnp.where(lane == count, high, jnp.where(lane == count + 1, low, value))
        cols = pl.ds(place * SLOT, SLOT)
        for tok in range(nt):
            for half in range(2):
                start = tok * rows + half * SHIFT
                part_ref[2 * tok + half, :, cols] = value[start : start + WINDOW].astype(BF16)


def windows_kernel(nt, nc, rows, flag_ref, blocks_ref, after_ref, tokens_ref, grads_ref):
    odd = flag_ref[0] == 1
    side = flag_ref[1] == 1
    feats = blocks_ref.shape[2]
    for pair in range(nt // 2):
        at = pl.ds(pair * 2 * WINDOW, 2 * WINDOW)
        for col in range(nc):
            two = block_pair(blocks_ref, odd, pair, col, rows)
            cols = pl.ds(col * feats, feats)
            low, high = [], []
            for start in (0, rows):
                low.append(jnp.concatenate([half[start : start + WINDOW] for half in two], axis=0))
                late = start + SHIFT
                high.append(jnp.concatenate([half[late : late + WINDOW] for half in two], axis=0))
            tokens_ref[at, cols] = jnp.where(side, high[0], low[0]).astype(BF16)
            grads_ref[0, at, cols] = jnp.where(side, high[1], low[1]).astype(BF16)
            grads_ref[1, at, cols] = jnp.where(side, low[1], high[1]).astype(BF16)


def swiglu_kernel(model, count, flag_ref, parts_ref, packed_ref):
    side = flag_ref[1]
    members = parts_ref.shape[0] // 2

    def summed(parity):
        total = parts_ref[parity].astype(F32)
        for at in range(1, members):
            total = total + parts_ref[2 * at + parity].astype(F32)
        return total

    inner = jnp.zeros((WINDOW, 1), F32)
    inv_rms = None
    for place, parity in enumerate((side, 1 - side)):
        sums = summed(parity)
        gate, up_proj, hidden_grad = sums[:, :SLOT], sums[:, SLOT : 2 * SLOT], sums[:, 2 * SLOT :]
        lane = lax.broadcasted_iota(jnp.int32, gate.shape, 1)
        if place == 0:
            at_squares = (lane >= count) & (lane < count + 2)
            squares = jnp.sum(jnp.where(at_squares, gate, 0.0), axis=1, keepdims=True)
            inv_rms = lax.rsqrt(squares / model + epsilon)
        keep = valid_rows(gate.shape, side) & (lane < count)
        gate = jnp.where(keep, gate * inv_rms, 0.0)
        up_proj = up_proj * inv_rms
        sig = jax.nn.sigmoid(gate)
        hidden = jnp.where(keep, gate * sig * up_proj, 0.0)
        gate_grad = jnp.where(keep, hidden_grad * up_proj * sig * (1.0 + gate * (1.0 - sig)), 0.0)
        up_grad = jnp.where(keep, hidden_grad * gate * sig, 0.0)
        gate_grad, up_grad = gate_grad.astype(BF16), up_grad.astype(BF16)
        inner_term = gate_grad.astype(F32) * gate + up_grad.astype(F32) * up_proj
        inner = inner + jnp.sum(inner_term, axis=1, keepdims=True)
        packed_ref[:, (2 * place) * SLOT : (2 * place + 1) * SLOT] = gate_grad
        packed_ref[:, (2 * place + 1) * SLOT : (2 * place + 2) * SLOT] = up_grad
        packed_ref[:, (4 + place) * SLOT : (5 + place) * SLOT] = hidden.astype(BF16)
    own = packed_ref[:, :SLOT].astype(F32)
    lane = lax.broadcasted_iota(jnp.int32, own.shape, 1)
    for place, value in enumerate((split_wide(inner) + split_wide(inv_rms)) * 2):
        own = jnp.where(lane == count + place, value, own)
    packed_ref[:, :SLOT] = own.astype(BF16)


def input_kernel(
    nt,
    shares,
    feats,
    count,
    flag_ref,
    packed_ref,
    own_ref,
    other_ref,
    tokens_ref,
    out_ref,
    inv_ref,
    extra_ref,
):
    base = count % 128
    side = flag_ref[1]
    spot = lax.broadcasted_iota(jnp.int32, (EXTRA, feats), 0) % 4

    @pl.when(pl.program_id(0) == 0)
    def _():
        tail = packed_ref[:, SLOT - 128 : SLOT].astype(F32)
        lane = lax.broadcasted_iota(jnp.int32, tail.shape, 1)
        at_inv = (lane >= base + 2) & (lane < base + 4)
        inv_ref[...] = jnp.sum(jnp.where(at_inv, tail, 0.0), axis=1, keepdims=True)
        for tok in range(nt):
            piece = tail[tok * WINDOW : (tok + 1) * WINDOW]
            square = jnp.concatenate([piece, jnp.zeros((128 - WINDOW, 128), F32)], axis=0)
            turned = square.T[base : base + EXTRA]
            share = jnp.where(flag_ref[2] == 1, turned[3:4], turned[2:3]) * (1.0 / shares)
            extra_ref[tok] = jnp.where(spot == 3, share, turned)

    fill = jnp.zeros((SLOT - count, own_ref.shape[2]), BF16)
    weights = [own_ref[0], own_ref[1]]
    weights += [jnp.concatenate([other_ref[place], fill], axis=0) for place in range(2)]
    term = jnp.zeros((packed_ref.shape[0], own_ref.shape[2]), F32)
    for place, weight in enumerate(weights):
        values = packed_ref[:, place * SLOT : (place + 1) * SLOT]
        term = term + jnp.dot(values, weight, preferred_element_type=F32)
    gain_term = jnp.sum(term * (tokens_ref[...].astype(F32) * inv_ref[...]), axis=0, keepdims=True)
    keep = valid_rows((WINDOW, feats), side)
    for part in range(own_ref.shape[2] // feats):
        cols = slice(part * feats, (part + 1) * feats)
        for tok in range(nt):
            extra = jnp.where(spot == 2, gain_term[:, cols], extra_ref[tok])
            extra = jnp.concatenate([extra] * (WINDOW // EXTRA), axis=0)
            block = jnp.where(keep, term[tok * WINDOW : (tok + 1) * WINDOW, cols], extra)
            out_ref[tok, part] = block.astype(BF16)


def down_mine_kernel(hidden_ref, grads_ref, out_ref):
    out_ref[...] = lax.dot_general(hidden_ref[...], grads_ref[0], TN_DIMS, preferred_element_type=F32)


def down_other_kernel(hidden_ref, grads_ref, mine_ref, out_ref):
    total = lax.dot_general(hidden_ref[...], grads_ref[0], TN_DIMS, preferred_element_type=F32)
    out_ref[...] = (total + mine_ref[...])[: out_ref.shape[0]].astype(BF16)


def copy_kernel(copies, own_ref, out_ref):
    own = own_ref[...].astype(F32)
    gain = jnp.broadcast_to(own[-1:], (EXTRA_SENT, own.shape[1]))
    block = jnp.concatenate([own[:-1], gain], axis=0).astype(BF16)
    for copy in range(copies):
        out_ref[copy] = block


def message_kernel(rows, first_ref, out_ref):
    count = first_ref.shape[0]
    for at in range(count):
        out_ref[pl.ds(at * rows, rows), :] = first_ref[at, :rows, :]
    out_ref[count * rows :, :] = first_ref[0, rows:, :]


def final_kernel(model, blocks_ref, tokens_ref, grads_ref, gain_ref, tokens_out_ref, gain_out_ref):
    rows, feats = tokens_ref.shape

    def add(at, sums):
        return (
            sums[0] + blocks_ref[2 * at].astype(F32),
            sums[1] + blocks_ref[2 * at + 1].astype(F32),
        )

    start = (blocks_ref[0].astype(F32), blocks_ref[1].astype(F32))
    low, high = lax.fori_loop(1, blocks_ref.shape[0] // 2, add, start)
    rest = jnp.zeros((feats - EXTRA, feats), F32)
    low_turned = jnp.concatenate([low[SHIFT:], rest], axis=0).T[:WINDOW]
    high_turned = jnp.concatenate([high[:EXTRA], rest], axis=0).T[:WINDOW]
    inner = join_windows(low_turned[:, 4:5] + low_turned[:, 5:6], high_turned[:, 0:1] + high_turned[:, 1:2])
    inner = inner / model
    inv = join_windows(low_turned[:, 7:8], high_turned[:, 3:4])
    gain_out_ref[...] = low[SHIFT + 6 : SHIFT + 7] + high[2:3]
    scaled = tokens_ref[...].astype(F32) * inv
    weighted = join_windows(low, high) * gain_ref[...].astype(F32)
    result = grads_ref[...].astype(F32) + inv * (weighted - scaled * inner)
    tokens_out_ref[...] = result.astype(BF16)


def whole(memory=pltpu.VMEM):
    return pl.BlockSpec(memory_space=memory)


def on_device(tokens, d_out, gain, gate_weight, up_weight, down_weight):
    nt, nr, nc = (lax.axis_size(a) for a in AXES)
    rows, feats = tokens.shape
    count = gate_weight.shape[0]
    width = nc * feats
    model = nr * width
    flags = jnp.stack([lax.rem(lax.axis_index(a), 2) for a in ("row", "col", "tok")]).astype(jnp.int32)

    neighbours = [(at, at ^ 1) for at in range(nc)]
    gain_row = gain.reshape(1, feats)
    tall = 2 * rows + EXTRA_SENT
    copies = pl.pallas_call(
        functools.partial(copy_kernel, nc),
        out_shape=jax.ShapeDtypeStruct((nc, tall, feats), BF16),
        in_specs=[whole()],
        out_specs=whole(),
        compiler_params=SMALL,
        name="own_copies",
    )(jnp.concatenate([tokens, d_out, gain_row], axis=0))
    first = mixed_groups(nt, nr, nc, False)
    stage = lax.all_to_all(copies, AXES, 0, 0, tiled=True, axis_index_groups=first)
    long = nc * 2 * rows + EXTRA_SENT
    message = pl.pallas_call(
        functools.partial(message_kernel, 2 * rows),
        out_shape=jax.ShapeDtypeStruct((long, feats), BF16),
        in_specs=[whole()],
        out_specs=whole(),
        compiler_params=SMALL,
        name="second_message",
    )(stage)
    copies = jnp.broadcast_to(message[None], (nt, long, feats))
    second = mixed_groups(nt, nr, nc, True)
    both = lax.all_to_all(copies, AXES, 0, 0, tiled=True, axis_index_groups=second)

    flops = 2 * nt * rows * width * SLOT
    weights, sent = pl.pallas_call(
        weight_kernel,
        out_shape=(
            jax.ShapeDtypeStruct((3, SLOT, width), BF16),
            jax.ShapeDtypeStruct((2, count, width), BF16),
        ),
        in_specs=[whole(pl.ANY)] + [whole()] * 3,
        out_specs=(whole(), whole()),
        compiler_params=SMALL,
        cost_estimate=pl.CostEstimate(flops=0, bytes_accessed=12 * SLOT * width, transcendentals=0),
        name="padded_weights",
    )(stage, gate_weight, up_weight, down_weight)
    parts = pl.pallas_call(
        functools.partial(forward_kernel, nt, nc, rows, count),
        out_shape=jax.ShapeDtypeStruct((2 * nt, WINDOW, 3 * SLOT), BF16),
        in_specs=[whole(pltpu.SMEM)] + [whole()] * 3,
        out_specs=whole(),
        scratch_shapes=[pltpu.VMEM((nt * rows, width), BF16)] * 2,
        compiler_params=LARGE,
        cost_estimate=pl.CostEstimate(flops=3 * flops, bytes_accessed=8 * nt * rows * width, transcendentals=0),
        name="forward_parts",
    )(flags, both, stage, weights)
    tokens_all, grad_all = pl.pallas_call(
        functools.partial(windows_kernel, nt, nc, rows),
        out_shape=(
            jax.ShapeDtypeStruct((nt * WINDOW, width), BF16),
            jax.ShapeDtypeStruct((2, nt * WINDOW, width), BF16),
        ),
        in_specs=[whole(pltpu.SMEM), whole(), whole(pl.ANY)],
        out_specs=(whole(), whole()),
        compiler_params=LARGE,
        cost_estimate=pl.CostEstimate(flops=0, bytes_accessed=8 * nt * rows * width, transcendentals=0),
        name="token_windows",
    )(flags, both, parts)
    sent, parts = lax.optimization_barrier((sent, parts))
    sent = lax.ppermute(sent, "col", neighbours)
    pairs = [
        [(tok * nr + row) * nc + 2 * pair + side for row in range(nr) for side in range(2)]
        for tok in range(nt)
        for pair in range(nc // 2)
    ]
    parts = lax.all_to_all(parts, AXES, 0, 0, tiled=True, axis_index_groups=pairs)
    packed = pl.pallas_call(
        functools.partial(swiglu_kernel, model, count),
        out_shape=jax.ShapeDtypeStruct((WINDOW, 6 * SLOT), BF16),
        in_specs=[whole(pltpu.SMEM), whole()],
        out_specs=whole(),
        compiler_params=SMALL,
        cost_estimate=pl.CostEstimate(
            flops=40 * WINDOW * SLOT, bytes_accessed=16 * WINDOW * SLOT * nr, transcendentals=2 * WINDOW * SLOT
        ),
        name="swiglu_grads",
    )(flags, parts)
    packed = lax.all_gather(packed, "row", axis=0, tiled=True)

    chunk = 2 * feats
    blocks = pl.pallas_call(
        functools.partial(input_kernel, nt, nt * nc // 4, feats, count),
        out_shape=jax.ShapeDtypeStruct((nt, nc, WINDOW, feats), BF16),
        grid=(width // chunk,),
        in_specs=[
            whole(pltpu.SMEM),
            whole(),
            pl.BlockSpec((2, SLOT, chunk), lambda j: (0, 0, j)),
            pl.BlockSpec((2, count, chunk), lambda j: (0, 0, j)),
            pl.BlockSpec((nt * WINDOW, chunk), lambda j: (0, j)),
        ],
        out_specs=pl.BlockSpec((nt, 2, WINDOW, feats), lambda j: (0, j, 0, 0)),
        scratch_shapes=[pltpu.VMEM((nt * WINDOW, 1), F32), pltpu.VMEM((nt, EXTRA, 128), F32)],
        compiler_params=LARGE,
        cost_estimate=pl.CostEstimate(flops=2 * flops, bytes_accessed=6 * nt * rows * width, transcendentals=0),
        name="input_grad_blocks",
    )(flags, packed, weights, sent, tokens_all)
    blocks = lax.all_to_all(blocks.reshape(nt * nc, WINDOW, feats), ("tok", "col"), 0, 0, tiled=True)

    hidden_other = lax.ppermute(packed[:, 5 * SLOT :], "col", neighbours)
    half_chunk = width // 2
    down_cost = pl.CostEstimate(flops=flops // 2, bytes_accessed=3 * nt * rows * width, transcendentals=0)
    mine = pl.pallas_call(
        down_mine_kernel,
        out_shape=jax.ShapeDtypeStruct((SLOT, width), F32),
        grid=(2,),
        in_specs=[
            pl.BlockSpec((nt * WINDOW, SLOT), lambda j: (0, 4)),
            pl.BlockSpec((1, nt * WINDOW, half_chunk), lambda j: (0, 0, j)),
        ],
        out_specs=pl.BlockSpec((SLOT, half_chunk), lambda j: (0, j)),
        compiler_params=LARGE,
        cost_estimate=down_cost,
        name="down_grads_mine",
    )(packed, grad_all)
    d_down = pl.pallas_call(
        down_other_kernel,
        out_shape=jax.ShapeDtypeStruct((count, width), BF16),
        grid=(2,),
        in_specs=[
            pl.BlockSpec((nt * WINDOW, SLOT), lambda j: (0, 0)),
            pl.BlockSpec((1, nt * WINDOW, half_chunk), lambda j: (1, 0, j)),
            pl.BlockSpec((SLOT, half_chunk), lambda j: (0, j)),
        ],
        out_specs=pl.BlockSpec((count, half_chunk), lambda j: (0, j)),
        compiler_params=LARGE,
        cost_estimate=down_cost,
        name="down_grads",
    )(hidden_other, grad_all, mine)

    d_tokens, d_gain = pl.pallas_call(
        functools.partial(final_kernel, model),
        out_shape=(
            jax.ShapeDtypeStruct((rows, feats), BF16),
            jax.ShapeDtypeStruct((1, feats), F32),
        ),
        in_specs=[whole()] * 4,
        out_specs=(whole(), whole()),
        compiler_params=SMALL,
        name="token_grads",
    )(blocks, tokens, d_out, gain_row)
    d_gain = d_gain.reshape(feats)
    return (d_tokens, d_gain, d_down)


def solution(mesh):
    placed = (
        P("tok", ("row", "col")),
        P("tok", ("row", "col")),
        P(("row", "col")),
        P(("tok", "col"), "row"),
        P(("tok", "col"), "row"),
        P(("tok", "col"), "row"),
    )
    return jax.shard_map(
        on_device,
        mesh=mesh,
        in_specs=placed,
        out_specs=(P("tok", ("row", "col")), P(("row", "col")), P(("tok", "col"), "row")),
        check_vma=False,
    )
```

time: 146 us -> 142 us (0.973)
  the two profiles are of different devices: /device:TPU:8 before, /device:TPU:10 now
where the time goes in v4:
time: 142 us; the launch traced here: 141 us
  waiting for transfers between devices  59 us (42%)
  blocking collectives  30.3 us (21%)
  starting transfers between devices  26.8 us (19%)
  Pallas kernels  12.9 us (9%)
  local copies, waits for them, and re-layouts  10.3 us (7%)
    all_to_all x1, waiting for transfers between devices, on_device(): lax.all_to_all(copies, AXES, 0, 0, tiled=True, axis_index_groups=second)  29 us
    all_to_all x1, blocking collectives, on_device(): lax.all_to_all(copies, AXES, 0, 0, tiled=True, axis_index_groups=first)  17.1 us
    ppermute x1, waiting for transfers between devices, on_device(): hidden_other = lax.ppermute(packed[:, 5 * SLOT:], 'col', neighbours)  14.9 us
    all_gather x1, blocking collectives, on_device(): packed = lax.all_gather(packed, 'row', axis=0, tiled=True)  13.2 us
    all_to_all x1, starting transfers between devices, on_device(): lax.all_to_all(copies, AXES, 0, 0, tiled=True, axis_index_groups=second)  10.4 us
    unnamed x28, local copies, waits for them, and re-layouts  8.57 us
    all_to_all x1, waiting for transfers between devices, on_device(): lax.all_to_all(parts, AXES, 0, 0, tiled=True, axis_index_groups=pairs)  6.96 us
    all_to_all x1, starting transfers between devices, on_device(): lax.all_to_all(parts, AXES, 0, 0, tiled=True, axis_index_groups=pairs)  5.75 us
  transfers between devices with their start and end apart: 5, of which 5 were waited for; matrix products, arithmetic and copies ran while one was open for 0% of the time, Pallas kernels for 3%

profile of v4, /device:TPU:10, one launch (start us, length us, event | category | flops | bytes accessed | tf_op | source)
XLA Modules:
  0.0 141.0 jit_solution(16573369343710733265)
XLA Ops:
  0.6 0.8 pad_maximum_fusion.own_ref
  1.4 17.1 %all_to_all.20.after_ref.first_ref = bf16[8,160,128]{2,1,0:T(8,128)(2,1)S(1)} all-to-all(bf16[8,160,128]{2,1,0:T(8,128)(2,1)S(1)} %own_copies.1), channel_id=1, replica_groups={{0,1,2,3,4,5,6,7},{64,65,66,67,68,69,70,71},{128,129,130,131,132,133,13..., dimensions={0} | all-to-all | bytes 655360 | tf_op jit(solution)/shard_map/all_to_all | solution.py:288
  18.5 1.8 %broadcast_in_dim.2 = bf16[8,1168,128]{2,1,0:T(8,128)(2,1)} broadcast(bf16[1168,128]{1,0:T(8,128)(2,1)S(1)} %second_message.1), dimensions={1,2} | broadcast | bytes 2691072 | tf_op jit(solution)/shard_map/broadcast_in_dim | solution.py:298
  20.3 0.0 copy-start.7
  20.3 10.4 %all-to-all-start.1 = ((bf16[8,1168,128]{2,1,0:T(8,128)(2,1)}), bf16[8,1168,128]{2,1,0:T(8,128)(2,1)S(1)}, u32[]{:S(2)}, u32[]{:S(2)}) async-start(bf16[8,1168,128]{2,1,0:T(8,128)(2,1)} %broadcast_in_dim.2), calls=%async_computation.1 | async-start | bytes 4784128 | tf_op jit(solution)/shard_map/all_to_all | solution.py:300
  30.7 0.1 pad_add_fusion.flag_ref
  30.8 0.0 copy-done.7
  30.8 0.0 copy-start.8
  30.8 1.0 copy-done.8
  31.8 0.0 copy-start.9
  31.9 1.0 copy-done.9
  32.9 0.2 padded_weights.1
  33.0 0.0 copy-start
  33.0 1.2 copy-done
  34.2 0.0 copy-start.13
  34.2 0.9 copy-done.13
  35.2 29.0 %all-to-all-done.1.blocks_ref = bf16[8,1168,128]{2,1,0:T(8,128)(2,1)S(1)} async-done(((bf16[8,1168,128]{2,1,0:T(8,128)(2,1)}), bf16[8,1168,128]{2,1,0:T(8,128)(2,1)S(1)}, u32[]{:S(2)}, u32[]{:S(2)}) %all-to-all-start.1) | async-done | bytes 2392096 | tf_op jit(solution)/shard_map/all_to_all | solution.py:300
  64.1 0.0 copy-start.1
  64.1 1.4 copy-done.1
  65.6 2.9 %forward_parts.1.after_ref = bf16[16,40,768]{2,1,0:T(8,128)(2,1)} custom-call(s32[3]{0:T(128)S(1)} %pad_add_fusion.flag_ref, bf16[8,1168,128]{2,1,0:T(8,128)(2,1)S(1)} %all-to-all-done.1.blocks_ref, bf16[8,160,128]{2,1,0:T(8,128)(2,1)S(1)} %all_to_all.20.after_ref.first_ref, bf16[3,256,1024]{2,1,0:T(8,128)(2,1)S(1)} %copy-done.1), custom_call_target="tpu_custom_call" | custom-call | flops 905969664 | bytes 4718592 | tf_op jit(solution)/shard_map/forward_parts/pallas_call | solution.py:315
  68.5 5.7 %all-to-all-start.2 = ((bf16[16,40,768]{2,1,0:T(8,128)(2,1)}), bf16[16,40,768]{2,1,0:T(8,128)(2,1)S(1)}, u32[]{:S(2)}, u32[]{:S(2)}) async-start(bf16[16,40,768]{2,1,0:T(8,128)(2,1)} %forward_parts.1.after_ref), calls=%async_computation.2 | async-start | bytes 1966080 | tf_op jit(solution)/shard_map/all_to_all | solution.py:344
  74.2 2.5 %collective-permute-start = (bf16[2,224,1024]{2,1,0:T(8,128)(2,1)}, bf16[2,224,1024]{2,1,0:T(8,128)(2,1)}, u32[]{:S(2)}, u32[]{:S(2)}) collective-permute-start(bf16[2,224,1024]{2,1,0:T(8,128)(2,1)} %copy-done.13), channel_id=1, source_target_pairs={{0,1},{1,0},{2,3},{3,2},{4,5},{5,4},{6,7},{7,6},{8,9},{9,8},{10,11... | collective-permute-start | bytes 2752520 | tf_op jit(solution)/shard_map/ppermute | solution.py:338
  76.7 1.1 token_windows.1
  77.8 0.0 copy-start.3
  77.8 1.1 copy-done.3
  78.9 0.0 copy-start.5
  78.9 0.8 copy-done.5
  79.7 0.0 copy-start.2
  79.7 7.0 %all-to-all-done.2.parts_ref = bf16[16,40,768]{2,1,0:T(8,128)(2,1)S(1)} async-done(((bf16[16,40,768]{2,1,0:T(8,128)(2,1)}), bf16[16,40,768]{2,1,0:T(8,128)(2,1)S(1)}, u32[]{:S(2)}, u32[]{:S(2)}) %all-to-all-start.2) | async-done | bytes 983072 | tf_op jit(solution)/shard_map/all_to_all | solution.py:344
  86.7 0.8 swiglu_grads.1
  87.5 13.2 %all_gather.3.packed_ref.hidden_ref = bf16[320,1536]{1,0:T(8,128)(2,1)S(1)} all-gather(bf16[40,1536]{1,0:T(8,128)(2,1)S(1)} %swiglu_grads.1), channel_id=1, replica_groups=mesh['tok'=8,'row'=8,'col'=8] {'row'}, dimensions={0}, use_global_device_ids=true | all-gather | bytes 1105920 | tf_op jit(solution)/shard_map/all_gather | solution.py:356
  100.8 5.6 %collective-permute-done.other_ref = bf16[2,224,1024]{2,1,0:T(8,128)(2,1)} collective-permute-done((bf16[2,224,1024]{2,1,0:T(8,128)(2,1)}, bf16[2,224,1024]{2,1,0:T(8,128)(2,1)}, u32[]{:S(2)}, u32[]{:S(2)}) %collective-permute-start) | collective-permute-done | bytes 917536 | tf_op jit(solution)/shard_map/ppermute | solution.py:338
  106.3 0.0 copy-done.2
  106.3 0.0 copy-start.6
  106.3 1.1 copy-done.6
  107.4 4.3 %input_grad_blocks.1 = bf16[8,8,40,128]{3,2,1,0:T(8,128)(2,1)} custom-call(s32[3]{0:T(128)S(1)} %pad_add_fusion.flag_ref, bf16[320,1536]{1,0:T(8,128)(2,1)S(1)} %all_gather.3.packed_ref.hidden_ref, bf16[3,256,1024]{2,1,0:T(8,128)(2,1)S(1)} %copy-done.2, bf16[2,224,1024]{2,1,0:T(8,128)(2,1)} %collective-permute-done.other_ref, bf16[320,1024]{1,0:T(8,128)(2,1)S(1)} %copy-done.6), custom_call_target="tpu_custom_call" | custom-call | flops 603979776 | bytes 3538944 | tf_op jit(solution)/shard_map/input_grad_blocks/pallas_call | solution.py:359
  111.7 0.0 copy-start.4
  111.7 5.7 %all-to-all-start.3 = ((bf16[64,40,128]{2,1,0:T(8,128)(2,1)}), bf16[64,40,128]{2,1,0:T(8,128)(2,1)S(1)}, u32[]{:S(2)}, u32[]{:S(2)}) async-start(bf16[64,40,128]{2,1,0:T(8,128)(2,1)} %bitcast.4), calls=%async_computation.3 | async-start | bytes 1310720 | tf_op jit(solution)/shard_map/all_to_all | solution.py:376
  117.4 2.5 %collective-permute-start.1 = (bf16[320,256]{1,0:T(8,128)(2,1)S(1)}, bf16[320,256]{1,0:T(8,128)(2,1)S(1)}, u32[]{:S(2)}, u32[]{:S(2)}) collective-permute-start(bf16[320,256]{1,0:T(8,128)(2,1)S(1)} %slice.4), channel_id=1, source_target_pairs={{0,1},{1,0},{2,3},{3,2},{4,5},{5,4},{6,7},{7,6},{8,9},{9,8},{10,11... | collective-permute-start | bytes 491528 | tf_op jit(solution)/shard_map/ppermute | solution.py:378
  119.9 0.0 copy-done.4
  119.9 0.0 copy-start.10
  119.9 0.0 copy-start.11
  119.9 0.0 copy-start.12
  119.9 0.8 down_grads_mine.1.mine_ref
  120.8 14.9 %collective-permute-done.1.hidden_ref = bf16[320,256]{1,0:T(8,128)(2,1)S(1)} collective-permute-done((bf16[320,256]{1,0:T(8,128)(2,1)S(1)}, bf16[320,256]{1,0:T(8,128)(2,1)S(1)}, u32[]{:S(2)}, u32[]{:S(2)}) %collective-permute-start.1) | collective-permute-done | bytes 163872 | tf_op jit(solution)/shard_map/ppermute | solution.py:378
  135.7 1.5 %down_grads.1 = bf16[224,1024]{1,0:T(8,128)(2,1)} custom-call(bf16[320,256]{1,0:T(8,128)(2,1)S(1)} %collective-permute-done.1.hidden_ref, bf16[2,320,1024]{2,1,0:T(8,128)(2,1)S(1)} %copy-done.4, f32[256,1024]{1,0:T(8,128)S(1)} %down_grads_mine.1.mine_ref), custom_call_target="tpu_custom_call" | custom-call | flops 150994944 | bytes 1769472 | tf_op jit(solution)/shard_map/down_grads/pallas_call | solution.py:394
  137.2 2.6 %all-to-all-done.3.blocks_ref = bf16[64,40,128]{2,1,0:T(8,128)(2,1)S(1)} async-done(((bf16[64,40,128]{2,1,0:T(8,128)(2,1)}), bf16[64,40,128]{2,1,0:T(8,128)(2,1)S(1)}, u32[]{:S(2)}, u32[]{:S(2)}) %all-to-all-start.3) | async-done | bytes 655392 | tf_op jit(solution)/shard_map/all_to_all | solution.py:376
  139.8 0.0 copy-done.10
  139.8 0.0 copy-done.11
  139.8 0.0 copy-done.12
  139.8 1.2 token_grads.1
  (3 shorter events, 0.1 us)
Async XLA Ops:
  20.3 10.5 %copy-start.7 = (bf16[224,1024]{1,0:T(8,128)(2,1)S(1)}, bf16[224,1024]{1,0:T(8,128)(2,1)}, u32[]{:S(2)}) copy-start(bf16[224,1024]{1,0:T(8,128)(2,1)} %gate_ref.1) | copy-start | bytes 1376260
  20.3 43.8 %all-to-all-start.1 = ((bf16[8,1168,128]{2,1,0:T(8,128)(2,1)}), bf16[8,1168,128]{2,1,0:T(8,128)(2,1)S(1)}, u32[]{:S(2)}, u32[]{:S(2)}) async-start(bf16[8,1168,128]{2,1,0:T(8,128)(2,1)} %broadcast_in_dim.2), calls=%async_computation.1 | async-start | bytes 4784128 | tf_op jit(solution)/shard_map/all_to_all | solution.py:300
  30.8 1.0 copy-start.8
  31.8 1.0 copy-start.9
  33.0 1.2 copy-start
  34.2 1.0 copy-start.13
  64.1 1.4 copy-start.1
  68.5 18.2 %all-to-all-start.2 = ((bf16[16,40,768]{2,1,0:T(8,128)(2,1)}), bf16[16,40,768]{2,1,0:T(8,128)(2,1)S(1)}, u32[]{:S(2)}, u32[]{:S(2)}) async-start(bf16[16,40,768]{2,1,0:T(8,128)(2,1)} %forward_parts.1.after_ref), calls=%async_computation.2 | async-start | bytes 1966080 | tf_op jit(solution)/shard_map/all_to_all | solution.py:344
  74.2 32.1 %collective-permute-start = (bf16[2,224,1024]{2,1,0:T(8,128)(2,1)}, bf16[2,224,1024]{2,1,0:T(8,128)(2,1)}, u32[]{:S(2)}, u32[]{:S(2)}) collective-permute-start(bf16[2,224,1024]{2,1,0:T(8,128)(2,1)} %copy-done.13), channel_id=1, source_target_pairs={{0,1},{1,0},{2,3},{3,2},{4,5},{5,4},{6,7},{7,6},{8,9},{9,8},{10,11... | collective-permute-start | bytes 2752520 | tf_op jit(solution)/shard_map/ppermute | solution.py:338
  77.8 1.1 copy-start.3
  78.9 0.8 copy-start.5
  79.7 26.6 %copy-start.2 = (bf16[3,256,1024]{2,1,0:T(8,128)(2,1)S(1)}, bf16[3,256,1024]{2,1,0:T(8,128)(2,1)}, u32[]{:S(2)}) copy-start(bf16[3,256,1024]{2,1,0:T(8,128)(2,1)} %copy-done) | copy-start | bytes 4718596
  106.3 1.1 copy-start.6
  111.7 8.2 %copy-start.4 = (bf16[2,320,1024]{2,1,0:T(8,128)(2,1)S(1)}, bf16[2,320,1024]{2,1,0:T(8,128)(2,1)}, u32[]{:S(2)}) copy-start(bf16[2,320,1024]{2,1,0:T(8,128)(2,1)} %copy-done.3) | copy-start | bytes 3932164
  111.7 28.1 %all-to-all-start.3 = ((bf16[64,40,128]{2,1,0:T(8,128)(2,1)}), bf16[64,40,128]{2,1,0:T(8,128)(2,1)S(1)}, u32[]{:S(2)}, u32[]{:S(2)}) async-start(bf16[64,40,128]{2,1,0:T(8,128)(2,1)} %bitcast.4), calls=%async_computation.3 | async-start | bytes 1310720 | tf_op jit(solution)/shard_map/all_to_all | solution.py:376
  117.4 18.3 %collective-permute-start.1 = (bf16[320,256]{1,0:T(8,128)(2,1)S(1)}, bf16[320,256]{1,0:T(8,128)(2,1)S(1)}, u32[]{:S(2)}, u32[]{:S(2)}) collective-permute-start(bf16[320,256]{1,0:T(8,128)(2,1)S(1)} %slice.4), channel_id=1, source_target_pairs={{0,1},{1,0},{2,3},{3,2},{4,5},{5,4},{6,7},{7,6},{8,9},{9,8},{10,11... | collective-permute-start | bytes 491528 | tf_op jit(solution)/shard_map/ppermute | solution.py:378
  119.9 19.9 %copy-start.10 = (bf16[72,128]{1,0:T(8,128)(2,1)S(1)}, bf16[72,128]{1,0:T(8,128)(2,1)}, u32[]{:S(2)}) copy-start(bf16[72,128]{1,0:T(8,128)(2,1)} %grads_ref.1) | copy-start | bytes 55300
  119.9 19.9 %copy-start.11 = (bf16[72,128]{1,0:T(8,128)(2,1)S(1)}, bf16[72,128]{1,0:T(8,128)(2,1)}, u32[]{:S(2)}) copy-start(bf16[72,128]{1,0:T(8,128)(2,1)} %tokens_ref.1) | copy-start | bytes 55300
  119.9 19.8 %copy-start.12 = (bf16[128]{0:T(256)(128)(2,1)S(1)}, bf16[128]{0:T(256)(128)(2,1)}, u32[]{:S(2)}) copy-start(bf16[128]{0:T(256)(128)(2,1)} %param.8) | copy-start | bytes 772

commit v5 on v4

--- a/solution.py
+++ b/solution.py
@@ -23,6 +23,10 @@
 LARGE = pltpu.CompilerParams(vmem_limit_bytes=24 * 1024 * 1024)
 
 
+def axis_parity(axis):
+    return lax.rem(lax.axis_index(axis), 2)
+
+
 def split_wide(value):
     high = value.astype(BF16).astype(F32)
     return high, value - high
@@ -40,13 +44,11 @@
     return groups
 
 
-def weight_kernel(after_ref, gate_ref, up_ref, down_ref, out_ref, sent_ref):
-    for place, weight in enumerate((gate_ref, up_ref, down_ref)):
-        count, width = weight.shape
-        out_ref[place, :count, :] = weight[...]
-        out_ref[place, count:, :] = jnp.zeros((SLOT - count, width), BF16)
-        if place < 2:
-            sent_ref[place] = weight[...]
+def padded_weight(ref, scratch):
+    count = ref.shape[0]
+    scratch[:count, :] = ref[...]
+    scratch[count:, :] = jnp.zeros((scratch.shape[0] - count, ref.shape[1]), BF16)
+    return scratch[...]
 
 
 def valid_rows(shape, side):
@@ -70,9 +72,21 @@
 
 
 def forward_kernel(
-    nt, nc, rows, count, flag_ref, blocks_ref, first_ref, w_ref, part_ref, grads_ref, scaled_ref
+    nt,
+    nc,
+    rows,
+    count,
+    blocks_ref,
+    first_ref,
+    gate_ref,
+    up_ref,
+    down_ref,
+    part_ref,
+    grads_ref,
+    scaled_ref,
+    w_ref,
 ):
-    odd = flag_ref[0] == 1
+    odd = axis_parity("row") == 1
     feats = blocks_ref.shape[2]
     gains = []
     for col in range(nc):
@@ -93,8 +107,9 @@
             squares = squares + wide * wide
         totals.append(jnp.sum(squares, axis=1, keepdims=True))
     high, low = split_wide(jnp.concatenate(totals, axis=0))
-    for place, source in enumerate((scaled_ref, scaled_ref, grads_ref)):
-        value = lax.dot_general(source[...], w_ref[place], NT_DIMS, preferred_element_type=F32)
+    for place, (source, weight) in enumerate(((scaled_ref, gate_ref), (scaled_ref, up_ref), (grads_ref, down_ref))):
+        padded = padded_weight(weight, w_ref.at[place])
+        value = lax.dot_general(source[...], padded, NT_DIMS, preferred_element_type=F32)
         if place == 0:
             lane = lax.broadcasted_iota(jnp.int32, value.shape, 1)
             value = jnp.where(lane == count, high, jnp.where(lane == count + 1, low, value))
@@ -105,9 +120,9 @@
                 part_ref[2 * tok + half, :, cols] = value[start : start + WINDOW].astype(BF16)
 
 
-def windows_kernel(nt, nc, rows, flag_ref, blocks_ref, after_ref, tokens_ref, grads_ref):
-    odd = flag_ref[0] == 1
-    side = flag_ref[1] == 1
+def windows_kernel(nt, nc, rows, blocks_ref, after_ref, tokens_ref, mine_ref, other_ref):
+    odd = axis_parity("row") == 1
+    side = axis_parity("col") == 1
     feats = blocks_ref.shape[2]
     for pair in range(nt // 2):
         at = pl.ds(pair * 2 * WINDOW, 2 * WINDOW)
@@ -120,12 +135,12 @@
                 late = start + SHIFT
                 high.append(jnp.concatenate([half[late : late + WINDOW] for half in two], axis=0))
             tokens_ref[at, cols] = jnp.where(side, high[0], low[0]).astype(BF16)
-            grads_ref[0, at, cols] = jnp.where(side, high[1], low[1]).astype(BF16)
-            grads_ref[1, at, cols] = jnp.where(side, low[1], high[1]).astype(BF16)
-
-
-def swiglu_kernel(model, count, flag_ref, parts_ref, packed_ref):
-    side = flag_ref[1]
+            mine_ref[at, cols] = jnp.where(side, high[1], low[1]).astype(BF16)
+            other_ref[at, cols] = jnp.where(side, low[1], high[1]).astype(BF16)
+
+
+def swiglu_kernel(model, count, parts_ref, packed_ref):
+    side = axis_parity("col")
     members = parts_ref.shape[0] // 2
 
     def summed(parity):
@@ -169,57 +184,56 @@
     shares,
     feats,
     count,
-    flag_ref,
     packed_ref,
-    own_ref,
-    other_ref,
+    gate_ref,
+    up_ref,
+    gate_other_ref,
+    up_other_ref,
     tokens_ref,
     out_ref,
-    inv_ref,
-    extra_ref,
 ):
     base = count % 128
-    side = flag_ref[1]
+    side = axis_parity("col")
     spot = lax.broadcasted_iota(jnp.int32, (EXTRA, feats), 0) % 4
-
-    @pl.when(pl.program_id(0) == 0)
-    def _():
-        tail = packed_ref[:, SLOT - 128 : SLOT].astype(F32)
-        lane = lax.broadcasted_iota(jnp.int32, tail.shape, 1)
-        at_inv = (lane >= base + 2) & (lane < base + 4)
-        inv_ref[...] = jnp.sum(jnp.where(at_inv, tail, 0.0), axis=1, keepdims=True)
-        for tok in range(nt):
-            piece = tail[tok * WINDOW : (tok + 1) * WINDOW]
-            square = jnp.concatenate([piece, jnp.zeros((128 - WINDOW, 128), F32)], axis=0)
-            turned = square.T[base : base + EXTRA]
-            share = jnp.where(flag_ref[2] == 1, turned[3:4], turned[2:3]) * (1.0 / shares)
-            extra_ref[tok] = jnp.where(spot == 3, share, turned)
-
-    fill = jnp.zeros((SLOT - count, own_ref.shape[2]), BF16)
-    weights = [own_ref[0], own_ref[1]]
-    weights += [jnp.concatenate([other_ref[place], fill], axis=0) for place in range(2)]
-    term = jnp.zeros((packed_ref.shape[0], own_ref.shape[2]), F32)
-    for place, weight in enumerate(weights):
-        values = packed_ref[:, place * SLOT : (place + 1) * SLOT]
-        term = term + jnp.dot(values, weight, preferred_element_type=F32)
-    gain_term = jnp.sum(term * (tokens_ref[...].astype(F32) * inv_ref[...]), axis=0, keepdims=True)
+    tail = packed_ref[:, SLOT - 128 : SLOT].astype(F32)
+    lane = lax.broadcasted_iota(jnp.int32, tail.shape, 1)
+    at_inv = (lane >= base + 2) & (lane < base + 4)
+    inv = jnp.sum(jnp.where(at_inv, tail, 0.0), axis=1, keepdims=True)
+    extras = []
+    for tok in range(nt):
+        piece = tail[tok * WINDOW : (tok + 1) * WINDOW]
+        square = jnp.concatenate([piece, jnp.zeros((128 - WINDOW, 128), F32)], axis=0)
+        turned = square.T[base : base + EXTRA]
+        share = jnp.where(axis_parity("tok") == 1, turned[3:4], turned[2:3]) * (1.0 / shares)
+        extras.append(jnp.where(spot == 3, share, turned))
     keep = valid_rows((WINDOW, feats), side)
-    for part in range(own_ref.shape[2] // feats):
-        cols = slice(part * feats, (part + 1) * feats)
-        for tok in range(nt):
-            extra = jnp.where(spot == 2, gain_term[:, cols], extra_ref[tok])
-            extra = jnp.concatenate([extra] * (WINDOW // EXTRA), axis=0)
-            block = jnp.where(keep, term[tok * WINDOW : (tok + 1) * WINDOW, cols], extra)
-            out_ref[tok, part] = block.astype(BF16)
+    step = 2 * feats
+    fill = jnp.zeros((SLOT - count, step), BF16)
+    for chunk in range(tokens_ref.shape[1] // step):
+        at = pl.ds(chunk * step, step)
+        term = jnp.zeros((packed_ref.shape[0], step), F32)
+        for place, ref in enumerate((gate_ref, up_ref, gate_other_ref, up_other_ref)):
+            values = packed_ref[:, place * SLOT : (place + 1) * SLOT]
+            weight = jnp.concatenate([ref[:, at], fill], axis=0)
+            term = term + jnp.dot(values, weight, preferred_element_type=F32)
+        gain_term = jnp.sum(term * (tokens_ref[:, at].astype(F32) * inv), axis=0, keepdims=True)
+        for part in range(2):
+            cols = slice(part * feats, (part + 1) * feats)
+            for tok in range(nt):
+                extra = jnp.where(spot == 2, gain_term[:, cols], extras[tok])
+                extra = jnp.concatenate([extra] * (WINDOW // EXTRA), axis=0)
+                block = jnp.where(keep, term[tok * WINDOW : (tok + 1) * WINDOW, cols], extra)
+                out_ref[tok, 2 * chunk + part] = block.astype(BF16)
 
 
 def down_mine_kernel(hidden_ref, grads_ref, out_ref):
-    out_ref[...] = lax.dot_general(hidden_ref[...], grads_ref[0], TN_DIMS, preferred_element_type=F32)
+    total = lax.dot_general(hidden_ref[...], grads_ref[...], TN_DIMS, preferred_element_type=F32)
+    out_ref[...] = total[: out_ref.shape[0]]
 
 
 def down_other_kernel(hidden_ref, grads_ref, mine_ref, out_ref):
-    total = lax.dot_general(hidden_ref[...], grads_ref[0], TN_DIMS, preferred_element_type=F32)
-    out_ref[...] = (total + mine_ref[...])[: out_ref.shape[0]].astype(BF16)
+    total = lax.dot_general(hidden_ref[...], grads_ref[...], TN_DIMS, preferred_element_type=F32)
+    out_ref[...] = (total[: out_ref.shape[0]] + mine_ref[...]).astype(BF16)
 
 
 def copy_kernel(copies, own_ref, out_ref):
@@ -230,11 +244,12 @@
         out_ref[copy] = block
 
 
-def message_kernel(rows, first_ref, out_ref):
+def message_kernel(copies, rows, first_ref, out_ref):
     count = first_ref.shape[0]
-    for at in range(count):
-        out_ref[pl.ds(at * rows, rows), :] = first_ref[at, :rows, :]
-    out_ref[count * rows :, :] = first_ref[0, rows:, :]
+    for copy in range(copies):
+        for at in range(count):
+            out_ref[copy, pl.ds(at * rows, rows), :] = first_ref[at, :rows, :]
+        out_ref[copy, count * rows :, :] = first_ref[0, rows:, :]
 
 
 def final_kernel(model, blocks_ref, tokens_ref, grads_ref, gain_ref, tokens_out_ref, gain_out_ref):
@@ -247,7 +262,7 @@
         )
 
     start = (blocks_ref[0].astype(F32), blocks_ref[1].astype(F32))
-    low, high = lax.fori_loop(1, blocks_ref.shape[0] // 2, add, start)
+    low, high = lax.fori_loop(1, blocks_ref.shape[0] // 2, add, start, unroll=True)
     rest = jnp.zeros((feats - EXTRA, feats), F32)
     low_turned = jnp.concatenate([low[SHIFT:], rest], axis=0).T[:WINDOW]
     high_turned = jnp.concatenate([high[:EXTRA], rest], axis=0).T[:WINDOW]
@@ -271,7 +286,6 @@
     count = gate_weight.shape[0]
     width = nc * feats
     model = nr * width
-    flags = jnp.stack([lax.rem(lax.axis_index(a), 2) for a in ("row", "col", "tok")]).astype(jnp.int32)
 
     neighbours = [(at, at ^ 1) for at in range(nc)]
     gain_row = gain.reshape(1, feats)
@@ -287,55 +301,31 @@
     first = mixed_groups(nt, nr, nc, False)
     stage = lax.all_to_all(copies, AXES, 0, 0, tiled=True, axis_index_groups=first)
     long = nc * 2 * rows + EXTRA_SENT
-    message = pl.pallas_call(
-        functools.partial(message_kernel, 2 * rows),
-        out_shape=jax.ShapeDtypeStruct((long, feats), BF16),
+    copies = pl.pallas_call(
+        functools.partial(message_kernel, nt, 2 * rows),
+        out_shape=jax.ShapeDtypeStruct((nt, long, feats), BF16),
         in_specs=[whole()],
         out_specs=whole(),
         compiler_params=SMALL,
-        name="second_message",
+        name="second_messages",
     )(stage)
-    copies = jnp.broadcast_to(message[None], (nt, long, feats))
     second = mixed_groups(nt, nr, nc, True)
     both = lax.all_to_all(copies, AXES, 0, 0, tiled=True, axis_index_groups=second)
 
     flops = 2 * nt * rows * width * SLOT
-    weights, sent = pl.pallas_call(
-        weight_kernel,
-        out_shape=(
-            jax.ShapeDtypeStruct((3, SLOT, width), BF16),
-            jax.ShapeDtypeStruct((2, count, width), BF16),
-        ),
-        in_specs=[whole(pl.ANY)] + [whole()] * 3,
-        out_specs=(whole(), whole()),
-        compiler_params=SMALL,
-        cost_estimate=pl.CostEstimate(flops=0, bytes_accessed=12 * SLOT * width, transcendentals=0),
-        name="padded_weights",
-    )(stage, gate_weight, up_weight, down_weight)
+    gate_sent, up_sent, both = lax.optimization_barrier((gate_weight, up_weight, both))
     parts = pl.pallas_call(
         functools.partial(forward_kernel, nt, nc, rows, count),
         out_shape=jax.ShapeDtypeStruct((2 * nt, WINDOW, 3 * SLOT), BF16),
-        in_specs=[whole(pltpu.SMEM)] + [whole()] * 3,
+        in_specs=[whole()] * 5,
         out_specs=whole(),
-        scratch_shapes=[pltpu.VMEM((nt * rows, width), BF16)] * 2,
+        scratch_shapes=[pltpu.VMEM((nt * rows, width), BF16)] * 2 + [pltpu.VMEM((3, SLOT, width), BF16)],
         compiler_params=LARGE,
         cost_estimate=pl.CostEstimate(flops=3 * flops, bytes_accessed=8 * nt * rows * width, transcendentals=0),
         name="forward_parts",
-    )(flags, both, stage, weights)
-    tokens_all, grad_all = pl.pallas_call(
-        functools.partial(windows_kernel, nt, nc, rows),
-        out_shape=(
-            jax.ShapeDtypeStruct((nt * WINDOW, width), BF16),
-            jax.ShapeDtypeStruct((2, nt * WINDOW, width), BF16),
-        ),
-        in_specs=[whole(pltpu.SMEM), whole(), whole(pl.ANY)],
-        out_specs=(whole(), whole()),
-        compiler_params=LARGE,
-        cost_estimate=pl.CostEstimate(flops=0, bytes_accessed=8 * nt * rows * width, transcendentals=0),
-        name="token_windows",
-    )(flags, both, parts)
-    sent, parts = lax.optimization_barrier((sent, parts))
-    sent = lax.ppermute(sent, "col", neighbours)
+    )(both, stage, gate_weight, up_weight, down_weight)
+    gate_other = lax.ppermute(gate_sent, "col", neighbours)
+    up_other = lax.ppermute(up_sent, "col", neighbours)
     pairs = [
         [(tok * nr + row) * nc + 2 * pair + side for row in range(nr) for side in range(2)]
         for tok in range(nt)
@@ -345,66 +335,68 @@
     packed = pl.pallas_call(
         functools.partial(swiglu_kernel, model, count),
         out_shape=jax.ShapeDtypeStruct((WINDOW, 6 * SLOT), BF16),
-        in_specs=[whole(pltpu.SMEM), whole()],
+        in_specs=[whole()],
         out_specs=whole(),
         compiler_params=SMALL,
         cost_estimate=pl.CostEstimate(
             flops=40 * WINDOW * SLOT, bytes_accessed=16 * WINDOW * SLOT * nr, transcendentals=2 * WINDOW * SLOT
         ),
         name="swiglu_grads",
-    )(flags, parts)
+    )(parts)
     packed = lax.all_gather(packed, "row", axis=0, tiled=True)
 
-    chunk = 2 * feats
+    window_cost = pl.CostEstimate(flops=0, bytes_accessed=8 * nt * rows * width, transcendentals=0)
+    tokens_all, grads_mine, grads_other = pl.pallas_call(
+        functools.partial(windows_kernel, nt, nc, rows),
+        out_shape=(jax.ShapeDtypeStruct((nt * WINDOW, width), BF16),) * 3,
+        in_specs=[whole(), whole(pl.ANY)],
+        out_specs=(whole(),) * 3,
+        compiler_params=SMALL,
+        cost_estimate=window_cost,
+        name="token_windows",
+    )(both, packed)
     blocks = pl.pallas_call(
         functools.partial(input_kernel, nt, nt * nc // 4, feats, count),
         out_shape=jax.ShapeDtypeStruct((nt, nc, WINDOW, feats), BF16),
-        grid=(width // chunk,),
-        in_specs=[
-            whole(pltpu.SMEM),
-            whole(),
-            pl.BlockSpec((2, SLOT, chunk), lambda j: (0, 0, j)),
-            pl.BlockSpec((2, count, chunk), lambda j: (0, 0, j)),
-            pl.BlockSpec((nt * WINDOW, chunk), lambda j: (0, j)),
-        ],
-        out_specs=pl.BlockSpec((nt, 2, WINDOW, feats), lambda j: (0, j, 0, 0)),
-        scratch_shapes=[pltpu.VMEM((nt * WINDOW, 1), F32), pltpu.VMEM((nt, EXTRA, 128), F32)],
+        in_specs=[whole()] * 6,
+        out_specs=whole(),
         compiler_params=LARGE,
         cost_estimate=pl.CostEstimate(flops=2 * flops, bytes_accessed=6 * nt * rows * width, transcendentals=0),
         name="input_grad_blocks",
-    )(flags, packed, weights, sent, tokens_all)
-    blocks = lax.all_to_all(blocks.reshape(nt * nc, WINDOW, feats), ("tok", "col"), 0, 0, tiled=True)
+    )(packed, gate_weight, up_weight, gate_other, up_other, tokens_all)
+    blocks_sent = blocks.reshape(nt * nc, WINDOW, feats)
+    blocks = lax.all_to_all(blocks_sent, ("tok", "col"), 0, 0, tiled=True)
 
     hidden_other = lax.ppermute(packed[:, 5 * SLOT :], "col", neighbours)
     half_chunk = width // 2
     down_cost = pl.CostEstimate(flops=flops // 2, bytes_accessed=3 * nt * rows * width, transcendentals=0)
     mine = pl.pallas_call(
         down_mine_kernel,
-        out_shape=jax.ShapeDtypeStruct((SLOT, width), F32),
+        out_shape=jax.ShapeDtypeStruct((count, width), F32),
         grid=(2,),
         in_specs=[
             pl.BlockSpec((nt * WINDOW, SLOT), lambda j: (0, 4)),
-            pl.BlockSpec((1, nt * WINDOW, half_chunk), lambda j: (0, 0, j)),
+            pl.BlockSpec((nt * WINDOW, half_chunk), lambda j: (0, j)),
         ],
-        out_specs=pl.BlockSpec((SLOT, half_chunk), lambda j: (0, j)),
+        out_specs=pl.BlockSpec((count, half_chunk), lambda j: (0, j)),
         compiler_params=LARGE,
         cost_estimate=down_cost,
         name="down_grads_mine",
-    )(packed, grad_all)
+    )(packed, grads_mine)
     d_down = pl.pallas_call(
         down_other_kernel,
         out_shape=jax.ShapeDtypeStruct((count, width), BF16),
         grid=(2,),
         in_specs=[
             pl.BlockSpec((nt * WINDOW, SLOT), lambda j: (0, 0)),
-            pl.BlockSpec((1, nt * WINDOW, half_chunk), lambda j: (1, 0, j)),
-            pl.BlockSpec((SLOT, half_chunk), lambda j: (0, j)),
+            pl.BlockSpec((nt * WINDOW, half_chunk), lambda j: (0, j)),
+            pl.BlockSpec((count, half_chunk), lambda j: (0, j)),
         ],
         out_specs=pl.BlockSpec((count, half_chunk), lambda j: (0, j)),
         compiler_params=LARGE,
         cost_estimate=down_cost,
         name="down_grads",
-    )(hidden_other, grad_all, mine)
+    )(hidden_other, grads_other, mine)
 
     d_tokens, d_gain = pl.pallas_call(
         functools.partial(final_kernel, model),

time: 142 us -> 135 us (0.951)
  blocking collectives: 30.3 us -> 74 us
  waiting for transfers between devices: 59 us -> 27.7 us
  local copies, waits for them, and re-layouts: 10.3 us -> 1.76 us
  starting transfers between devices: 26.8 us -> 19.9 us
  Pallas kernels: 12.9 us -> 9.79 us
    all_to_all x0 -> x1, blocking collectives: none -> 43.5 us  [on_device(): lax.all_to_all(copies, AXES, 0, 0, tiled=True, axis_index_groups=second)]
    all_to_all x2 -> x1, waiting for transfers between devices: 31.6 us -> 2.57 us  [on_device(): blocks = lax.all_to_all(blocks_sent, ('tok', 'col'), 0, 0, tiled=True)]
    all_to_all x2 -> x1, starting transfers between devices: 16.1 us -> 5.66 us  [on_device(): blocks = lax.all_to_all(blocks_sent, ('tok', 'col'), 0, 0, tiled=True)]
    unnamed x28 -> x24, local copies, waits for them, and re-layouts: 8.57 us -> 1.75 us
    ppermute x1 -> x2, starting transfers between devices: 2.46 us -> 5.84 us  [the longest x1 3.37 us: on_device(): up_other = lax.ppermute(up_sent, 'col', neighbours)]
    ppermute x1 -> x2, waiting for transfers between devices: 5.57 us -> 3.68 us  [the longest x1 3.68 us: on_device(): up_other = lax.ppermute(up_sent, 'col', neighbours)]
    broadcast_in_dim x1 -> x0, local copies, waits for them, and re-layouts: 1.76 us -> none  [on_device(): copies = jnp.broadcast_to(message[None], (nt, long, feats))]
  transfers between devices with their start and end apart: 5 -> 5, of which waited for: 5 -> 4; matrix products, arithmetic and copies ran while one was open for 0% -> 0% of each run, Pallas kernels for 3% -> 2%
where the time goes in v5:
time: 135 us
  blocking collectives  74 us (55%)
  waiting for transfers between devices  27.7 us (21%)
  starting transfers between devices  19.9 us (15%)
  Pallas kernels  9.79 us (7%)
  local copies, waits for them, and re-layouts  1.76 us (1%)
    all_to_all x1, blocking collectives, on_device(): lax.all_to_all(copies, AXES, 0, 0, tiled=True, axis_index_groups=second)  43.5 us
    all_to_all x1, blocking collectives, on_device(): lax.all_to_all(copies, AXES, 0, 0, tiled=True, axis_index_groups=first)  17.1 us
    ppermute x1, waiting for transfers between devices, on_device(): hidden_other = lax.ppermute(packed[:, 5 * SLOT:], 'col', neighbours)  14.8 us
    all_gather x1, blocking collectives, on_device(): packed = lax.all_gather(packed, 'row', axis=0, tiled=True)  13.4 us
    all_to_all x1, waiting for transfers between devices, on_device(): lax.all_to_all(parts, AXES, 0, 0, tiled=True, axis_index_groups=pairs)  6.6 us
    all_to_all x1, starting transfers between devices, on_device(): lax.all_to_all(parts, AXES, 0, 0, tiled=True, axis_index_groups=pairs)  5.75 us
    all_to_all x1, starting transfers between devices, on_device(): blocks = lax.all_to_all(blocks_sent, ('tok', 'col'), 0, 0, tiled=True)  5.66 us
    ppermute x1, waiting for transfers between devices, on_device(): up_other = lax.ppermute(up_sent, 'col', neighbours)  3.68 us
  transfers between devices with their start and end apart: 5, of which 4 were waited for; matrix products, arithmetic and copies ran while one was open for 0% of the time, Pallas kernels for 2%

profile of v5, /device:TPU:10, one launch (start us, length us, event | category | flops | bytes accessed | tf_op | source)
XLA Modules:
  0.0 134.7 jit_solution(1237843899669514929)
XLA Ops:
  0.6 0.8 pad_maximum_fusion.own_ref
  1.4 17.1 %all_to_all.20.first_ref = bf16[8,160,128]{2,1,0:T(8,128)(2,1)S(1)} all-to-all(bf16[8,160,128]{2,1,0:T(8,128)(2,1)S(1)} %own_copies.1), channel_id=1, replica_groups={{0,1,2,3,4,5,6,7},{64,65,66,67,68,69,70,71},{128,129,130,131,132,133,13..., dimensions={0} | all-to-all | bytes 655360 | tf_op jit(solution)/shard_map/all_to_all | solution.py:302
  18.5 0.3 second_messages.1
  18.8 0.0 copy-start
  18.8 0.0 copy-start.2
  18.8 0.0 copy-start.8
  18.9 43.5 %all_to_all.21.blocks_ref = bf16[8,1168,128]{2,1,0:T(8,128)(2,1)S(1)} all-to-all(bf16[8,1168,128]{2,1,0:T(8,128)(2,1)S(1)} %second_messages.1), channel_id=1, replica_groups={{0,64,128,192,256,320,384,448},{1,65,129,193,257,321,385,449},{2,66,130..., dimensions={0} | all-to-all | bytes 4784128 | tf_op jit(solution)/shard_map/all_to_all | solution.py:313
  62.4 0.0 copy-done
  62.4 0.0 copy-done.2
  62.4 0.0 copy-done.8
  62.4 2.4 %forward_parts.1 = bf16[16,40,768]{2,1,0:T(8,128)(2,1)} custom-call(bf16[8,1168,128]{2,1,0:T(8,128)(2,1)S(1)} %all_to_all.21.blocks_ref, bf16[8,160,128]{2,1,0:T(8,128)(2,1)S(1)} %all_to_all.20.first_ref, bf16[224,1024]{1,0:T(8,128)(2,1)S(1)} %copy-done, bf16[224,1024]{1,0:T(8,128)(2,1)S(1)} %copy-done.2, bf16[224,1024]{1,0:T(8,128)(2,1)S(1)} %copy-done.8), custom_call_target="tpu_custom_call" | custom-call | flops 905969664 | bytes 4718592 | tf_op jit(solution)/shard_map/forward_parts/pallas_call | solution.py:317
  64.8 5.8 %all-to-all-start.2 = ((bf16[16,40,768]{2,1,0:T(8,128)(2,1)}), bf16[16,40,768]{2,1,0:T(8,128)(2,1)S(1)}, u32[]{:S(2)}, u32[]{:S(2)}) async-start(bf16[16,40,768]{2,1,0:T(8,128)(2,1)} %forward_parts.1), calls=%async_computation.2 | async-start | bytes 1966080 | tf_op jit(solution)/shard_map/all_to_all | solution.py:334
  70.5 2.5 %collective-permute-start = (bf16[224,1024]{1,0:T(8,128)(2,1)}, bf16[224,1024]{1,0:T(8,128)(2,1)}, u32[]{:S(2)}, u32[]{:S(2)}) collective-permute-start(bf16[224,1024]{1,0:T(8,128)(2,1)} %gate_ref.3), channel_id=1, source_target_pairs={{0,1},{1,0},{2,3},{3,2},{4,5},{5,4},{6,7},{7,6},{8,9},{9,8},{10,11... | collective-permute-start | bytes 1376264 | tf_op jit(solution)/shard_map/ppermute | solution.py:327
  73.0 3.4 %collective-permute-start.1 = (bf16[224,1024]{1,0:T(8,128)(2,1)}, bf16[224,1024]{1,0:T(8,128)(2,1)}, u32[]{:S(2)}, u32[]{:S(2)}) collective-permute-start(bf16[224,1024]{1,0:T(8,128)(2,1)} %up_ref.3), channel_id=1, source_target_pairs={{0,1},{1,0},{2,3},{3,2},{4,5},{5,4},{6,7},{7,6},{8,9},{9,8},{10,11... | collective-permute-start | bytes 1376264 | tf_op jit(solution)/shard_map/ppermute | solution.py:328
  76.4 6.6 %all-to-all-done.2.parts_ref = bf16[16,40,768]{2,1,0:T(8,128)(2,1)S(1)} async-done(((bf16[16,40,768]{2,1,0:T(8,128)(2,1)}), bf16[16,40,768]{2,1,0:T(8,128)(2,1)S(1)}, u32[]{:S(2)}, u32[]{:S(2)}) %all-to-all-start.2) | async-done | bytes 983072 | tf_op jit(solution)/shard_map/all_to_all | solution.py:334
  83.0 0.3 swiglu_grads.1
  83.3 0.0 copy-start.1
  83.3 0.0 copy-start.3
  83.3 13.4 %all_gather.3.after_ref.packed_ref.hidden_ref = bf16[320,1536]{1,0:T(8,128)(2,1)S(1)} all-gather(bf16[40,1536]{1,0:T(8,128)(2,1)S(1)} %swiglu_grads.1), channel_id=1, replica_groups=mesh['tok'=8,'row'=8,'col'=8] {'row'}, dimensions={0}, use_global_device_ids=true | all-gather | bytes 1105920 | tf_op jit(solution)/shard_map/all_gather | solution.py:346
  96.7 0.6 token_windows.1
  97.3 0.0 copy-start.4
  97.3 0.8 copy-done.4
  98.1 0.0 copy-start.6
  98.1 0.8 copy-done.6
  99.0 0.0 collective-permute-done.gate_other_ref
  99.0 3.7 %collective-permute-done.1.up_other_ref = bf16[224,1024]{1,0:T(8,128)(2,1)} collective-permute-done((bf16[224,1024]{1,0:T(8,128)(2,1)}, bf16[224,1024]{1,0:T(8,128)(2,1)}, u32[]{:S(2)}, u32[]{:S(2)}) %collective-permute-start.1) | collective-permute-done | bytes 458784 | tf_op jit(solution)/shard_map/ppermute | solution.py:328
  102.6 0.0 copy-done.1
  102.6 0.0 copy-done.3
  102.6 0.0 copy-start.5
  102.7 3.0 %input_grad_blocks.1 = bf16[8,8,40,128]{3,2,1,0:T(8,128)(2,1)} custom-call(bf16[320,1536]{1,0:T(8,128)(2,1)S(1)} %all_gather.3.after_ref.packed_ref.hidden_ref, bf16[224,1024]{1,0:T(8,128)(2,1)S(1)} %copy-done.1, bf16[224,1024]{1,0:T(8,128)(2,1)S(1)} %copy-done.3, bf16[224,1024]{1,0:T(8,128)(2,1)} %collective-permute-done.gate_other_ref, ...), custom_call_target="tpu_custom_call" | custom-call | flops 603979776 | bytes 3538944 | tf_op jit(solution)/shard_map/input_grad_blocks/pallas_call | solution.py:358
  105.6 0.0 copy-start.7
  105.6 5.7 %all-to-all-start.3 = ((bf16[64,40,128]{2,1,0:T(8,128)(2,1)}), bf16[64,40,128]{2,1,0:T(8,128)(2,1)S(1)}, u32[]{:S(2)}, u32[]{:S(2)}) async-start(bf16[64,40,128]{2,1,0:T(8,128)(2,1)} %bitcast.1), calls=%async_computation.3 | async-start | bytes 1310720 | tf_op jit(solution)/shard_map/all_to_all | solution.py:368
  111.3 0.0 copy-start.9
  111.3 0.0 copy-start.10
  111.3 0.0 copy-start.11
  111.4 2.6 %collective-permute-start.2 = (bf16[320,256]{1,0:T(8,128)(2,1)S(1)}, bf16[320,256]{1,0:T(8,128)(2,1)S(1)}, u32[]{:S(2)}, u32[]{:S(2)}) collective-permute-start(bf16[320,256]{1,0:T(8,128)(2,1)S(1)} %slice.4), channel_id=1, source_target_pairs={{0,1},{1,0},{2,3},{3,2},{4,5},{5,4},{6,7},{7,6},{8,9},{9,8},{10,11... | collective-permute-start | bytes 491528 | tf_op jit(solution)/shard_map/ppermute | solution.py:370
  114.0 0.0 copy-done.5
  114.0 0.8 down_grads_mine.1.mine_ref
  114.8 14.8 %collective-permute-done.2.hidden_ref = bf16[320,256]{1,0:T(8,128)(2,1)S(1)} collective-permute-done((bf16[320,256]{1,0:T(8,128)(2,1)S(1)}, bf16[320,256]{1,0:T(8,128)(2,1)S(1)}, u32[]{:S(2)}, u32[]{:S(2)}) %collective-permute-start.2) | collective-permute-done | bytes 163872 | tf_op jit(solution)/shard_map/ppermute | solution.py:370
  129.6 0.0 copy-done.7
  129.6 1.5 %down_grads.1 = bf16[224,1024]{1,0:T(8,128)(2,1)} custom-call(bf16[320,256]{1,0:T(8,128)(2,1)S(1)} %collective-permute-done.2.hidden_ref, bf16[320,1024]{1,0:T(8,128)(2,1)S(1)} %copy-done.7, f32[224,1024]{1,0:T(8,128)S(1)} %down_grads_mine.1.mine_ref), custom_call_target="tpu_custom_call" | custom-call | flops 150994944 | bytes 1769472 | tf_op jit(solution)/shard_map/down_grads/pallas_call | solution.py:386
  131.1 2.6 %all-to-all-done.3.blocks_ref = bf16[64,40,128]{2,1,0:T(8,128)(2,1)S(1)} async-done(((bf16[64,40,128]{2,1,0:T(8,128)(2,1)}), bf16[64,40,128]{2,1,0:T(8,128)(2,1)S(1)}, u32[]{:S(2)}, u32[]{:S(2)}) %all-to-all-start.3) | async-done | bytes 655392 | tf_op jit(solution)/shard_map/all_to_all | solution.py:368
  133.7 0.0 copy-done.9
  133.7 0.0 copy-done.10
  133.7 0.0 copy-done.11
  133.7 1.0 token_grads.1
  (2 shorter events, 0.1 us)
Async XLA Ops:
  18.8 43.6 %copy-start = (bf16[224,1024]{1,0:T(8,128)(2,1)S(1)}, bf16[224,1024]{1,0:T(8,128)(2,1)}, u32[]{:S(2)}) copy-start(bf16[224,1024]{1,0:T(8,128)(2,1)} %gate_ref.3) | copy-start | bytes 1376260
  18.8 43.6 %copy-start.2 = (bf16[224,1024]{1,0:T(8,128)(2,1)S(1)}, bf16[224,1024]{1,0:T(8,128)(2,1)}, u32[]{:S(2)}) copy-start(bf16[224,1024]{1,0:T(8,128)(2,1)} %up_ref.3) | copy-start | bytes 1376260
  18.8 43.6 %copy-start.8 = (bf16[224,1024]{1,0:T(8,128)(2,1)S(1)}, bf16[224,1024]{1,0:T(8,128)(2,1)}, u32[]{:S(2)}) copy-start(bf16[224,1024]{1,0:T(8,128)(2,1)} %down_ref.1) | copy-start | bytes 1376260
  64.8 18.2 %all-to-all-start.2 = ((bf16[16,40,768]{2,1,0:T(8,128)(2,1)}), bf16[16,40,768]{2,1,0:T(8,128)(2,1)S(1)}, u32[]{:S(2)}, u32[]{:S(2)}) async-start(bf16[16,40,768]{2,1,0:T(8,128)(2,1)} %forward_parts.1), calls=%async_computation.2 | async-start | bytes 1966080 | tf_op jit(solution)/shard_map/all_to_all | solution.py:334
  70.5 28.4 %collective-permute-start = (bf16[224,1024]{1,0:T(8,128)(2,1)}, bf16[224,1024]{1,0:T(8,128)(2,1)}, u32[]{:S(2)}, u32[]{:S(2)}) collective-permute-start(bf16[224,1024]{1,0:T(8,128)(2,1)} %gate_ref.3), channel_id=1, source_target_pairs={{0,1},{1,0},{2,3},{3,2},{4,5},{5,4},{6,7},{7,6},{8,9},{9,8},{10,11... | collective-permute-start | bytes 1376264 | tf_op jit(solution)/shard_map/ppermute | solution.py:327
  73.0 29.6 %collective-permute-start.1 = (bf16[224,1024]{1,0:T(8,128)(2,1)}, bf16[224,1024]{1,0:T(8,128)(2,1)}, u32[]{:S(2)}, u32[]{:S(2)}) collective-permute-start(bf16[224,1024]{1,0:T(8,128)(2,1)} %up_ref.3), channel_id=1, source_target_pairs={{0,1},{1,0},{2,3},{3,2},{4,5},{5,4},{6,7},{7,6},{8,9},{9,8},{10,11... | collective-permute-start | bytes 1376264 | tf_op jit(solution)/shard_map/ppermute | solution.py:328
  83.3 19.4 %copy-start.1 = (bf16[224,1024]{1,0:T(8,128)(2,1)S(1)}, bf16[224,1024]{1,0:T(8,128)(2,1)}, u32[]{:S(2)}) copy-start(bf16[224,1024]{1,0:T(8,128)(2,1)} %gate_ref.3) | copy-start | bytes 1376260
  83.3 19.4 %copy-start.3 = (bf16[224,1024]{1,0:T(8,128)(2,1)S(1)}, bf16[224,1024]{1,0:T(8,128)(2,1)}, u32[]{:S(2)}) copy-start(bf16[224,1024]{1,0:T(8,128)(2,1)} %up_ref.3) | copy-start | bytes 1376260
  97.3 0.8 copy-start.4
  98.1 0.9 copy-start.6
  102.6 11.3 %copy-start.5 = (bf16[320,1024]{1,0:T(8,128)(2,1)S(1)}, bf16[320,1024]{1,0:T(8,128)(2,1)}, u32[]{:S(2)}) copy-start(bf16[320,1024]{1,0:T(8,128)(2,1)} %copy-done.4) | copy-start | bytes 1966084
  105.6 24.0 %copy-start.7 = (bf16[320,1024]{1,0:T(8,128)(2,1)S(1)}, bf16[320,1024]{1,0:T(8,128)(2,1)}, u32[]{:S(2)}) copy-start(bf16[320,1024]{1,0:T(8,128)(2,1)} %copy-done.6) | copy-start | bytes 1966084
  105.6 28.0 %all-to-all-start.3 = ((bf16[64,40,128]{2,1,0:T(8,128)(2,1)}), bf16[64,40,128]{2,1,0:T(8,128)(2,1)S(1)}, u32[]{:S(2)}, u32[]{:S(2)}) async-start(bf16[64,40,128]{2,1,0:T(8,128)(2,1)} %bitcast.1), calls=%async_computation.3 | async-start | bytes 1310720 | tf_op jit(solution)/shard_map/all_to_all | solution.py:368
  111.3 22.4 %copy-start.9 = (bf16[72,128]{1,0:T(8,128)(2,1)S(1)}, bf16[72,128]{1,0:T(8,128)(2,1)}, u32[]{:S(2)}) copy-start(bf16[72,128]{1,0:T(8,128)(2,1)} %grads_ref.1) | copy-start | bytes 55300
  111.3 22.3 %copy-start.10 = (bf16[72,128]{1,0:T(8,128)(2,1)S(1)}, bf16[72,128]{1,0:T(8,128)(2,1)}, u32[]{:S(2)}) copy-start(bf16[72,128]{1,0:T(8,128)(2,1)} %tokens_ref.1) | copy-start | bytes 55300
  111.3 22.3 %copy-start.11 = (bf16[128]{0:T(256)(128)(2,1)S(1)}, bf16[128]{0:T(256)(128)(2,1)}, u32[]{:S(2)}) copy-start(bf16[128]{0:T(256)(128)(2,1)} %param.8) | copy-start | bytes 772
  111.4 18.3 %collective-permute-start.2 = (bf16[320,256]{1,0:T(8,128)(2,1)S(1)}, bf16[320,256]{1,0:T(8,128)(2,1)S(1)}, u32[]{:S(2)}, u32[]{:S(2)}) collective-permute-start(bf16[320,256]{1,0:T(8,128)(2,1)S(1)} %slice.4), channel_id=1, source_target_pairs={{0,1},{1,0},{2,3},{3,2},{4,5},{5,4},{6,7},{7,6},{8,9},{9,8},{10,11... | collective-permute-start | bytes 491528 | tf_op jit(solution)/shard_map/ppermute | solution.py:370

commit v6 on v5

--- a/solution.py
+++ b/solution.py
@@ -179,19 +179,39 @@
     packed_ref[:, :SLOT] = own.astype(BF16)
 
 
+def weight_columns(ref, at):
+    fill = jnp.zeros((SLOT - ref.shape[0], at.size), BF16)
+    return jnp.concatenate([ref[:, at], fill], axis=0)
+
+
+def three_terms_kernel(step, packed_ref, gate_ref, up_ref, gate_other_ref, out_ref):
+    for chunk in range(out_ref.shape[1] // step):
+        at = pl.ds(chunk * step, step)
+        term = jnp.zeros((out_ref.shape[0], step), F32)
+        for place, ref in enumerate((gate_ref, up_ref, gate_other_ref)):
+            values = packed_ref[:, place * SLOT : (place + 1) * SLOT]
+            term = term + jnp.dot(values, weight_columns(ref, at), preferred_element_type=F32)
+        out_ref[:, at] = term
+
+
 def input_kernel(
     nt,
     shares,
     feats,
     count,
     packed_ref,
-    gate_ref,
-    up_ref,
-    gate_other_ref,
+    three_ref,
     up_other_ref,
     tokens_ref,
     out_ref,
+    w_ref,
+    block_ref,
+    in_sem,
+    out_sems,
 ):
+    load = pltpu.make_async_copy(up_other_ref, w_ref.at[pl.ds(0, count)], in_sem)
+    load.start()
+    w_ref[count:, :] = jnp.zeros((SLOT - count, w_ref.shape[1]), BF16)
     base = count % 128
     side = axis_parity("col")
     spot = lax.broadcasted_iota(jnp.int32, (EXTRA, feats), 0) % 4
@@ -208,14 +228,12 @@
         extras.append(jnp.where(spot == 3, share, turned))
     keep = valid_rows((WINDOW, feats), side)
     step = 2 * feats
-    fill = jnp.zeros((SLOT - count, step), BF16)
+    stores = []
+    load.wait()
     for chunk in range(tokens_ref.shape[1] // step):
         at = pl.ds(chunk * step, step)
-        term = jnp.zeros((packed_ref.shape[0], step), F32)
-        for place, ref in enumerate((gate_ref, up_ref, gate_other_ref, up_other_ref)):
-            values = packed_ref[:, place * SLOT : (place + 1) * SLOT]
-            weight = jnp.concatenate([ref[:, at], fill], axis=0)
-            term = term + jnp.dot(values, weight, preferred_element_type=F32)
+        values = packed_ref[:, 3 * SLOT : 4 * SLOT]
+        term = jnp.dot(values, w_ref[:, at], preferred_element_type=F32) + three_ref[:, at]
         gain_term = jnp.sum(term * (tokens_ref[:, at].astype(F32) * inv), axis=0, keepdims=True)
         for part in range(2):
             cols = slice(part * feats, (part + 1) * feats)
@@ -223,7 +241,12 @@
                 extra = jnp.where(spot == 2, gain_term[:, cols], extras[tok])
                 extra = jnp.concatenate([extra] * (WINDOW // EXTRA), axis=0)
                 block = jnp.where(keep, term[tok * WINDOW : (tok + 1) * WINDOW, cols], extra)
-                out_ref[tok, 2 * chunk + part] = block.astype(BF16)
+                block_ref[tok, 2 * chunk + part] = block.astype(BF16)
+        two = pl.ds(2 * chunk, 2)
+        stores.append(pltpu.make_async_copy(block_ref.at[:, two], out_ref.at[:, two], out_sems.at[chunk]))
+        stores[-1].start()
+    for store in stores:
+        store.wait()
 
 
 def down_mine_kernel(hidden_ref, grads_ref, out_ref):
@@ -355,15 +378,30 @@
         cost_estimate=window_cost,
         name="token_windows",
     )(both, packed)
+    three = pl.pallas_call(
+        functools.partial(three_terms_kernel, 2 * feats),
+        out_shape=jax.ShapeDtypeStruct((nt * WINDOW, width), F32),
+        in_specs=[whole()] * 4,
+        out_specs=whole(),
+        compiler_params=LARGE,
+        cost_estimate=pl.CostEstimate(flops=flops, bytes_accessed=4 * nt * rows * width, transcendentals=0),
+        name="three_terms",
+    )(packed, gate_weight, up_weight, gate_other)
     blocks = pl.pallas_call(
         functools.partial(input_kernel, nt, nt * nc // 4, feats, count),
         out_shape=jax.ShapeDtypeStruct((nt, nc, WINDOW, feats), BF16),
-        in_specs=[whole()] * 6,
-        out_specs=whole(),
+        in_specs=[whole(), whole(), whole(pl.ANY), whole()],
+        out_specs=whole(pl.ANY),
+        scratch_shapes=[
+            pltpu.VMEM((SLOT, width), BF16),
+            pltpu.VMEM((nt, nc, WINDOW, feats), BF16),
+            pltpu.SemaphoreType.DMA(()),
+            pltpu.SemaphoreType.DMA((nc // 2,)),
+        ],
         compiler_params=LARGE,
-        cost_estimate=pl.CostEstimate(flops=2 * flops, bytes_accessed=6 * nt * rows * width, transcendentals=0),
+        cost_estimate=pl.CostEstimate(flops=flops, bytes_accessed=6 * nt * rows * width, transcendentals=0),
         name="input_grad_blocks",
-    )(packed, gate_weight, up_weight, gate_other, up_other, tokens_all)
+    )(packed, three, up_other, tokens_all)
     blocks_sent = blocks.reshape(nt * nc, WINDOW, feats)
     blocks = lax.all_to_all(blocks_sent, ("tok", "col"), 0, 0, tiled=True)
 

time: 135 us -> 135 us (level)
  the two profiles are of different devices: /device:TPU:10 before, /device:TPU:8 now
where the time goes in v6:
time: 135 us; the launch traced here: 134 us
  blocking collectives  75 us (56%)
  waiting for transfers between devices  25.8 us (19%)
  starting transfers between devices  19.4 us (14%)
  Pallas kernels  10.8 us (8%)
  local copies, waits for them, and re-layouts  1.76 us (1%)
    all_to_all x1, blocking collectives, on_device(): lax.all_to_all(copies, AXES, 0, 0, tiled=True, axis_index_groups=second)  42.7 us
    all_to_all x1, blocking collectives, on_device(): lax.all_to_all(copies, AXES, 0, 0, tiled=True, axis_index_groups=first)  17.9 us
    ppermute x1, waiting for transfers between devices, on_device(): hidden_other = lax.ppermute(packed[:, 5 * SLOT:], 'col', neighbours)  15.2 us
    all_gather x1, blocking collectives, on_device(): packed = lax.all_gather(packed, 'row', axis=0, tiled=True)  14.4 us
    all_to_all x1, waiting for transfers between devices, on_device(): lax.all_to_all(parts, AXES, 0, 0, tiled=True, axis_index_groups=pairs)  8.01 us
    all_to_all x1, starting transfers between devices, on_device(): lax.all_to_all(parts, AXES, 0, 0, tiled=True, axis_index_groups=pairs)  5.78 us
    all_to_all x1, starting transfers between devices, on_device(): blocks = lax.all_to_all(blocks_sent, ('tok', 'col'), 0, 0, tiled=True)  5.18 us
    ppermute x1, starting transfers between devices, on_device(): up_other = lax.ppermute(up_sent, 'col', neighbours)  3.83 us
  transfers between devices with their start and end apart: 5, of which 3 were waited for; matrix products, arithmetic and copies ran while one was open for 0% of the time, Pallas kernels for 4%

profile of v6, /device:TPU:8, one launch (start us, length us, event | category | flops | bytes accessed | tf_op | source)
XLA Modules:
  0.0 134.4 jit_solution(15312201627127358088)
XLA Ops:
  0.6 0.8 pad_maximum_fusion.own_ref
  1.4 17.9 %all_to_all.20.first_ref = bf16[8,160,128]{2,1,0:T(8,128)(2,1)S(1)} all-to-all(bf16[8,160,128]{2,1,0:T(8,128)(2,1)S(1)} %own_copies.1), channel_id=1, replica_groups={{0,1,2,3,4,5,6,7},{64,65,66,67,68,69,70,71},{128,129,130,131,132,133,13..., dimensions={0} | all-to-all | bytes 655360 | tf_op jit(solution)/shard_map/all_to_all | solution.py:325
  19.4 0.3 second_messages.1
  19.7 0.0 copy-start
  19.7 0.0 copy-start.2
  19.7 0.0 copy-start.8
  19.7 42.7 %all_to_all.21.blocks_ref = bf16[8,1168,128]{2,1,0:T(8,128)(2,1)S(1)} all-to-all(bf16[8,1168,128]{2,1,0:T(8,128)(2,1)S(1)} %second_messages.1), channel_id=1, replica_groups={{0,64,128,192,256,320,384,448},{1,65,129,193,257,321,385,449},{2,66,130..., dimensions={0} | all-to-all | bytes 4784128 | tf_op jit(solution)/shard_map/all_to_all | solution.py:336
  62.4 0.0 copy-done
  62.4 0.0 copy-done.2
  62.4 0.0 copy-done.8
  62.4 2.4 %forward_parts.1 = bf16[16,40,768]{2,1,0:T(8,128)(2,1)} custom-call(bf16[8,1168,128]{2,1,0:T(8,128)(2,1)S(1)} %all_to_all.21.blocks_ref, bf16[8,160,128]{2,1,0:T(8,128)(2,1)S(1)} %all_to_all.20.first_ref, bf16[224,1024]{1,0:T(8,128)(2,1)S(1)} %copy-done, bf16[224,1024]{1,0:T(8,128)(2,1)S(1)} %copy-done.2, bf16[224,1024]{1,0:T(8,128)(2,1)S(1)} %copy-done.8), custom_call_target="tpu_custom_call" | custom-call | flops 905969664 | bytes 4718592 | tf_op jit(solution)/shard_map/forward_parts/pallas_call | solution.py:340
  64.8 5.8 %all-to-all-start.2 = ((bf16[16,40,768]{2,1,0:T(8,128)(2,1)}), bf16[16,40,768]{2,1,0:T(8,128)(2,1)S(1)}, u32[]{:S(2)}, u32[]{:S(2)}) async-start(bf16[16,40,768]{2,1,0:T(8,128)(2,1)} %forward_parts.1), calls=%async_computation.2 | async-start | bytes 1966080 | tf_op jit(solution)/shard_map/all_to_all | solution.py:357
  70.6 2.0 %collective-permute-start = (bf16[224,1024]{1,0:T(8,128)(2,1)}, bf16[224,1024]{1,0:T(8,128)(2,1)}, u32[]{:S(2)}, u32[]{:S(2)}) collective-permute-start(bf16[224,1024]{1,0:T(8,128)(2,1)} %gate_ref.3), channel_id=1, source_target_pairs={{0,1},{1,0},{2,3},{3,2},{4,5},{5,4},{6,7},{7,6},{8,9},{9,8},{10,11... | collective-permute-start | bytes 1376264 | tf_op jit(solution)/shard_map/ppermute | solution.py:350
  72.6 3.8 %collective-permute-start.1 = (bf16[224,1024]{1,0:T(8,128)(2,1)}, bf16[224,1024]{1,0:T(8,128)(2,1)}, u32[]{:S(2)}, u32[]{:S(2)}) collective-permute-start(bf16[224,1024]{1,0:T(8,128)(2,1)} %up_ref.3), channel_id=1, source_target_pairs={{0,1},{1,0},{2,3},{3,2},{4,5},{5,4},{6,7},{7,6},{8,9},{9,8},{10,11... | collective-permute-start | bytes 1376264 | tf_op jit(solution)/shard_map/ppermute | solution.py:351
  76.4 8.0 %all-to-all-done.2.parts_ref = bf16[16,40,768]{2,1,0:T(8,128)(2,1)S(1)} async-done(((bf16[16,40,768]{2,1,0:T(8,128)(2,1)}), bf16[16,40,768]{2,1,0:T(8,128)(2,1)S(1)}, u32[]{:S(2)}, u32[]{:S(2)}) %all-to-all-start.2) | async-done | bytes 983072 | tf_op jit(solution)/shard_map/all_to_all | solution.py:357
  84.4 0.3 swiglu_grads.1
  84.7 0.0 copy-start.1
  84.7 0.0 copy-start.3
  84.7 14.4 %all_gather.3.packed_ref.after_ref.hidden_ref = bf16[320,1536]{1,0:T(8,128)(2,1)S(1)} all-gather(bf16[40,1536]{1,0:T(8,128)(2,1)S(1)} %swiglu_grads.1), channel_id=1, replica_groups=mesh['tok'=8,'row'=8,'col'=8] {'row'}, dimensions={0}, use_global_device_ids=true | all-gather | bytes 1105920 | tf_op jit(solution)/shard_map/all_gather | solution.py:369
  99.1 0.6 token_windows.1
  99.7 0.0 copy-start.4
  99.7 0.8 copy-done.4
  100.6 0.0 copy-start.6
  100.6 0.8 copy-done.6
  101.4 0.0 collective-permute-done.gate_other_ref
  101.4 0.0 copy-done.1
  101.4 0.0 copy-done.3
  101.4 1.7 %three_terms.1.three_ref = f32[320,1024]{1,0:T(8,128)S(1)} custom-call(bf16[320,1536]{1,0:T(8,128)(2,1)S(1)} %all_gather.3.packed_ref.after_ref.hidden_ref, bf16[224,1024]{1,0:T(8,128)(2,1)S(1)} %copy-done.1, bf16[224,1024]{1,0:T(8,128)(2,1)S(1)} %copy-done.3, bf16[224,1024]{1,0:T(8,128)(2,1)} %collective-permute-done.gate_other_ref), custom_call_target="tpu_custom_call" | custom-call | flops 301989888 | bytes 2359296 | tf_op jit(solution)/shard_map/three_terms/pallas_call | solution.py:381
  103.1 0.0 collective-permute-done.1.up_other_ref
  103.1 0.0 copy-start.5
  103.1 2.3 %input_grad_blocks.1 = bf16[8,8,40,128]{3,2,1,0:T(8,128)(2,1)} custom-call(bf16[320,1536]{1,0:T(8,128)(2,1)S(1)} %all_gather.3.packed_ref.after_ref.hidden_ref, f32[320,1024]{1,0:T(8,128)S(1)} %three_terms.1.three_ref, bf16[224,1024]{1,0:T(8,128)(2,1)} %collective-permute-done.1.up_other_ref, bf16[320,1024]{1,0:T(8,128)(2,1)S(1)} %get-tuple-element.14.tokens_ref), custom_call_target="tpu_custom_call" | custom-call | flops 301989888 | bytes 3538944 | tf_op jit(solution)/shard_map/input_grad_blocks/pallas_call | solution.py:390
  105.5 0.0 copy-start.7
  105.5 5.2 %all-to-all-start.3 = ((bf16[64,40,128]{2,1,0:T(8,128)(2,1)}), bf16[64,40,128]{2,1,0:T(8,128)(2,1)S(1)}, u32[]{:S(2)}, u32[]{:S(2)}) async-start(bf16[64,40,128]{2,1,0:T(8,128)(2,1)} %bitcast.1), calls=%async_computation.3 | async-start | bytes 1310720 | tf_op jit(solution)/shard_map/all_to_all | solution.py:406
  110.7 0.0 copy-start.9
  110.7 0.0 copy-start.10
  110.7 0.0 copy-start.11
  110.7 2.6 %collective-permute-start.2 = (bf16[320,256]{1,0:T(8,128)(2,1)S(1)}, bf16[320,256]{1,0:T(8,128)(2,1)S(1)}, u32[]{:S(2)}, u32[]{:S(2)}) collective-permute-start(bf16[320,256]{1,0:T(8,128)(2,1)S(1)} %slice.4), channel_id=1, source_target_pairs={{0,1},{1,0},{2,3},{3,2},{4,5},{5,4},{6,7},{7,6},{8,9},{9,8},{10,11... | collective-permute-start | bytes 491528 | tf_op jit(solution)/shard_map/ppermute | solution.py:408
  113.3 0.0 copy-done.5
  113.4 0.8 down_grads_mine.1.mine_ref
  114.2 15.2 %collective-permute-done.2.hidden_ref = bf16[320,256]{1,0:T(8,128)(2,1)S(1)} collective-permute-done((bf16[320,256]{1,0:T(8,128)(2,1)S(1)}, bf16[320,256]{1,0:T(8,128)(2,1)S(1)}, u32[]{:S(2)}, u32[]{:S(2)}) %collective-permute-start.2) | collective-permute-done | bytes 163872 | tf_op jit(solution)/shard_map/ppermute | solution.py:408
  129.4 0.0 copy-done.7
  129.4 1.5 %down_grads.1 = bf16[224,1024]{1,0:T(8,128)(2,1)} custom-call(bf16[320,256]{1,0:T(8,128)(2,1)S(1)} %collective-permute-done.2.hidden_ref, bf16[320,1024]{1,0:T(8,128)(2,1)S(1)} %copy-done.7, f32[224,1024]{1,0:T(8,128)S(1)} %down_grads_mine.1.mine_ref), custom_call_target="tpu_custom_call" | custom-call | flops 150994944 | bytes 1769472 | tf_op jit(solution)/shard_map/down_grads/pallas_call | solution.py:424
  130.8 2.5 %all-to-all-done.3.blocks_ref = bf16[64,40,128]{2,1,0:T(8,128)(2,1)S(1)} async-done(((bf16[64,40,128]{2,1,0:T(8,128)(2,1)}), bf16[64,40,128]{2,1,0:T(8,128)(2,1)S(1)}, u32[]{:S(2)}, u32[]{:S(2)}) %all-to-all-start.3) | async-done | bytes 655392 | tf_op jit(solution)/shard_map/all_to_all | solution.py:406
  133.4 0.0 copy-done.9
  133.4 0.0 copy-done.10
  133.4 0.0 copy-done.11
  133.4 1.0 token_grads.1
  (2 shorter events, 0.1 us)
Async XLA Ops:
  19.7 42.7 %copy-start = (bf16[224,1024]{1,0:T(8,128)(2,1)S(1)}, bf16[224,1024]{1,0:T(8,128)(2,1)}, u32[]{:S(2)}) copy-start(bf16[224,1024]{1,0:T(8,128)(2,1)} %gate_ref.3) | copy-start | bytes 1376260
  19.7 42.7 %copy-start.2 = (bf16[224,1024]{1,0:T(8,128)(2,1)S(1)}, bf16[224,1024]{1,0:T(8,128)(2,1)}, u32[]{:S(2)}) copy-start(bf16[224,1024]{1,0:T(8,128)(2,1)} %up_ref.3) | copy-start | bytes 1376260
  19.7 42.7 %copy-start.8 = (bf16[224,1024]{1,0:T(8,128)(2,1)S(1)}, bf16[224,1024]{1,0:T(8,128)(2,1)}, u32[]{:S(2)}) copy-start(bf16[224,1024]{1,0:T(8,128)(2,1)} %down_ref.1) | copy-start | bytes 1376260
  64.8 19.6 %all-to-all-start.2 = ((bf16[16,40,768]{2,1,0:T(8,128)(2,1)}), bf16[16,40,768]{2,1,0:T(8,128)(2,1)S(1)}, u32[]{:S(2)}, u32[]{:S(2)}) async-start(bf16[16,40,768]{2,1,0:T(8,128)(2,1)} %forward_parts.1), calls=%async_computation.2 | async-start | bytes 1966080 | tf_op jit(solution)/shard_map/all_to_all | solution.py:357
  70.6 30.9 %collective-permute-start = (bf16[224,1024]{1,0:T(8,128)(2,1)}, bf16[224,1024]{1,0:T(8,128)(2,1)}, u32[]{:S(2)}, u32[]{:S(2)}) collective-permute-start(bf16[224,1024]{1,0:T(8,128)(2,1)} %gate_ref.3), channel_id=1, source_target_pairs={{0,1},{1,0},{2,3},{3,2},{4,5},{5,4},{6,7},{7,6},{8,9},{9,8},{10,11... | collective-permute-start | bytes 1376264 | tf_op jit(solution)/shard_map/ppermute | solution.py:350
  72.6 30.5 %collective-permute-start.1 = (bf16[224,1024]{1,0:T(8,128)(2,1)}, bf16[224,1024]{1,0:T(8,128)(2,1)}, u32[]{:S(2)}, u32[]{:S(2)}) collective-permute-start(bf16[224,1024]{1,0:T(8,128)(2,1)} %up_ref.3), channel_id=1, source_target_pairs={{0,1},{1,0},{2,3},{3,2},{4,5},{5,4},{6,7},{7,6},{8,9},{9,8},{10,11... | collective-permute-start | bytes 1376264 | tf_op jit(solution)/shard_map/ppermute | solution.py:351
  84.7 16.7 %copy-start.1 = (bf16[224,1024]{1,0:T(8,128)(2,1)S(1)}, bf16[224,1024]{1,0:T(8,128)(2,1)}, u32[]{:S(2)}) copy-start(bf16[224,1024]{1,0:T(8,128)(2,1)} %gate_ref.3) | copy-start | bytes 1376260
  84.7 16.7 %copy-start.3 = (bf16[224,1024]{1,0:T(8,128)(2,1)S(1)}, bf16[224,1024]{1,0:T(8,128)(2,1)}, u32[]{:S(2)}) copy-start(bf16[224,1024]{1,0:T(8,128)(2,1)} %up_ref.3) | copy-start | bytes 1376260
  99.7 0.9 copy-start.4
  100.6 0.8 copy-start.6
  103.1 10.2 %copy-start.5 = (bf16[320,1024]{1,0:T(8,128)(2,1)S(1)}, bf16[320,1024]{1,0:T(8,128)(2,1)}, u32[]{:S(2)}) copy-start(bf16[320,1024]{1,0:T(8,128)(2,1)} %copy-done.4) | copy-start | bytes 1966084
  105.5 23.9 %copy-start.7 = (bf16[320,1024]{1,0:T(8,128)(2,1)S(1)}, bf16[320,1024]{1,0:T(8,128)(2,1)}, u32[]{:S(2)}) copy-start(bf16[320,1024]{1,0:T(8,128)(2,1)} %copy-done.6) | copy-start | bytes 1966084
  105.5 27.9 %all-to-all-start.3 = ((bf16[64,40,128]{2,1,0:T(8,128)(2,1)}), bf16[64,40,128]{2,1,0:T(8,128)(2,1)S(1)}, u32[]{:S(2)}, u32[]{:S(2)}) async-start(bf16[64,40,128]{2,1,0:T(8,128)(2,1)} %bitcast.1), calls=%async_computation.3 | async-start | bytes 1310720 | tf_op jit(solution)/shard_map/all_to_all | solution.py:406
  110.7 22.7 %copy-start.9 = (bf16[72,128]{1,0:T(8,128)(2,1)S(1)}, bf16[72,128]{1,0:T(8,128)(2,1)}, u32[]{:S(2)}) copy-start(bf16[72,128]{1,0:T(8,128)(2,1)} %grads_ref.1) | copy-start | bytes 55300
  110.7 22.7 %copy-start.10 = (bf16[72,128]{1,0:T(8,128)(2,1)S(1)}, bf16[72,128]{1,0:T(8,128)(2,1)}, u32[]{:S(2)}) copy-start(bf16[72,128]{1,0:T(8,128)(2,1)} %tokens_ref.1) | copy-start | bytes 55300
  110.7 22.7 %copy-start.11 = (bf16[128]{0:T(256)(128)(2,1)S(1)}, bf16[128]{0:T(256)(128)(2,1)}, u32[]{:S(2)}) copy-start(bf16[128]{0:T(256)(128)(2,1)} %param.8) | copy-start | bytes 772
  110.7 18.6 %collective-permute-start.2 = (bf16[320,256]{1,0:T(8,128)(2,1)S(1)}, bf16[320,256]{1,0:T(8,128)(2,1)S(1)}, u32[]{:S(2)}, u32[]{:S(2)}) collective-permute-start(bf16[320,256]{1,0:T(8,128)(2,1)S(1)} %slice.4), channel_id=1, source_target_pairs={{0,1},{1,0},{2,3},{3,2},{4,5},{5,4},{6,7},{7,6},{8,9},{9,8},{10,11... | collective-permute-start | bytes 491528 | tf_op jit(solution)/shard_map/ppermute | solution.py:408

commit v7 on v6

--- a/solution.py
+++ b/solution.py
@@ -249,8 +249,9 @@
         store.wait()
 
 
-def down_mine_kernel(hidden_ref, grads_ref, out_ref):
-    total = lax.dot_general(hidden_ref[...], grads_ref[...], TN_DIMS, preferred_element_type=F32)
+def down_mine_kernel(packed_ref, grads_ref, out_ref):
+    hidden = packed_ref[:, 4 * SLOT : 5 * SLOT]
+    total = lax.dot_general(hidden, grads_ref[...], TN_DIMS, preferred_element_type=F32)
     out_ref[...] = total[: out_ref.shape[0]]
 
 
@@ -406,17 +407,12 @@
     blocks = lax.all_to_all(blocks_sent, ("tok", "col"), 0, 0, tiled=True)
 
     hidden_other = lax.ppermute(packed[:, 5 * SLOT :], "col", neighbours)
-    half_chunk = width // 2
     down_cost = pl.CostEstimate(flops=flops // 2, bytes_accessed=3 * nt * rows * width, transcendentals=0)
     mine = pl.pallas_call(
         down_mine_kernel,
         out_shape=jax.ShapeDtypeStruct((count, width), F32),
-        grid=(2,),
-        in_specs=[
-            pl.BlockSpec((nt * WINDOW, SLOT), lambda j: (0, 4)),
-            pl.BlockSpec((nt * WINDOW, half_chunk), lambda j: (0, j)),
-        ],
-        out_specs=pl.BlockSpec((count, half_chunk), lambda j: (0, j)),
+        in_specs=[whole()] * 2,
+        out_specs=whole(),
         compiler_params=LARGE,
         cost_estimate=down_cost,
         name="down_grads_mine",
@@ -424,13 +420,8 @@
     d_down = pl.pallas_call(
         down_other_kernel,
         out_shape=jax.ShapeDtypeStruct((count, width), BF16),
-        grid=(2,),
-        in_specs=[
-            pl.BlockSpec((nt * WINDOW, SLOT), lambda j: (0, 0)),
-            pl.BlockSpec((nt * WINDOW, half_chunk), lambda j: (0, j)),
-            pl.BlockSpec((count, half_chunk), lambda j: (0, j)),
-        ],
-        out_specs=pl.BlockSpec((count, half_chunk), lambda j: (0, j)),
+        in_specs=[whole()] * 3,
+        out_specs=whole(),
         compiler_params=LARGE,
         cost_estimate=down_cost,
         name="down_grads",

time: 135 us -> 135 us (level)
  transfers between devices with their start and end apart: 5 -> 5, of which waited for: 3 -> 3; matrix products, arithmetic and copies ran while one was open for 0% -> 0% of each run, Pallas kernels for 4% -> 3%
where the time goes in v7:
time: 135 us; the launch traced here: 134 us
  blocking collectives  75 us (56%)
  waiting for transfers between devices  26.4 us (20%)
  starting transfers between devices  19.4 us (14%)
  Pallas kernels  10.2 us (8%)
  local copies, waits for them, and re-layouts  1.76 us (1%)
    all_to_all x1, blocking collectives, on_device(): lax.all_to_all(copies, AXES, 0, 0, tiled=True, axis_index_groups=second)  42.7 us
    all_to_all x1, blocking collectives, on_device(): lax.all_to_all(copies, AXES, 0, 0, tiled=True, axis_index_groups=first)  17.9 us
    ppermute x1, waiting for transfers between devices, on_device(): hidden_other = lax.ppermute(packed[:, 5 * SLOT:], 'col', neighbours)  15.6 us
    all_gather x1, blocking collectives, on_device(): packed = lax.all_gather(packed, 'row', axis=0, tiled=True)  14.4 us
    all_to_all x1, waiting for transfers between devices, on_device(): lax.all_to_all(parts, AXES, 0, 0, tiled=True, axis_index_groups=pairs)  8.01 us
    all_to_all x1, starting transfers between devices, on_device(): lax.all_to_all(parts, AXES, 0, 0, tiled=True, axis_index_groups=pairs)  5.78 us
    all_to_all x1, starting transfers between devices, on_device(): blocks = lax.all_to_all(blocks_sent, ('tok', 'col'), 0, 0, tiled=True)  5.18 us
    ppermute x1, starting transfers between devices, on_device(): up_other = lax.ppermute(up_sent, 'col', neighbours)  3.83 us
  transfers between devices with their start and end apart: 5, of which 3 were waited for; matrix products, arithmetic and copies ran while one was open for 0% of the time, Pallas kernels for 3%

profile of v7, /device:TPU:8, one launch (start us, length us, event | category | flops | bytes accessed | tf_op | source)
XLA Modules:
  0.0 134.4 jit_solution(289806479461653786)
XLA Ops:
  0.6 0.8 pad_maximum_fusion.own_ref
  1.4 17.9 %all_to_all.20.first_ref = bf16[8,160,128]{2,1,0:T(8,128)(2,1)S(1)} all-to-all(bf16[8,160,128]{2,1,0:T(8,128)(2,1)S(1)} %own_copies.1), channel_id=1, replica_groups={{0,1,2,3,4,5,6,7},{64,65,66,67,68,69,70,71},{128,129,130,131,132,133,13..., dimensions={0} | all-to-all | bytes 655360 | tf_op jit(solution)/shard_map/all_to_all | solution.py:326
  19.4 0.3 second_messages.1
  19.7 0.0 copy-start
  19.7 0.0 copy-start.2
  19.7 0.0 copy-start.8
  19.7 42.7 %all_to_all.21.blocks_ref = bf16[8,1168,128]{2,1,0:T(8,128)(2,1)S(1)} all-to-all(bf16[8,1168,128]{2,1,0:T(8,128)(2,1)S(1)} %second_messages.1), channel_id=1, replica_groups={{0,64,128,192,256,320,384,448},{1,65,129,193,257,321,385,449},{2,66,130..., dimensions={0} | all-to-all | bytes 4784128 | tf_op jit(solution)/shard_map/all_to_all | solution.py:337
  62.4 0.0 copy-done
  62.4 0.0 copy-done.2
  62.4 0.0 copy-done.8
  62.4 2.4 %forward_parts.1 = bf16[16,40,768]{2,1,0:T(8,128)(2,1)} custom-call(bf16[8,1168,128]{2,1,0:T(8,128)(2,1)S(1)} %all_to_all.21.blocks_ref, bf16[8,160,128]{2,1,0:T(8,128)(2,1)S(1)} %all_to_all.20.first_ref, bf16[224,1024]{1,0:T(8,128)(2,1)S(1)} %copy-done, bf16[224,1024]{1,0:T(8,128)(2,1)S(1)} %copy-done.2, bf16[224,1024]{1,0:T(8,128)(2,1)S(1)} %copy-done.8), custom_call_target="tpu_custom_call" | custom-call | flops 905969664 | bytes 4718592 | tf_op jit(solution)/shard_map/forward_parts/pallas_call | solution.py:341
  64.8 5.8 %all-to-all-start.2 = ((bf16[16,40,768]{2,1,0:T(8,128)(2,1)}), bf16[16,40,768]{2,1,0:T(8,128)(2,1)S(1)}, u32[]{:S(2)}, u32[]{:S(2)}) async-start(bf16[16,40,768]{2,1,0:T(8,128)(2,1)} %forward_parts.1), calls=%async_computation.2 | async-start | bytes 1966080 | tf_op jit(solution)/shard_map/all_to_all | solution.py:358
  70.6 2.0 %collective-permute-start = (bf16[224,1024]{1,0:T(8,128)(2,1)}, bf16[224,1024]{1,0:T(8,128)(2,1)}, u32[]{:S(2)}, u32[]{:S(2)}) collective-permute-start(bf16[224,1024]{1,0:T(8,128)(2,1)} %gate_ref.3), channel_id=1, source_target_pairs={{0,1},{1,0},{2,3},{3,2},{4,5},{5,4},{6,7},{7,6},{8,9},{9,8},{10,11... | collective-permute-start | bytes 1376264 | tf_op jit(solution)/shard_map/ppermute | solution.py:351
  72.6 3.8 %collective-permute-start.1 = (bf16[224,1024]{1,0:T(8,128)(2,1)}, bf16[224,1024]{1,0:T(8,128)(2,1)}, u32[]{:S(2)}, u32[]{:S(2)}) collective-permute-start(bf16[224,1024]{1,0:T(8,128)(2,1)} %up_ref.3), channel_id=1, source_target_pairs={{0,1},{1,0},{2,3},{3,2},{4,5},{5,4},{6,7},{7,6},{8,9},{9,8},{10,11... | collective-permute-start | bytes 1376264 | tf_op jit(solution)/shard_map/ppermute | solution.py:352
  76.4 8.0 %all-to-all-done.2.parts_ref = bf16[16,40,768]{2,1,0:T(8,128)(2,1)S(1)} async-done(((bf16[16,40,768]{2,1,0:T(8,128)(2,1)}), bf16[16,40,768]{2,1,0:T(8,128)(2,1)S(1)}, u32[]{:S(2)}, u32[]{:S(2)}) %all-to-all-start.2) | async-done | bytes 983072 | tf_op jit(solution)/shard_map/all_to_all | solution.py:358
  84.4 0.3 swiglu_grads.1
  84.7 0.0 copy-start.1
  84.7 0.0 copy-start.3
  84.7 14.4 %all_gather.3.packed_ref.after_ref = bf16[320,1536]{1,0:T(8,128)(2,1)S(1)} all-gather(bf16[40,1536]{1,0:T(8,128)(2,1)S(1)} %swiglu_grads.1), channel_id=1, replica_groups=mesh['tok'=8,'row'=8,'col'=8] {'row'}, dimensions={0}, use_global_device_ids=true | all-gather | bytes 1105920 | tf_op jit(solution)/shard_map/all_gather | solution.py:370
  99.1 0.6 token_windows.1
  99.7 0.0 copy-start.4
  99.7 0.8 copy-done.4
  100.6 0.0 copy-start.6
  100.6 0.8 copy-done.6
  101.4 0.0 collective-permute-done.gate_other_ref
  101.4 0.0 copy-done.1
  101.4 0.0 copy-done.3
  101.4 1.7 %three_terms.1.three_ref = f32[320,1024]{1,0:T(8,128)S(1)} custom-call(bf16[320,1536]{1,0:T(8,128)(2,1)S(1)} %all_gather.3.packed_ref.after_ref, bf16[224,1024]{1,0:T(8,128)(2,1)S(1)} %copy-done.1, bf16[224,1024]{1,0:T(8,128)(2,1)S(1)} %copy-done.3, bf16[224,1024]{1,0:T(8,128)(2,1)} %collective-permute-done.gate_other_ref), custom_call_target="tpu_custom_call" | custom-call | flops 301989888 | bytes 2359296 | tf_op jit(solution)/shard_map/three_terms/pallas_call | solution.py:382
  103.1 0.0 collective-permute-done.1.up_other_ref
  103.1 0.0 copy-start.5
  103.1 2.3 %input_grad_blocks.1 = bf16[8,8,40,128]{3,2,1,0:T(8,128)(2,1)} custom-call(bf16[320,1536]{1,0:T(8,128)(2,1)S(1)} %all_gather.3.packed_ref.after_ref, f32[320,1024]{1,0:T(8,128)S(1)} %three_terms.1.three_ref, bf16[224,1024]{1,0:T(8,128)(2,1)} %collective-permute-done.1.up_other_ref, bf16[320,1024]{1,0:T(8,128)(2,1)S(1)} %get-tuple-element.14.tokens_ref), custom_call_target="tpu_custom_call" | custom-call | flops 301989888 | bytes 3538944 | tf_op jit(solution)/shard_map/input_grad_blocks/pallas_call | solution.py:391
  105.5 0.0 copy-start.7
  105.5 5.2 %all-to-all-start.3 = ((bf16[64,40,128]{2,1,0:T(8,128)(2,1)}), bf16[64,40,128]{2,1,0:T(8,128)(2,1)S(1)}, u32[]{:S(2)}, u32[]{:S(2)}) async-start(bf16[64,40,128]{2,1,0:T(8,128)(2,1)} %bitcast.1), calls=%async_computation.3 | async-start | bytes 1310720 | tf_op jit(solution)/shard_map/all_to_all | solution.py:407
  110.7 0.0 copy-start.9
  110.7 0.0 copy-start.10
  110.7 0.0 copy-start.11
  110.7 2.6 %collective-permute-start.2 = (bf16[320,256]{1,0:T(8,128)(2,1)S(1)}, bf16[320,256]{1,0:T(8,128)(2,1)S(1)}, u32[]{:S(2)}, u32[]{:S(2)}) collective-permute-start(bf16[320,256]{1,0:T(8,128)(2,1)S(1)} %slice.4), channel_id=1, source_target_pairs={{0,1},{1,0},{2,3},{3,2},{4,5},{5,4},{6,7},{7,6},{8,9},{9,8},{10,11... | collective-permute-start | bytes 491528 | tf_op jit(solution)/shard_map/ppermute | solution.py:409
  113.3 0.0 copy-done.5
  113.4 0.4 down_grads_mine.1.mine_ref
  113.8 15.6 %collective-permute-done.2.hidden_ref = bf16[320,256]{1,0:T(8,128)(2,1)S(1)} collective-permute-done((bf16[320,256]{1,0:T(8,128)(2,1)S(1)}, bf16[320,256]{1,0:T(8,128)(2,1)S(1)}, u32[]{:S(2)}, u32[]{:S(2)}) %collective-permute-start.2) | collective-permute-done | bytes 163872 | tf_op jit(solution)/shard_map/ppermute | solution.py:409
  129.4 0.0 copy-done.7
  129.4 1.2 down_grads.1
  130.6 2.8 %all-to-all-done.3.blocks_ref = bf16[64,40,128]{2,1,0:T(8,128)(2,1)S(1)} async-done(((bf16[64,40,128]{2,1,0:T(8,128)(2,1)}), bf16[64,40,128]{2,1,0:T(8,128)(2,1)S(1)}, u32[]{:S(2)}, u32[]{:S(2)}) %all-to-all-start.3) | async-done | bytes 655392 | tf_op jit(solution)/shard_map/all_to_all | solution.py:407
  133.4 0.0 copy-done.9
  133.4 0.0 copy-done.10
  133.4 0.0 copy-done.11
  133.4 1.0 token_grads.1
  (2 shorter events, 0.1 us)
Async XLA Ops:
  19.7 42.7 %copy-start = (bf16[224,1024]{1,0:T(8,128)(2,1)S(1)}, bf16[224,1024]{1,0:T(8,128)(2,1)}, u32[]{:S(2)}) copy-start(bf16[224,1024]{1,0:T(8,128)(2,1)} %gate_ref.3) | copy-start | bytes 1376260
  19.7 42.7 %copy-start.2 = (bf16[224,1024]{1,0:T(8,128)(2,1)S(1)}, bf16[224,1024]{1,0:T(8,128)(2,1)}, u32[]{:S(2)}) copy-start(bf16[224,1024]{1,0:T(8,128)(2,1)} %up_ref.3) | copy-start | bytes 1376260
  19.7 42.7 %copy-start.8 = (bf16[224,1024]{1,0:T(8,128)(2,1)S(1)}, bf16[224,1024]{1,0:T(8,128)(2,1)}, u32[]{:S(2)}) copy-start(bf16[224,1024]{1,0:T(8,128)(2,1)} %down_ref.1) | copy-start | bytes 1376260
  64.8 19.6 %all-to-all-start.2 = ((bf16[16,40,768]{2,1,0:T(8,128)(2,1)}), bf16[16,40,768]{2,1,0:T(8,128)(2,1)S(1)}, u32[]{:S(2)}, u32[]{:S(2)}) async-start(bf16[16,40,768]{2,1,0:T(8,128)(2,1)} %forward_parts.1), calls=%async_computation.2 | async-start | bytes 1966080 | tf_op jit(solution)/shard_map/all_to_all | solution.py:358
  70.6 30.9 %collective-permute-start = (bf16[224,1024]{1,0:T(8,128)(2,1)}, bf16[224,1024]{1,0:T(8,128)(2,1)}, u32[]{:S(2)}, u32[]{:S(2)}) collective-permute-start(bf16[224,1024]{1,0:T(8,128)(2,1)} %gate_ref.3), channel_id=1, source_target_pairs={{0,1},{1,0},{2,3},{3,2},{4,5},{5,4},{6,7},{7,6},{8,9},{9,8},{10,11... | collective-permute-start | bytes 1376264 | tf_op jit(solution)/shard_map/ppermute | solution.py:351
  72.6 30.5 %collective-permute-start.1 = (bf16[224,1024]{1,0:T(8,128)(2,1)}, bf16[224,1024]{1,0:T(8,128)(2,1)}, u32[]{:S(2)}, u32[]{:S(2)}) collective-permute-start(bf16[224,1024]{1,0:T(8,128)(2,1)} %up_ref.3), channel_id=1, source_target_pairs={{0,1},{1,0},{2,3},{3,2},{4,5},{5,4},{6,7},{7,6},{8,9},{9,8},{10,11... | collective-permute-start | bytes 1376264 | tf_op jit(solution)/shard_map/ppermute | solution.py:352
  84.7 16.7 %copy-start.1 = (bf16[224,1024]{1,0:T(8,128)(2,1)S(1)}, bf16[224,1024]{1,0:T(8,128)(2,1)}, u32[]{:S(2)}) copy-start(bf16[224,1024]{1,0:T(8,128)(2,1)} %gate_ref.3) | copy-start | bytes 1376260
  84.7 16.7 %copy-start.3 = (bf16[224,1024]{1,0:T(8,128)(2,1)S(1)}, bf16[224,1024]{1,0:T(8,128)(2,1)}, u32[]{:S(2)}) copy-start(bf16[224,1024]{1,0:T(8,128)(2,1)} %up_ref.3) | copy-start | bytes 1376260
  99.7 0.9 copy-start.4
  100.6 0.8 copy-start.6
  103.1 10.2 %copy-start.5 = (bf16[320,1024]{1,0:T(8,128)(2,1)S(1)}, bf16[320,1024]{1,0:T(8,128)(2,1)}, u32[]{:S(2)}) copy-start(bf16[320,1024]{1,0:T(8,128)(2,1)} %copy-done.4) | copy-start | bytes 1966084
  105.5 23.9 %copy-start.7 = (bf16[320,1024]{1,0:T(8,128)(2,1)S(1)}, bf16[320,1024]{1,0:T(8,128)(2,1)}, u32[]{:S(2)}) copy-start(bf16[320,1024]{1,0:T(8,128)(2,1)} %copy-done.6) | copy-start | bytes 1966084
  105.5 27.9 %all-to-all-start.3 = ((bf16[64,40,128]{2,1,0:T(8,128)(2,1)}), bf16[64,40,128]{2,1,0:T(8,128)(2,1)S(1)}, u32[]{:S(2)}, u32[]{:S(2)}) async-start(bf16[64,40,128]{2,1,0:T(8,128)(2,1)} %bitcast.1), calls=%async_computation.3 | async-start | bytes 1310720 | tf_op jit(solution)/shard_map/all_to_all | solution.py:407
  110.7 22.7 %copy-start.9 = (bf16[72,128]{1,0:T(8,128)(2,1)S(1)}, bf16[72,128]{1,0:T(8,128)(2,1)}, u32[]{:S(2)}) copy-start(bf16[72,128]{1,0:T(8,128)(2,1)} %grads_ref.1) | copy-start | bytes 55300
  110.7 22.7 %copy-start.10 = (bf16[72,128]{1,0:T(8,128)(2,1)S(1)}, bf16[72,128]{1,0:T(8,128)(2,1)}, u32[]{:S(2)}) copy-start(bf16[72,128]{1,0:T(8,128)(2,1)} %tokens_ref.1) | copy-start | bytes 55300
  110.7 22.7 %copy-start.11 = (bf16[128]{0:T(256)(128)(2,1)S(1)}, bf16[128]{0:T(256)(128)(2,1)}, u32[]{:S(2)}) copy-start(bf16[128]{0:T(256)(128)(2,1)} %param.8) | copy-start | bytes 772
  110.7 18.6 %collective-permute-start.2 = (bf16[320,256]{1,0:T(8,128)(2,1)S(1)}, bf16[320,256]{1,0:T(8,128)(2,1)S(1)}, u32[]{:S(2)}, u32[]{:S(2)}) collective-permute-start(bf16[320,256]{1,0:T(8,128)(2,1)S(1)} %slice.4), channel_id=1, source_target_pairs={{0,1},{1,0},{2,3},{3,2},{4,5},{5,4},{6,7},{7,6},{8,9},{9,8},{10,11... | collective-permute-start | bytes 491528 | tf_op jit(solution)/shard_map/ppermute | solution.py:409

commit v8 on v7

--- a/solution.py
+++ b/solution.py
@@ -184,7 +184,16 @@
     return jnp.concatenate([ref[:, at], fill], axis=0)
 
 
-def three_terms_kernel(step, packed_ref, gate_ref, up_ref, gate_other_ref, out_ref):
+def three_terms_kernel(nt, shares, count, step, packed_ref, gate_ref, up_ref, gate_other_ref, out_ref, extra_ref):
+    base = count % 128
+    spot = lax.broadcasted_iota(jnp.int32, (EXTRA, 128), 0) % 4
+    tail = packed_ref[:, SLOT - 128 : SLOT].astype(F32)
+    for tok in range(nt):
+        piece = tail[tok * WINDOW : (tok + 1) * WINDOW]
+        square = jnp.concatenate([piece, jnp.zeros((128 - WINDOW, 128), F32)], axis=0)
+        turned = square.T[base : base + EXTRA]
+        share = jnp.where(axis_parity("tok") == 1, turned[3:4], turned[2:3]) * (1.0 / shares)
+        extra_ref[tok] = jnp.where(spot == 3, share, turned)
     for chunk in range(out_ref.shape[1] // step):
         at = pl.ds(chunk * step, step)
         term = jnp.zeros((out_ref.shape[0], step), F32)
@@ -196,11 +205,11 @@
 
 def input_kernel(
     nt,
-    shares,
     feats,
     count,
     packed_ref,
     three_ref,
+    extra_ref,
     up_other_ref,
     tokens_ref,
     out_ref,
@@ -219,13 +228,6 @@
     lane = lax.broadcasted_iota(jnp.int32, tail.shape, 1)
     at_inv = (lane >= base + 2) & (lane < base + 4)
     inv = jnp.sum(jnp.where(at_inv, tail, 0.0), axis=1, keepdims=True)
-    extras = []
-    for tok in range(nt):
-        piece = tail[tok * WINDOW : (tok + 1) * WINDOW]
-        square = jnp.concatenate([piece, jnp.zeros((128 - WINDOW, 128), F32)], axis=0)
-        turned = square.T[base : base + EXTRA]
-        share = jnp.where(axis_parity("tok") == 1, turned[3:4], turned[2:3]) * (1.0 / shares)
-        extras.append(jnp.where(spot == 3, share, turned))
     keep = valid_rows((WINDOW, feats), side)
     step = 2 * feats
     stores = []
@@ -238,7 +240,7 @@
         for part in range(2):
             cols = slice(part * feats, (part + 1) * feats)
             for tok in range(nt):
-                extra = jnp.where(spot == 2, gain_term[:, cols], extras[tok])
+                extra = jnp.where(spot == 2, gain_term[:, cols], extra_ref[tok])
                 extra = jnp.concatenate([extra] * (WINDOW // EXTRA), axis=0)
                 block = jnp.where(keep, term[tok * WINDOW : (tok + 1) * WINDOW, cols], extra)
                 block_ref[tok, 2 * chunk + part] = block.astype(BF16)
@@ -379,19 +381,22 @@
         cost_estimate=window_cost,
         name="token_windows",
     )(both, packed)
-    three = pl.pallas_call(
-        functools.partial(three_terms_kernel, 2 * feats),
-        out_shape=jax.ShapeDtypeStruct((nt * WINDOW, width), F32),
+    three, extras = pl.pallas_call(
+        functools.partial(three_terms_kernel, nt, nt * nc // 4, count, 2 * feats),
+        out_shape=(
+            jax.ShapeDtypeStruct((nt * WINDOW, width), F32),
+            jax.ShapeDtypeStruct((nt, EXTRA, feats), F32),
+        ),
         in_specs=[whole()] * 4,
-        out_specs=whole(),
+        out_specs=(whole(), whole()),
         compiler_params=LARGE,
         cost_estimate=pl.CostEstimate(flops=flops, bytes_accessed=4 * nt * rows * width, transcendentals=0),
         name="three_terms",
     )(packed, gate_weight, up_weight, gate_other)
     blocks = pl.pallas_call(
-        functools.partial(input_kernel, nt, nt * nc // 4, feats, count),
+        functools.partial(input_kernel, nt, feats, count),
         out_shape=jax.ShapeDtypeStruct((nt, nc, WINDOW, feats), BF16),
-        in_specs=[whole(), whole(), whole(pl.ANY), whole()],
+        in_specs=[whole(), whole(), whole(), whole(pl.ANY), whole()],
         out_specs=whole(pl.ANY),
         scratch_shapes=[
             pltpu.VMEM((SLOT, width), BF16),
@@ -402,7 +407,7 @@
         compiler_params=LARGE,
         cost_estimate=pl.CostEstimate(flops=flops, bytes_accessed=6 * nt * rows * width, transcendentals=0),
         name="input_grad_blocks",
-    )(packed, three, up_other, tokens_all)
+    )(packed, three, extras, up_other, tokens_all)
     blocks_sent = blocks.reshape(nt * nc, WINDOW, feats)
     blocks = lax.all_to_all(blocks_sent, ("tok", "col"), 0, 0, tiled=True)
 

time: 135 us -> 135 us (level)
  no operation moved by 1% of the time
where the time goes in v8:
time: 135 us; the launch traced here: 134 us
  blocking collectives  75 us (56%)
  waiting for transfers between devices  26.4 us (20%)
  starting transfers between devices  19.4 us (14%)
  Pallas kernels  10.2 us (8%)
  local copies, waits for them, and re-layouts  1.77 us (1%)
    all_to_all x1, blocking collectives, on_device(): lax.all_to_all(copies, AXES, 0, 0, tiled=True, axis_index_groups=second)  42.7 us
    all_to_all x1, blocking collectives, on_device(): lax.all_to_all(copies, AXES, 0, 0, tiled=True, axis_index_groups=first)  17.9 us
    ppermute x1, waiting for transfers between devices, on_device(): hidden_other = lax.ppermute(packed[:, 5 * SLOT:], 'col', neighbours)  15.6 us
    all_gather x1, blocking collectives, on_device(): packed = lax.all_gather(packed, 'row', axis=0, tiled=True)  14.4 us
    all_to_all x1, waiting for transfers between devices, on_device(): lax.all_to_all(parts, AXES, 0, 0, tiled=True, axis_index_groups=pairs)  8.01 us
    all_to_all x1, starting transfers between devices, on_device(): lax.all_to_all(parts, AXES, 0, 0, tiled=True, axis_index_groups=pairs)  5.78 us
    all_to_all x1, starting transfers between devices, on_device(): blocks = lax.all_to_all(blocks_sent, ('tok', 'col'), 0, 0, tiled=True)  5.17 us
    ppermute x1, starting transfers between devices, on_device(): up_other = lax.ppermute(up_sent, 'col', neighbours)  3.83 us
  transfers between devices with their start and end apart: 5, of which 3 were waited for; matrix products, arithmetic and copies ran while one was open for 0% of the time, Pallas kernels for 3%

profile of v8, /device:TPU:8, one launch (start us, length us, event | category | flops | bytes accessed | tf_op | source)
XLA Modules:
  0.0 134.4 jit_solution(14765818368343210296)
XLA Ops:
  0.6 0.8 pad_maximum_fusion.own_ref
  1.4 17.9 %all_to_all.20.first_ref = bf16[8,160,128]{2,1,0:T(8,128)(2,1)S(1)} all-to-all(bf16[8,160,128]{2,1,0:T(8,128)(2,1)S(1)} %own_copies.1), channel_id=1, replica_groups={{0,1,2,3,4,5,6,7},{64,65,66,67,68,69,70,71},{128,129,130,131,132,133,13..., dimensions={0} | all-to-all | bytes 655360 | tf_op jit(solution)/shard_map/all_to_all | solution.py:328
  19.4 0.3 second_messages.1
  19.7 0.0 copy-start
  19.7 0.0 copy-start.2
  19.7 0.0 copy-start.8
  19.7 42.7 %all_to_all.21.blocks_ref = bf16[8,1168,128]{2,1,0:T(8,128)(2,1)S(1)} all-to-all(bf16[8,1168,128]{2,1,0:T(8,128)(2,1)S(1)} %second_messages.1), channel_id=1, replica_groups={{0,64,128,192,256,320,384,448},{1,65,129,193,257,321,385,449},{2,66,130..., dimensions={0} | all-to-all | bytes 4784128 | tf_op jit(solution)/shard_map/all_to_all | solution.py:339
  62.4 0.0 copy-done
  62.4 0.0 copy-done.2
  62.4 0.0 copy-done.8
  62.4 2.4 %forward_parts.1 = bf16[16,40,768]{2,1,0:T(8,128)(2,1)} custom-call(bf16[8,1168,128]{2,1,0:T(8,128)(2,1)S(1)} %all_to_all.21.blocks_ref, bf16[8,160,128]{2,1,0:T(8,128)(2,1)S(1)} %all_to_all.20.first_ref, bf16[224,1024]{1,0:T(8,128)(2,1)S(1)} %copy-done, bf16[224,1024]{1,0:T(8,128)(2,1)S(1)} %copy-done.2, bf16[224,1024]{1,0:T(8,128)(2,1)S(1)} %copy-done.8), custom_call_target="tpu_custom_call" | custom-call | flops 905969664 | bytes 4718592 | tf_op jit(solution)/shard_map/forward_parts/pallas_call | solution.py:343
  64.8 5.8 %all-to-all-start.2 = ((bf16[16,40,768]{2,1,0:T(8,128)(2,1)}), bf16[16,40,768]{2,1,0:T(8,128)(2,1)S(1)}, u32[]{:S(2)}, u32[]{:S(2)}) async-start(bf16[16,40,768]{2,1,0:T(8,128)(2,1)} %forward_parts.1), calls=%async_computation.2 | async-start | bytes 1966080 | tf_op jit(solution)/shard_map/all_to_all | solution.py:360
  70.6 2.0 %collective-permute-start = (bf16[224,1024]{1,0:T(8,128)(2,1)}, bf16[224,1024]{1,0:T(8,128)(2,1)}, u32[]{:S(2)}, u32[]{:S(2)}) collective-permute-start(bf16[224,1024]{1,0:T(8,128)(2,1)} %gate_ref.3), channel_id=1, source_target_pairs={{0,1},{1,0},{2,3},{3,2},{4,5},{5,4},{6,7},{7,6},{8,9},{9,8},{10,11... | collective-permute-start | bytes 1376264 | tf_op jit(solution)/shard_map/ppermute | solution.py:353
  72.6 3.8 %collective-permute-start.1 = (bf16[224,1024]{1,0:T(8,128)(2,1)}, bf16[224,1024]{1,0:T(8,128)(2,1)}, u32[]{:S(2)}, u32[]{:S(2)}) collective-permute-start(bf16[224,1024]{1,0:T(8,128)(2,1)} %up_ref.3), channel_id=1, source_target_pairs={{0,1},{1,0},{2,3},{3,2},{4,5},{5,4},{6,7},{7,6},{8,9},{9,8},{10,11... | collective-permute-start | bytes 1376264 | tf_op jit(solution)/shard_map/ppermute | solution.py:354
  76.4 8.0 %all-to-all-done.2.parts_ref = bf16[16,40,768]{2,1,0:T(8,128)(2,1)S(1)} async-done(((bf16[16,40,768]{2,1,0:T(8,128)(2,1)}), bf16[16,40,768]{2,1,0:T(8,128)(2,1)S(1)}, u32[]{:S(2)}, u32[]{:S(2)}) %all-to-all-start.2) | async-done | bytes 983072 | tf_op jit(solution)/shard_map/all_to_all | solution.py:360
  84.4 0.3 swiglu_grads.1
  84.7 0.0 copy-start.1
  84.7 0.0 copy-start.3
  84.7 14.4 %all_gather.3.packed_ref.after_ref = bf16[320,1536]{1,0:T(8,128)(2,1)S(1)} all-gather(bf16[40,1536]{1,0:T(8,128)(2,1)S(1)} %swiglu_grads.1), channel_id=1, replica_groups=mesh['tok'=8,'row'=8,'col'=8] {'row'}, dimensions={0}, use_global_device_ids=true | all-gather | bytes 1105920 | tf_op jit(solution)/shard_map/all_gather | solution.py:372
  99.1 0.6 token_windows.1
  99.7 0.0 copy-start.4
  99.7 0.8 copy-done.4
  100.6 0.0 copy-start.6
  100.6 0.9 copy-done.6
  101.4 0.0 collective-permute-done.gate_other_ref
  101.4 0.0 copy-done.1
  101.4 0.0 copy-done.3
  101.4 1.7 %three_terms.1 = (f32[320,1024]{1,0:T(8,128)S(1)}, f32[8,8,128]{2,1,0:T(8,128)S(1)}) custom-call(bf16[320,1536]{1,0:T(8,128)(2,1)S(1)} %all_gather.3.packed_ref.after_ref, bf16[224,1024]{1,0:T(8,128)(2,1)S(1)} %copy-done.1, bf16[224,1024]{1,0:T(8,128)(2,1)S(1)} %copy-done.3, bf16[224,1024]{1,0:T(8,128)(2,1)} %collective-permute-done.gate_other_ref), custom_call_target="tpu_custom_call" | custom-call | flops 301989888 | bytes 2359296 | tf_op jit(solution)/shard_map/three_terms/pallas_call | solution.py:384
  103.1 0.0 collective-permute-done.1.up_other_ref
  103.1 0.0 copy-start.5
  103.1 2.3 %input_grad_blocks.1 = bf16[8,8,40,128]{3,2,1,0:T(8,128)(2,1)} custom-call(bf16[320,1536]{1,0:T(8,128)(2,1)S(1)} %all_gather.3.packed_ref.after_ref, f32[320,1024]{1,0:T(8,128)S(1)} %get-tuple-element.15.three_ref, f32[8,8,128]{2,1,0:T(8,128)S(1)} %get-tuple-element.16.extra_ref, bf16[224,1024]{1,0:T(8,128)(2,1)} %collective-permute-done.1.up_other_ref, ...), custom_call_target="tpu_custom_call" | custom-call | flops 301989888 | bytes 3538944 | tf_op jit(solution)/shard_map/input_grad_blocks/pallas_call | solution.py:396
  105.5 0.0 copy-start.7
  105.5 5.2 %all-to-all-start.3 = ((bf16[64,40,128]{2,1,0:T(8,128)(2,1)}), bf16[64,40,128]{2,1,0:T(8,128)(2,1)S(1)}, u32[]{:S(2)}, u32[]{:S(2)}) async-start(bf16[64,40,128]{2,1,0:T(8,128)(2,1)} %bitcast.1), calls=%async_computation.3 | async-start | bytes 1310720 | tf_op jit(solution)/shard_map/all_to_all | solution.py:412
  110.7 0.0 copy-start.9
  110.7 0.0 copy-start.10
  110.7 0.0 copy-start.11
  110.7 2.6 %collective-permute-start.2 = (bf16[320,256]{1,0:T(8,128)(2,1)S(1)}, bf16[320,256]{1,0:T(8,128)(2,1)S(1)}, u32[]{:S(2)}, u32[]{:S(2)}) collective-permute-start(bf16[320,256]{1,0:T(8,128)(2,1)S(1)} %slice.4), channel_id=1, source_target_pairs={{0,1},{1,0},{2,3},{3,2},{4,5},{5,4},{6,7},{7,6},{8,9},{9,8},{10,11... | collective-permute-start | bytes 491528 | tf_op jit(solution)/shard_map/ppermute | solution.py:414
  113.3 0.0 copy-done.5
  113.4 0.4 down_grads_mine.1.mine_ref
  113.8 15.6 %collective-permute-done.2.hidden_ref = bf16[320,256]{1,0:T(8,128)(2,1)S(1)} collective-permute-done((bf16[320,256]{1,0:T(8,128)(2,1)S(1)}, bf16[320,256]{1,0:T(8,128)(2,1)S(1)}, u32[]{:S(2)}, u32[]{:S(2)}) %collective-permute-start.2) | collective-permute-done | bytes 163872 | tf_op jit(solution)/shard_map/ppermute | solution.py:414
  129.4 0.0 copy-done.7
  129.4 1.2 down_grads.1
  130.6 2.8 %all-to-all-done.3.blocks_ref = bf16[64,40,128]{2,1,0:T(8,128)(2,1)S(1)} async-done(((bf16[64,40,128]{2,1,0:T(8,128)(2,1)}), bf16[64,40,128]{2,1,0:T(8,128)(2,1)S(1)}, u32[]{:S(2)}, u32[]{:S(2)}) %all-to-all-start.3) | async-done | bytes 655392 | tf_op jit(solution)/shard_map/all_to_all | solution.py:412
  133.4 0.0 copy-done.9
  133.4 0.0 copy-done.10
  133.4 0.0 copy-done.11
  133.4 1.0 token_grads.1
  (2 shorter events, 0.1 us)
Async XLA Ops:
  19.7 42.7 %copy-start = (bf16[224,1024]{1,0:T(8,128)(2,1)S(1)}, bf16[224,1024]{1,0:T(8,128)(2,1)}, u32[]{:S(2)}) copy-start(bf16[224,1024]{1,0:T(8,128)(2,1)} %gate_ref.3) | copy-start | bytes 1376260
  19.7 42.7 %copy-start.2 = (bf16[224,1024]{1,0:T(8,128)(2,1)S(1)}, bf16[224,1024]{1,0:T(8,128)(2,1)}, u32[]{:S(2)}) copy-start(bf16[224,1024]{1,0:T(8,128)(2,1)} %up_ref.3) | copy-start | bytes 1376260
  19.7 42.7 %copy-start.8 = (bf16[224,1024]{1,0:T(8,128)(2,1)S(1)}, bf16[224,1024]{1,0:T(8,128)(2,1)}, u32[]{:S(2)}) copy-start(bf16[224,1024]{1,0:T(8,128)(2,1)} %down_ref.1) | copy-start | bytes 1376260
  64.8 19.6 %all-to-all-start.2 = ((bf16[16,40,768]{2,1,0:T(8,128)(2,1)}), bf16[16,40,768]{2,1,0:T(8,128)(2,1)S(1)}, u32[]{:S(2)}, u32[]{:S(2)}) async-start(bf16[16,40,768]{2,1,0:T(8,128)(2,1)} %forward_parts.1), calls=%async_computation.2 | async-start | bytes 1966080 | tf_op jit(solution)/shard_map/all_to_all | solution.py:360
  70.6 30.9 %collective-permute-start = (bf16[224,1024]{1,0:T(8,128)(2,1)}, bf16[224,1024]{1,0:T(8,128)(2,1)}, u32[]{:S(2)}, u32[]{:S(2)}) collective-permute-start(bf16[224,1024]{1,0:T(8,128)(2,1)} %gate_ref.3), channel_id=1, source_target_pairs={{0,1},{1,0},{2,3},{3,2},{4,5},{5,4},{6,7},{7,6},{8,9},{9,8},{10,11... | collective-permute-start | bytes 1376264 | tf_op jit(solution)/shard_map/ppermute | solution.py:353
  72.6 30.5 %collective-permute-start.1 = (bf16[224,1024]{1,0:T(8,128)(2,1)}, bf16[224,1024]{1,0:T(8,128)(2,1)}, u32[]{:S(2)}, u32[]{:S(2)}) collective-permute-start(bf16[224,1024]{1,0:T(8,128)(2,1)} %up_ref.3), channel_id=1, source_target_pairs={{0,1},{1,0},{2,3},{3,2},{4,5},{5,4},{6,7},{7,6},{8,9},{9,8},{10,11... | collective-permute-start | bytes 1376264 | tf_op jit(solution)/shard_map/ppermute | solution.py:354
  84.7 16.7 %copy-start.1 = (bf16[224,1024]{1,0:T(8,128)(2,1)S(1)}, bf16[224,1024]{1,0:T(8,128)(2,1)}, u32[]{:S(2)}) copy-start(bf16[224,1024]{1,0:T(8,128)(2,1)} %gate_ref.3) | copy-start | bytes 1376260
  84.7 16.7 %copy-start.3 = (bf16[224,1024]{1,0:T(8,128)(2,1)S(1)}, bf16[224,1024]{1,0:T(8,128)(2,1)}, u32[]{:S(2)}) copy-start(bf16[224,1024]{1,0:T(8,128)(2,1)} %up_ref.3) | copy-start | bytes 1376260
  99.7 0.9 copy-start.4
  100.6 0.9 copy-start.6
  103.1 10.2 %copy-start.5 = (bf16[320,1024]{1,0:T(8,128)(2,1)S(1)}, bf16[320,1024]{1,0:T(8,128)(2,1)}, u32[]{:S(2)}) copy-start(bf16[320,1024]{1,0:T(8,128)(2,1)} %copy-done.4) | copy-start | bytes 1966084
  105.5 23.9 %copy-start.7 = (bf16[320,1024]{1,0:T(8,128)(2,1)S(1)}, bf16[320,1024]{1,0:T(8,128)(2,1)}, u32[]{:S(2)}) copy-start(bf16[320,1024]{1,0:T(8,128)(2,1)} %copy-done.6) | copy-start | bytes 1966084
  105.5 27.9 %all-to-all-start.3 = ((bf16[64,40,128]{2,1,0:T(8,128)(2,1)}), bf16[64,40,128]{2,1,0:T(8,128)(2,1)S(1)}, u32[]{:S(2)}, u32[]{:S(2)}) async-start(bf16[64,40,128]{2,1,0:T(8,128)(2,1)} %bitcast.1), calls=%async_computation.3 | async-start | bytes 1310720 | tf_op jit(solution)/shard_map/all_to_all | solution.py:412
  110.7 22.7 %copy-start.9 = (bf16[72,128]{1,0:T(8,128)(2,1)S(1)}, bf16[72,128]{1,0:T(8,128)(2,1)}, u32[]{:S(2)}) copy-start(bf16[72,128]{1,0:T(8,128)(2,1)} %grads_ref.1) | copy-start | bytes 55300
  110.7 22.7 %copy-start.10 = (bf16[72,128]{1,0:T(8,128)(2,1)S(1)}, bf16[72,128]{1,0:T(8,128)(2,1)}, u32[]{:S(2)}) copy-start(bf16[72,128]{1,0:T(8,128)(2,1)} %tokens_ref.1) | copy-start | bytes 55300
  110.7 22.7 %copy-start.11 = (bf16[128]{0:T(256)(128)(2,1)S(1)}, bf16[128]{0:T(256)(128)(2,1)}, u32[]{:S(2)}) copy-start(bf16[128]{0:T(256)(128)(2,1)} %param.8) | copy-start | bytes 772
  110.7 18.7 %collective-permute-start.2 = (bf16[320,256]{1,0:T(8,128)(2,1)S(1)}, bf16[320,256]{1,0:T(8,128)(2,1)S(1)}, u32[]{:S(2)}, u32[]{:S(2)}) collective-permute-start(bf16[320,256]{1,0:T(8,128)(2,1)S(1)} %slice.4), channel_id=1, source_target_pairs={{0,1},{1,0},{2,3},{3,2},{4,5},{5,4},{6,7},{7,6},{8,9},{9,8},{10,11... | collective-permute-start | bytes 491528 | tf_op jit(solution)/shard_map/ppermute | solution.py:414
